TPU v7x, 256 devices: a whole 4x4x8 slice. The times are simulated.
256 devices in a mesh: dp: 8 (over z_lo, y), seq: 32 (over z_hi, x, core).
Axes of the slice: x: 4, y: 4, z: 8 (z_hi: 4, z_lo: 2; z = z_hi * 2 + z_lo), core: 2. Of those that a mesh axis runs over, the one named last changes fastest.
Arguments:
- queries: bfloat16 [32768, 4096], P(('dp', 'seq')), may hold values from -64 to 64
- keys: bfloat16 [32768, 4096], P(('dp', 'seq')), may hold values from -64 to 64
- values: bfloat16 [32768, 4096], P(('dp', 'seq')), may hold values from -6 to 6
- out_grad: bfloat16 [32768, 4096], P(('dp', 'seq')), may hold values from -6 to 6
- gain_q: float32 [32, 128], P('seq', 'dp'), may hold values from 0.5 to 10
- gain_k: float32 [32, 128], P('seq', 'dp'), may hold values from 0.5 to 10
- clip_ids: int32 [8, 4096], P('dp', 'seq'), may hold values from 0 to 31, never falling along the last dimension, each value on 1 to 256 neighbouring positions
- counts: int32 [8, 32], P('dp', 'seq'), may hold values from 42 to 128, as said below
Outputs:
- grad_queries: bfloat16 [32768, 4096], P(('dp', 'seq'))
- grad_keys: bfloat16 [32768, 4096], P(('dp', 'seq'))
- grad_values: bfloat16 [32768, 4096], P(('dp', 'seq'))
- grad_gain_q: float32 [32, 128], P('seq')
- grad_gain_k: float32 [32, 128], P('seq')
Inputs may be any that keep to these rules, and one draw needn't show every extreme that they name: `counts`: in every row one device holds 128 live slots and another a third of 128, rounded down. `clip_ids`: along a row clip numbers never fall; each clip takes 1 to 256 consecutive slots, one exactly 256.
All inputs are finite; a program needn't handle non-finite values.
Results may differ from a plain program's by a relative error of at most 0.011.
The roundings to bfloat16 on the way count: a program that leaves them out, or rounds other values in their place, can miss the bound.
Values may be sent and summed in bfloat16 or wider, within the bound.
No kernel may reach another device: no remote copies, remote signals or barrier semaphores. Data moves between devices by JAX's collectives and lax.ppermute only.
A program may use at most 192 MiB of HBM per device.

v0:
```python
import jax
import jax.numpy as jnp
from jax import lax
from jax.sharding import PartitionSpec as P

EPS = 1e-06
NEG = -1e30


def norm_parts(rows, gain):
    widened = rows.astype(jnp.float32)
    scaled = lax.rsqrt(jnp.mean(widened * widened, axis=-1, keepdims=True) + EPS)
    unit_rows = widened * scaled
    return (scaled, unit_rows, (unit_rows * gain).astype(jnp.bfloat16))


def norm_back(scaled, unit_rows, gain, upper):
    weighted = gain * upper
    return scaled * (weighted - unit_rows * jnp.mean(unit_rows * weighted, axis=-1, keepdims=True))


def attend(q_norm, k_norm, v_rows, d_rows, linked, q_live):
    score_scale = q_norm.shape[-1] ** (-0.5)
    scores = (
        jnp.einsum("brd,bcd->brc", q_norm, k_norm, preferred_element_type=jnp.float32) * score_scale
    )
    masked = jnp.where(linked, scores, NEG)
    row_top = jnp.max(masked, axis=-1, keepdims=True)
    exponent = jnp.where(linked, jnp.exp(masked - row_top), 0.0)
    row_total = jnp.sum(exponent, axis=-1, keepdims=True) + (1.0 - q_live)[:, None]
    weights = (exponent / row_total).astype(jnp.bfloat16)
    outputs = jnp.einsum("brc,bcd->brd", weights, v_rows, preferred_element_type=jnp.float32)
    row_delta = jnp.sum(d_rows.astype(jnp.float32) * outputs, axis=-1, keepdims=True)
    d_weights = jnp.einsum("brd,bcd->brc", d_rows, v_rows, preferred_element_type=jnp.float32)
    d_scores = (weights.astype(jnp.float32) * (d_weights - row_delta)).astype(jnp.bfloat16)
    dq_norm = (
        jnp.einsum("brc,bcd->brd", d_scores, k_norm, preferred_element_type=jnp.float32)
        * score_scale
    )
    dk_norm = (
        jnp.einsum("brc,brd->bcd", d_scores, q_norm, preferred_element_type=jnp.float32)
        * score_scale
    )
    dv_rows = jnp.einsum("brc,brd->bcd", weights, d_rows, preferred_element_type=jnp.float32)
    return (dq_norm, dk_norm, dv_rows)


def group_head(q_rows, k_rows, v_rows, d_rows, gain_q, gain_k, clip, live_rows, q_block, key_reach):
    batch = q_rows.shape[0]
    length = q_rows.shape[1]
    depth = q_rows.shape[2]
    q_scale, q_unit, q_norm = norm_parts(q_rows, gain_q[:, None, :])
    k_scale, k_unit, k_norm = norm_parts(k_rows, gain_k[:, None, :])
    padding = ((0, 0), (key_reach, key_reach), (0, 0))
    k_wide = jnp.pad(k_norm, padding)
    v_wide = jnp.pad(v_rows, padding)
    clip_wide = jnp.pad(clip, (key_reach, key_reach), constant_values=-1)
    live_wide = jnp.pad(live_rows, (key_reach, key_reach))
    key_span = q_block + 2 * key_reach

    def one_block(totals, position):
        dk_acc, dv_acc = totals
        first_row = position * q_block
        q_part = lax.dynamic_slice_in_dim(q_norm, first_row, q_block, 1)
        d_part = lax.dynamic_slice_in_dim(d_rows, first_row, q_block, 1)
        k_part = lax.dynamic_slice_in_dim(k_wide, first_row, key_span, 1)
        v_part = lax.dynamic_slice_in_dim(v_wide, first_row, key_span, 1)
        clip_q = lax.dynamic_slice_in_dim(clip, first_row, q_block)
        live_q = lax.dynamic_slice_in_dim(live_rows, first_row, q_block)
        clip_k = lax.dynamic_slice_in_dim(clip_wide, first_row, key_span)
        live_k = lax.dynamic_slice_in_dim(live_wide, first_row, key_span)
        linked = (
            (clip_q[:, None] == clip_k[None, :]) & (live_q[:, None] > 0) & (live_k[None, :] > 0)
        )
        dq_part, dk_part, dv_part = attend(
            q_part, k_part, v_part, d_part, linked, live_q.astype(jnp.float32)
        )
        dk_acc = lax.dynamic_update_slice_in_dim(
            dk_acc, lax.dynamic_slice_in_dim(dk_acc, first_row, key_span, 1) + dk_part, first_row, 1
        )
        dv_acc = lax.dynamic_update_slice_in_dim(
            dv_acc, lax.dynamic_slice_in_dim(dv_acc, first_row, key_span, 1) + dv_part, first_row, 1
        )
        return ((dk_acc, dv_acc), dq_part)

    zero_rows = jnp.zeros((batch, length + 2 * key_reach, depth), jnp.float32)
    steps_index = jnp.arange(length // q_block, dtype=jnp.int32)
    (dk_acc, dv_acc), dq_parts = lax.scan(one_block, (zero_rows, zero_rows), steps_index)
    dq_norm = dq_parts.transpose(1, 0, 2, 3).reshape(batch, length, depth)
    dk_norm = dk_acc[:, key_reach : key_reach + length]
    dv_full = dv_acc[:, key_reach : key_reach + length]
    grad_q = norm_back(q_scale, q_unit, gain_q[:, None, :], dq_norm).astype(jnp.bfloat16)
    grad_k = norm_back(k_scale, k_unit, gain_k[:, None, :], dk_norm).astype(jnp.bfloat16)
    gain_grad_q = jnp.sum(dq_norm * q_unit, axis=1)
    gain_grad_k = jnp.sum(dk_norm * k_unit, axis=1)
    return (grad_q, grad_k, dv_full.astype(jnp.bfloat16), gain_grad_q, gain_grad_k)


def shards(queries, keys, values, out_grad, gain_q, gain_k, clip_ids, counts):
    tok_rows = queries.shape[0]
    feat_width = queries.shape[1]
    groups = lax.axis_size("seq")
    key_reach = 2 * tok_rows
    gain_cols = (
        lax.all_gather(gain_q, "dp", axis=1, tiled=True),
        lax.all_gather(gain_k, "dp", axis=1, tiled=True),
    )
    head_dim = gain_cols[0].shape[1]
    head_count = feat_width // head_dim
    own_heads = head_count // groups
    clip_all, count_all = (
        lax.all_gather(clip_ids, "seq", axis=1, tiled=True),
        lax.all_gather(counts, "seq", axis=1, tiled=True),
    )
    slot_index = jnp.arange(tok_rows, dtype=jnp.int32)
    length = tok_rows * groups
    live_rows = (slot_index[None, :] < count_all[0][:, None]).astype(jnp.int32).reshape(length)

    def to_heads(tensor):
        return tensor.reshape(tok_rows, groups, own_heads * head_dim)

    head_data = (
        lax.all_to_all(to_heads(queries), "seq", split_axis=1, concat_axis=0, tiled=True),
        lax.all_to_all(to_heads(keys), "seq", split_axis=1, concat_axis=0, tiled=True),
        lax.all_to_all(to_heads(values), "seq", split_axis=1, concat_axis=0, tiled=True),
        lax.all_to_all(to_heads(out_grad), "seq", split_axis=1, concat_axis=0, tiled=True),
    )

    def to_local(tensor):
        return tensor.transpose(1, 0, 2)

    q_block = min(512, length)
    grad_q, grad_k, grad_v, gain_grad_q, gain_grad_k = group_head(
        to_local(head_data[0]),
        to_local(head_data[1]),
        to_local(head_data[2]),
        to_local(head_data[3]),
        gain_cols[0],
        gain_cols[1],
        clip_all[0],
        live_rows,
        q_block,
        key_reach,
    )

    def to_tokens(tensor):
        return tensor.transpose(1, 0, 2)

    token_data = (
        lax.all_to_all(to_tokens(grad_q), "seq", split_axis=0, concat_axis=1, tiled=True),
        lax.all_to_all(to_tokens(grad_k), "seq", split_axis=0, concat_axis=1, tiled=True),
        lax.all_to_all(to_tokens(grad_v), "seq", split_axis=0, concat_axis=1, tiled=True),
    )
    grad_queries = token_data[0].reshape(tok_rows, feat_width)
    grad_keys = token_data[1].reshape(tok_rows, feat_width)
    grad_values = token_data[2].reshape(tok_rows, feat_width)
    gain_grad_q, gain_grad_k = lax.psum((gain_grad_q, gain_grad_k), "dp")
    return (grad_queries, grad_keys, grad_values, gain_grad_q, gain_grad_k)


def solution(mesh):
    placed = (
        P(("dp", "seq"), None),
        P(("dp", "seq"), None),
        P(("dp", "seq"), None),
        P(("dp", "seq"), None),
        P("seq", "dp"),
        P("seq", "dp"),
        P("dp", "seq"),
        P("dp", "seq"),
    )
    return jax.shard_map(
        shards,
        mesh=mesh,
        in_specs=placed,
        out_specs=(
            P(("dp", "seq"), None),
            P(("dp", "seq"), None),
            P(("dp", "seq"), None),
            P("seq", None),
            P("seq", None),
        ),
        check_vma=False,
    )
```

profile of v0, /device:TPU:1, one launch (start us, length us, event | category | flops | bytes accessed | tf_op | source)
XLA Modules:
  0.0 522.9 jit_solution(446608080853303513)
XLA Ops:
  3.1 12.6 %all-to-all-start = ((bf16[128,32,128]{2,0,1:T(8,128)(2,1)}), bf16[128,32,128]{2,0,1:T(8,128)(2,1)S(1)}, u32[]{:S(2)}, u32[]{:S(2)}) async-start(bf16[128,32,128]{2,0,1:T(8,128)(2,1)} %copy_bitcast_fusion.2), calls=%async_computation | async-start | bytes 2097152 | tf_op jit(solution)/shard_map/all_to_all | solution.py:123
  17.0 26.4 %all-to-all-done = bf16[128,32,128]{2,0,1:T(8,128)(2,1)S(1)} async-done(((bf16[128,32,128]{2,0,1:T(8,128)(2,1)}), bf16[128,32,128]{2,0,1:T(8,128)(2,1)S(1)}, u32[]{:S(2)}, u32[]{:S(2)}) %all-to-all-start) | async-done | bytes 1048608 | tf_op jit(solution)/shard_map/all_to_all | solution.py:123
  43.3 6.4 %all-to-all-start.1 = ((bf16[128,32,128]{2,0,1:T(8,128)(2,1)}), bf16[128,32,128]{2,0,1:T(8,128)(2,1)S(1)}, u32[]{:S(2)}, u32[]{:S(2)}) async-start(bf16[128,32,128]{2,0,1:T(8,128)(2,1)} %copy_bitcast_fusion.1), calls=%async_computation.1 | async-start | bytes 2097152 | tf_op jit(solution)/shard_map/all_to_all | solution.py:124
  49.8 2.5 copy_bitcast_fusion
  52.3 26.2 %all-to-all-done.1 = bf16[128,32,128]{2,0,1:T(8,128)(2,1)S(1)} async-done(((bf16[128,32,128]{2,0,1:T(8,128)(2,1)}), bf16[128,32,128]{2,0,1:T(8,128)(2,1)S(1)}, u32[]{:S(2)}, u32[]{:S(2)}) %all-to-all-start.1) | async-done | bytes 1048608 | tf_op jit(solution)/shard_map/all_to_all | solution.py:124
  78.5 5.7 %all-to-all-start.3 = ((bf16[128,32,128]{2,0,1:T(8,128)(2,1)}), bf16[128,32,128]{2,0,1:T(8,128)(2,1)}, u32[]{:S(2)}, u32[]{:S(2)}) async-start(bf16[128,32,128]{2,0,1:T(8,128)(2,1)} %copy_bitcast_fusion), calls=%async_computation.3 | async-start | bytes 2097152 | tf_op jit(solution)/shard_map/all_to_all | solution.py:125
  89.7 24.4 %all-reduce.5 = s32[32]{0:T(128)S(1)} all-reduce(s32[32]{0:T(128)S(1)} %bitcast_dynamic-update-slice_fusion.1), channel_id=1, replica_groups=mesh['dp'=8,'seq'=32] {'seq'}, use_global_device_ids=true, to_apply=%add.5 | all-reduce | flops 32 | bytes 256
  114.3 7.6 %all-to-all-start.2 = ((bf16[128,32,128]{0,2,1:T(8,128)(2,1)}), bf16[128,32,128]{0,2,1:T(8,128)(2,1)}, u32[]{:S(2)}, u32[]{:S(2)}) async-start(bf16[128,32,128]{0,2,1:T(8,128)(2,1)} %bitcast.187), calls=%async_computation.2 | async-start | bytes 2097152 | tf_op jit(solution)/shard_map/all_to_all | solution.py:126
  122.0 60.0 %all_gather.16 = s32[1,4096]{1,0:T(1,128)S(1)} all-gather(s32[1,128]{1,0:T(1,128)S(1)} %copy-done.6), channel_id=1, replica_groups=mesh['dp'=8,'seq'=32] {'seq'}, dimensions={1}, use_global_device_ids=true | all-gather | bytes 16896 | tf_op jit(solution)/shard_map/all_gather | solution.py:112
  182.1 13.9 %all-reduce.8 = (f32[128]{0:T(128)S(1)}, f32[128]{0:T(128)S(1)}) all-reduce(f32[128]{0:T(128)S(1)} %bitcast_dynamic-update-slice_fusion.2, f32[128]{0:T(128)S(1)} %bitcast_dynamic-update-slice_fusion), channel_id=1, replica_groups=mesh['dp'=8,'seq'=32] {'dp'}, use_global_device_ids=true, to_apply=%add.4 | all-reduce | flops 256 | bytes 2048 | tf_op jit(solution)/shard_map/all_gather | solution.py:105
  198.5 2.4 pad.17
  208.4 130.1 %while.14 = (s32[]{:T(128)}, f32[1,4608,128]{2,1,0:T(8,128)}, f32[1,4608,128]{2,1,0:T(8,128)}, f32[8,1,512,128]{3,2,1,0:T(8,128)}, s32[8]{0:T(128)S(1)}, /*index...) while((s32[]{:T(128)}, f32[1,4608,128]{2,1,0:T(8,128)}, ...), condition=%wide.region_6.7_spmd, body=%wide.region_2.6_spmd.sunk | while | flops 820119040 | bytes 18283312 | solution.py:88
  282.9 2.4 fusion.70
  299.2 2.4 fusion.70
  315.5 2.4 fusion.70
  338.5 2.8 multiply_reduce_fusion
  341.3 4.9 multiply_convert_fusion.1
  348.6 16.4 %multiply_convert_fusion.2 = bf16[4096,1,128]{2,1,0:T(2,128)(2,1)} fusion(f32[4096,1,128]{2,1,0:T(1,128)S(1)} %bitcast.180, f32[4096,1,128]{2,1,0:T(1,128)S(1)} %bitcast.183, f32[4096]{0:T(1024)S(1)} %broadcast_multiply_fusion.1, f32[128]{0:T(128)S(1)} %get-tuple-element.153, f32[4096]{0:T(1024)S(1)} %get-tuple-element.158), kind=kLoop, calls=%fused_computation.51 | loop fusion | flops 3145728 | bytes 5276160 | tf_op jit(solution)/shard_map/convert_element_type | solution.py:92
  365.6 23.7 %reduce.15 = bf16[4096,128]{1,0:T(8,128)(2,1)S(1)} reduce(bf16[4096,1,128]{2,1,0:T(2,128)(2,1)} %multiply_convert_fusion.2, bf16[]{:T(256)} %broadcast.364), dimensions={1}, to_apply=%multiply_convert_fusion.2.reduce_sub_computation | reduce | bytes 2097154 | tf_op jit(solution)/shard_map/convert_element_type | solution.py:92
  390.3 10.8 %all-to-all-start.4 = ((bf16[32,2,8192]{2,1,0:T(2,128)(2,1)}), bf16[32,2,8192]{2,1,0:T(2,128)(2,1)S(1)}, u32[]{:S(2)}, u32[]{:S(2)}) async-start(bf16[32,2,8192]{2,1,0:T(2,128)(2,1)} %reshape.664), calls=%async_computation.4 | async-start | bytes 2097152 | tf_op jit(solution)/shard_map/all_to_all | solution.py:150
  401.1 2.7 reduce.16
  404.9 20.2 %all-to-all-done.4 = bf16[32,2,8192]{2,1,0:T(2,128)(2,1)S(1)} async-done(((bf16[32,2,8192]{2,1,0:T(2,128)(2,1)}), bf16[32,2,8192]{2,1,0:T(2,128)(2,1)S(1)}, u32[]{:S(2)}, u32[]{:S(2)}) %all-to-all-start.4) | async-done | bytes 1048608 | tf_op jit(solution)/shard_map/all_to_all | solution.py:150
  425.1 9.9 %all-to-all-start.5 = ((bf16[32,2,8192]{2,1,0:T(2,128)(2,1)}), bf16[32,2,8192]{2,1,0:T(2,128)(2,1)S(1)}, u32[]{:S(2)}, u32[]{:S(2)}) async-start(bf16[32,2,8192]{2,1,0:T(2,128)(2,1)} %reshape.666), calls=%async_computation.5 | async-start | bytes 2097152 | tf_op jit(solution)/shard_map/all_to_all | solution.py:151
  435.0 2.7 fusion.31
  437.7 3.3 reduce.17
  443.2 15.9 %all-to-all-done.5 = bf16[32,2,8192]{2,1,0:T(2,128)(2,1)S(1)} async-done(((bf16[32,2,8192]{2,1,0:T(2,128)(2,1)}), bf16[32,2,8192]{2,1,0:T(2,128)(2,1)S(1)}, u32[]{:S(2)}, u32[]{:S(2)}) %all-to-all-start.5) | async-done | bytes 1048608 | tf_op jit(solution)/shard_map/all_to_all | solution.py:151
  459.0 10.0 %all-to-all-start.6 = ((bf16[32,2,8192]{2,1,0:T(2,128)(2,1)}), bf16[32,2,8192]{2,1,0:T(2,128)(2,1)}, u32[]{:S(2)}, u32[]{:S(2)}) async-start(bf16[32,2,8192]{2,1,0:T(2,128)(2,1)} %reshape.668), calls=%async_computation.6 | async-start | bytes 2097152 | tf_op jit(solution)/shard_map/all_to_all | solution.py:152
  469.0 2.5 multiply_reduce_fusion.1
  471.6 25.9 %all-reduce.7 = (f32[1,128]{1,0:T(1,128)}, f32[1,128]{1,0:T(1,128)}) all-reduce(f32[1,128]{1,0:T(1,128)S(1)} %bitcast.196, f32[1,128]{1,0:T(1,128)S(1)} %bitcast.195), channel_id=1, replica_groups=mesh['dp'=8,'seq'=32] {'dp'}, use_global_device_ids=true, to_apply=%region_10.11 | all-reduce | flops 256 | bytes 2048 | tf_op jit(solution)/shard_map/psum | solution.py:157
  497.5 3.5 reshape.665
  506.2 3.5 reshape.667
  513.4 5.8 %reshape.669 = bf16[4096,1,128]{2,1,0:T(2,128)(2,1)} reshape(bf16[32,2,8192]{2,1,0:T(2,128)(2,1)} %all-to-all-done.6) | data formatting | bytes 2097152
  (193 shorter events, 155.3 us)
Async XLA Ops:
  0.6 1.2 copy-start
  0.6 15.1 %copy-start.5 = (bf16[128,4096]{1,0:T(8,128)(2,1)S(1)}, bf16[128,4096]{1,0:T(8,128)(2,1)}, u32[]{:S(2)}) copy-start(bf16[128,4096]{1,0:T(8,128)(2,1)} %param.11) | copy-start | bytes 3145732
  3.1 40.2 %all-to-all-start = ((bf16[128,32,128]{2,0,1:T(8,128)(2,1)}), bf16[128,32,128]{2,0,1:T(8,128)(2,1)S(1)}, u32[]{:S(2)}, u32[]{:S(2)}) async-start(bf16[128,32,128]{2,0,1:T(8,128)(2,1)} %copy_bitcast_fusion.2), calls=%async_computation | async-start | bytes 2097152 | tf_op jit(solution)/shard_map/all_to_all | solution.py:123
  43.3 35.2 %all-to-all-start.1 = ((bf16[128,32,128]{2,0,1:T(8,128)(2,1)}), bf16[128,32,128]{2,0,1:T(8,128)(2,1)S(1)}, u32[]{:S(2)}, u32[]{:S(2)}) async-start(bf16[128,32,128]{2,0,1:T(8,128)(2,1)} %copy_bitcast_fusion.1), calls=%async_computation.1 | async-start | bytes 2097152 | tf_op jit(solution)/shard_map/all_to_all | solution.py:124
  49.8 34.4 %copy-start.10 = (u32[256]{0:T(256)S(1)}, u32[256]{0:T(256)}, u32[]{:S(2)}) copy-start(u32[256]{0:T(256)} %constant.65) | copy-start | bytes 3076
  49.8 35.0 %copy-start.9 = (u32[256]{0:T(256)S(1)}, u32[256]{0:T(256)}, u32[]{:S(2)}) copy-start(u32[256]{0:T(256)} %constant.70) | copy-start | bytes 3076
  78.5 118.2 %copy-start.2 = (bf16[128,32,128]{2,0,1:T(8,128)(2,1)}, bf16[128,32,128]{2,0,1:T(8,128)(2,1)S(1)}, u32[]{:S(2)}) copy-start(bf16[128,32,128]{2,0,1:T(8,128)(2,1)S(1)} %all-to-all-done.1) | copy-start | bytes 3145732
  78.5 35.8 %all-to-all-start.3 = ((bf16[128,32,128]{2,0,1:T(8,128)(2,1)}), bf16[128,32,128]{2,0,1:T(8,128)(2,1)}, u32[]{:S(2)}, u32[]{:S(2)}) async-start(bf16[128,32,128]{2,0,1:T(8,128)(2,1)} %copy_bitcast_fusion), calls=%async_computation.3 | async-start | bytes 2097152 | tf_op jit(solution)/shard_map/all_to_all | solution.py:125
  86.1 35.8 %copy-start.7 = (f32[1,16]{1,0:T(1,128)S(1)}, f32[1,16]{1,0:T(1,128)}, u32[]{:S(2)}) copy-start(f32[1,16]{1,0:T(1,128)} %param.15) | copy-start | bytes 196
  86.1 35.9 %copy-start.6 = (s32[1,128]{1,0:T(1,128)S(1)}, s32[1,128]{1,0:T(1,128)}, u32[]{:S(2)}) copy-start(s32[1,128]{1,0:T(1,128)} %param.16) | copy-start | bytes 1540
  86.1 95.9 %copy-start.8 = (f32[1,16]{1,0:T(1,128)S(1)}, f32[1,16]{1,0:T(1,128)}, u32[]{:S(2)}) copy-start(f32[1,16]{1,0:T(1,128)} %param.14) | copy-start | bytes 196
  114.3 87.3 %all-to-all-start.2 = ((bf16[128,32,128]{0,2,1:T(8,128)(2,1)}), bf16[128,32,128]{0,2,1:T(8,128)(2,1)}, u32[]{:S(2)}, u32[]{:S(2)}) async-start(bf16[128,32,128]{0,2,1:T(8,128)(2,1)} %bitcast.187), calls=%async_computation.2 | async-start | bytes 2097152 | tf_op jit(solution)/shard_map/all_to_all | solution.py:126
  338.5 2.8 copy-start.1
  346.2 2.3 copy-start.4
  346.5 1.4 copy-start.3
  390.3 34.8 %all-to-all-start.4 = ((bf16[32,2,8192]{2,1,0:T(2,128)(2,1)}), bf16[32,2,8192]{2,1,0:T(2,128)(2,1)S(1)}, u32[]{:S(2)}, u32[]{:S(2)}) async-start(bf16[32,2,8192]{2,1,0:T(2,128)(2,1)} %reshape.664), calls=%async_computation.4 | async-start | bytes 2097152 | tf_op jit(solution)/shard_map/all_to_all | solution.py:150
  425.1 33.9 %all-to-all-start.5 = ((bf16[32,2,8192]{2,1,0:T(2,128)(2,1)}), bf16[32,2,8192]{2,1,0:T(2,128)(2,1)S(1)}, u32[]{:S(2)}, u32[]{:S(2)}) async-start(bf16[32,2,8192]{2,1,0:T(2,128)(2,1)} %reshape.666), calls=%async_computation.5 | async-start | bytes 2097152 | tf_op jit(solution)/shard_map/all_to_all | solution.py:151
  459.0 54.4 %all-to-all-start.6 = ((bf16[32,2,8192]{2,1,0:T(2,128)(2,1)}), bf16[32,2,8192]{2,1,0:T(2,128)(2,1)}, u32[]{:S(2)}, u32[]{:S(2)}) async-start(bf16[32,2,8192]{2,1,0:T(2,128)(2,1)} %reshape.668), calls=%async_computation.6 | async-start | bytes 2097152 | tf_op jit(solution)/shard_map/all_to_all | solution.py:152
where the time goes:
time: 533 us; the launch traced here: 523 us
  blocking collectives  124 us (23%)
  matrix products  91.6 us (17%)
  waiting for transfers between devices  88.7 us (17%)
  other arithmetic  78.9 us (15%)
  local copies, waits for them, and re-layouts  68.7 us (13%)
  starting transfers between devices  63.1 us (12%)
  loops' own time  5.55 us (1%)
    all_gather x1, blocking collectives, shards(): lax.all_gather(clip_ids, 'seq', axis=1, tiled=True)  60 us
    convert_element_type x2, other arithmetic, group_head(): norm_back(q_scale, q_unit, gain_q[:, None, :], dq_norm).astype(jnp.bfloat16)  40.1 us
    unnamed x43, local copies, waits for them, and re-layouts  34.8 us
    all_to_all x1, waiting for transfers between devices, shards(): lax.all_to_all(to_heads(queries), 'seq', split_axis=1, concat_axis=0, til...  26.4 us
    all_to_all x1, waiting for transfers between devices, shards(): lax.all_to_all(to_heads(keys), 'seq', split_axis=1, concat_axis=0, tiled=...  26.2 us
    psum x1, blocking collectives, shards(): gain_grad_q, gain_grad_k = lax.psum((gain_grad_q, gain_grad_k), 'dp')  25.9 us
    unnamed x1, blocking collectives  24.4 us
    all_to_all x1, waiting for transfers between devices, shards(): lax.all_to_all(to_tokens(grad_q), 'seq', split_axis=0, concat_axis=1, til...  20.2 us
  transfers between devices with their start and end apart: 7, of which 4 were waited for; matrix products, arithmetic and copies ran while one was open for 8% of the time, Pallas kernels for 0%

commit v1 on v0

v1 whole, which is shorter than its diff:
```python
import jax
import jax.numpy as jnp
from jax import lax
from jax.experimental import pallas as pl
from jax.experimental.pallas import tpu as pltpu
from jax.sharding import PartitionSpec as P

EPS = 1e-06
NEG = -1e30
HD = 128
ROWS = 128
PAIR = 256
HEADS = 16
ALIGN = 16
CAP = 1152
PADDED = CAP + PAIR
SCALE = HD**-0.5
LOG2E = 1.4426950408889634
BF = jnp.bfloat16
F32 = jnp.float32
CORE, A_L, B_L, A_R, B_R, N_L, N_R, PA_L, PB_L, PA_R, PB_R = range(11)


def aligned(index):
    return pl.multiple_of(index, ALIGN)


def lanes(position):
    return pl.ds(pl.multiple_of(position * HD, HD), HD)


def dims(*semantics):
    return pltpu.CompilerParams(
        dimension_semantics=semantics or ("arbitrary",), vmem_limit_bytes=48 * 1024 * 1024
    )


def pick_kernel(core_ref, q_ref, k_ref, v_ref, d_ref, out_ref):
    other = 1 - core_ref[0]
    for t, ref in enumerate((q_ref, k_ref, v_ref, d_ref)):
        for i in range(out_ref.shape[2] // HD):
            out_ref[t, :, i * HD : (i + 1) * HD] = ref[:, lanes(2 * i + other)]


def pick_other(core, tensors, per=4):
    return pl.pallas_call(
        pick_kernel,
        out_shape=jax.ShapeDtypeStruct((4, ROWS, HEADS * HD), BF),
        grid_spec=pltpu.PrefetchScalarGridSpec(
            num_scalar_prefetch=1,
            grid=(HEADS // per,),
            in_specs=[pl.BlockSpec((ROWS, 2 * per * HD), lambda j, m: (0, j))] * 4,
            out_specs=pl.BlockSpec((4, ROWS, per * HD), lambda j, m: (0, 0, j)),
        ),
        compiler_params=dims(),
    )(core, *tensors)


def fill_window(win, slot, core, own_refs, rec_ref, i):
    mine = pl.ds(pl.multiple_of(core * ROWS, ROWS), ROWS)
    theirs = pl.ds(pl.multiple_of((1 - core) * ROWS, ROWS), ROWS)
    for t, ref in enumerate(own_refs):
        win[slot, t, mine, :] = ref[:, lanes(2 * i + core)]
        win[slot, t, theirs, :] = rec_ref[t, :, i * HD : (i + 1) * HD]


def pack_kernel(meta, q_ref, k_ref, v_ref, d_ref, rec_ref, left_ref, right_ref, win):
    per = rec_ref.shape[2] // HD
    core = meta[CORE]
    for i in range(per):
        head = pl.program_id(0) * per + i
        fill_window(win, i, core, (q_ref, k_ref, v_ref, d_ref), rec_ref, i)
        to_left = jnp.where(head < meta[N_L], meta[PB_L] // ALIGN, 0)
        to_right = jnp.where(head >= meta[N_R], meta[PA_R] // ALIGN, 0)
        left_at = head * meta[PB_L]
        right_at = (HEADS - 1 - head) * meta[PA_R]
        tail = PAIR - meta[PA_R]

        def copy_left(n, carry):
            for t in range(4):
                left_ref[t, pl.ds(aligned(left_at + n * ALIGN), ALIGN), :] = win[
                    i, t, pl.ds(aligned(n * ALIGN), ALIGN), :
                ]
            return carry

        def copy_right(n, carry):
            for t in range(4):
                right_ref[t, pl.ds(aligned(right_at + n * ALIGN), ALIGN), :] = win[
                    i, t, pl.ds(aligned(tail + n * ALIGN), ALIGN), :
                ]
            return carry

        lax.fori_loop(0, to_left, copy_left, 0)
        lax.fori_loop(0, to_right, copy_right, 0)


def pack_halos(meta, tensors, rec, per=4):
    out = jax.ShapeDtypeStruct((4, CAP, HD), BF)
    whole = pl.BlockSpec((4, CAP, HD), lambda j, m: (0, 0, 0))
    return pl.pallas_call(
        pack_kernel,
        out_shape=(out, out),
        grid_spec=pltpu.PrefetchScalarGridSpec(
            num_scalar_prefetch=1,
            grid=(HEADS // per,),
            in_specs=[pl.BlockSpec((ROWS, 2 * per * HD), lambda j, m: (0, j))] * 4
            + [pl.BlockSpec((4, ROWS, per * HD), lambda j, m: (0, 0, j))],
            out_specs=(whole, whole),
            scratch_shapes=[pltpu.VMEM((per, 4, PAIR, HD), BF)],
        ),
        compiler_params=dims(),
    )(meta, *tensors, rec)


def matmul(a, b, contract_a, contract_b):
    return lax.dot_general(
        a, b, (((contract_a,), (contract_b,)), ((), ())), preferred_element_type=F32
    )


def norm_parts(rows, gain):
    widened = rows.astype(F32)
    scaled = lax.rsqrt(jnp.mean(widened * widened, axis=-1, keepdims=True) + EPS)
    unit_rows = widened * scaled
    return scaled, unit_rows, (unit_rows * gain).astype(BF)


def norm_back(scaled, unit_rows, gain, upper):
    weighted = gain * upper
    return scaled * (weighted - unit_rows * jnp.mean(unit_rows * weighted, axis=-1, keepdims=True))


def solve(q_rows, k_rows, v_rows, d_rows, gain_q, gain_k, bias, q_live):
    q_scale, q_unit, q_norm = norm_parts(q_rows, gain_q)
    k_scale, k_unit, k_norm = norm_parts(k_rows, gain_k)
    scores = matmul(k_norm, q_norm, 1, 1) * (SCALE * LOG2E) + bias
    exponent = jnp.exp2(scores - jnp.max(scores, axis=0, keepdims=True))
    total = jnp.sum(exponent, axis=0, keepdims=True)
    weights = (exponent * (q_live / total)).astype(BF)
    d_weights = matmul(v_rows, d_rows, 1, 1)
    wide = weights.astype(F32)
    row_delta = jnp.sum(wide * d_weights, axis=0, keepdims=True)
    d_scores = (wide * (d_weights - row_delta)).astype(BF)
    dq_norm = matmul(d_scores, k_norm, 0, 0) * SCALE
    dk_norm = matmul(d_scores, q_norm, 1, 0) * SCALE
    dv_rows = matmul(weights, d_rows, 1, 0)
    grads = (
        norm_back(q_scale, q_unit, gain_q, dq_norm).astype(BF),
        norm_back(k_scale, k_unit, gain_k, dk_norm).astype(BF),
        dv_rows.astype(BF),
    )
    gain_q_part = jnp.sum(dq_norm * q_unit, axis=0, keepdims=True)
    gain_k_part = jnp.sum(dk_norm * k_unit, axis=0, keepdims=True)
    return grads, gain_q_part, gain_k_part


def link_bias(code_row, code_col):
    return jnp.where((code_col == code_row) & (code_row >= 0), 0.0, NEG).astype(F32)


def mid_kernel(
    meta, q_ref, k_ref, v_ref, d_ref, rec_ref, gains_ref, row_ref, col_ref, out_ref, gg_ref, win, bias
):
    per = rec_ref.shape[2] // HD
    core = meta[CORE]

    @pl.when(pl.program_id(0) == 0)
    def _():
        bias[...] = link_bias(row_ref[0:1, :], col_ref[:, 0:1])

    q_live = (row_ref[0:1, :] >= 0).astype(F32)
    for i in range(per):
        fill_window(win, i, core, (q_ref, k_ref, v_ref, d_ref), rec_ref, i)
    for i in range(per):
        head = pl.program_id(0) * per + i
        gains = gains_ref[head]
        grads, part_q, part_k = solve(
            win[i, 0], win[i, 1], win[i, 2], win[i, 3], gains[0:1], gains[1:2], bias[...], q_live
        )
        for t in range(3):
            out_ref[t, :, i * HD : (i + 1) * HD] = grads[t]
        gg_ref[head] = jnp.concatenate([part_q, part_k], axis=0)


def own_specs(per):
    return [pl.BlockSpec((ROWS, 2 * per * HD), lambda j, m: (0, j))] * 4 + [
        pl.BlockSpec((4, ROWS, per * HD), lambda j, m: (0, 0, j))
    ]


def code_specs():
    return [
        pl.BlockSpec((HEADS, 2, HD), lambda j, m: (0, 0, 0)),
        pl.BlockSpec((8, PAIR), lambda j, m: (0, 0)),
        pl.BlockSpec((PAIR, 8), lambda j, m: (0, 0)),
    ]


def solve_mid(meta, tensors, rec, gains, code_rows, code_cols, per=2):
    return pl.pallas_call(
        mid_kernel,
        out_shape=(
            jax.ShapeDtypeStruct((3, PAIR, HEADS * HD), BF),
            jax.ShapeDtypeStruct((HEADS, 2, HD), F32),
        ),
        grid_spec=pltpu.PrefetchScalarGridSpec(
            num_scalar_prefetch=1,
            grid=(HEADS // per,),
            in_specs=own_specs(per) + code_specs(),
            out_specs=(
                pl.BlockSpec((3, PAIR, per * HD), lambda j, m: (0, 0, j)),
                pl.BlockSpec((HEADS, 2, HD), lambda j, m: (0, 0, 0)),
            ),
            scratch_shapes=[
                pltpu.VMEM((per, 4, PAIR, HD), BF),
                pltpu.VMEM((PAIR, PAIR), F32),
            ],
        ),
        compiler_params=dims(),
    )(meta, *tensors, rec, gains, code_rows, code_cols)


def edge_kernel(
    meta,
    q_ref,
    k_ref,
    v_ref,
    d_ref,
    rec_ref,
    gains_ref,
    row_ref,
    col_ref,
    mid_ref,
    gg_mid_ref,
    from_left,
    from_right,
    out_ref,
    gg_ref,
    to_left,
    to_right,
    win,
    bias,
    held_left,
    held_right,
    back_left,
    back_right,
    sems,
):
    per = rec_ref.shape[2] // HD
    core = meta[CORE]
    step = pl.program_id(0)
    row = lax.broadcasted_iota(jnp.int32, (PAIR, HD), 0)

    @pl.when(step == 0)
    def _():
        copies = [
            pltpu.make_async_copy(from_left, held_left.at[:, pl.ds(PAIR, CAP), :], sems.at[0]),
            pltpu.make_async_copy(from_right, held_right.at[:, pl.ds(0, CAP), :], sems.at[1]),
        ]
        for copy in copies:
            copy.start()
        for side in range(2):
            bias[side] = link_bias(
                row_ref[side + 1 : side + 2, :], col_ref[:, side + 1 : side + 2]
            )
        for copy in copies:
            copy.wait()

    out_ref[...] = mid_ref[...]
    for i in range(per):
        fill_window(win, i, core, (q_ref, k_ref, v_ref, d_ref), rec_ref, i)
    for i in range(per):
        head = step * per + i
        gains = gains_ref[head]
        gg_ref[head] = gg_mid_ref[head]
        cols = slice(i * HD, (i + 1) * HD)

        def side_solve(side, held, back, at, halo, local):
            live = (row_ref[side + 1 : side + 2, :] >= 0).astype(F32)
            span = pl.ds(aligned(at), PAIR)
            window = [jnp.where(halo, held[t, span, :], win[i, t]) for t in range(4)]
            grads, part_q, part_k = solve(*window, gains[0:1], gains[1:2], bias[side], live)
            for t in range(3):
                back[t, span, :] = grads[t]
                out_ref[t, :, cols] = jnp.where(local, grads[t], out_ref[t, :, cols])
            gg_ref[head] += jnp.concatenate([part_q, part_k], axis=0)

        @pl.when(head >= meta[N_L])
        def _():
            side_solve(
                0,
                held_left,
                back_left,
                (HEADS - head) * meta[PA_L],
                row >= PAIR - meta[A_L],
                row < meta[B_L],
            )

        @pl.when(head < meta[N_R])
        def _():
            side_solve(
                1,
                held_right,
                back_right,
                head * meta[PB_R],
                row < meta[B_R],
                row >= PAIR - meta[A_R],
            )

    @pl.when(step == pl.num_programs(0) - 1)
    def _():
        copies = [
            pltpu.make_async_copy(back_left.at[:, pl.ds(PAIR, CAP), :], to_left, sems.at[0]),
            pltpu.make_async_copy(back_right.at[:, pl.ds(0, CAP), :], to_right, sems.at[1]),
        ]
        for copy in copies:
            copy.start()
        for copy in copies:
            copy.wait()


def solve_edges(meta, tensors, rec, gains, code_rows, code_cols, mid, gg_mid, halos, per=2):
    block = pl.BlockSpec((3, PAIR, per * HD), lambda j, m: (0, 0, j))
    small = pl.BlockSpec((HEADS, 2, HD), lambda j, m: (0, 0, 0))
    anywhere = pl.BlockSpec(memory_space=pl.ANY)
    back = jax.ShapeDtypeStruct((3, CAP, HD), BF)
    return pl.pallas_call(
        edge_kernel,
        out_shape=(
            jax.ShapeDtypeStruct((3, PAIR, HEADS * HD), BF),
            jax.ShapeDtypeStruct((HEADS, 2, HD), F32),
            back,
            back,
        ),
        grid_spec=pltpu.PrefetchScalarGridSpec(
            num_scalar_prefetch=1,
            grid=(HEADS // per,),
            in_specs=own_specs(per) + code_specs() + [block, small, anywhere, anywhere],
            out_specs=(block, small, anywhere, anywhere),
            scratch_shapes=[
                pltpu.VMEM((per, 4, PAIR, HD), BF),
                pltpu.VMEM((2, PAIR, PAIR), F32),
                pltpu.VMEM((4, PADDED, HD), BF),
                pltpu.VMEM((4, PADDED, HD), BF),
                pltpu.VMEM((3, PADDED, HD), BF),
                pltpu.VMEM((3, PADDED, HD), BF),
                pltpu.SemaphoreType.DMA((2,)),
            ],
        ),
        compiler_params=dims(),
    )(meta, *tensors, rec, gains, code_rows, code_cols, mid, gg_mid, *halos)


def merge_kernel(meta, own_ref, from_left, from_right, keep_ref, send_ref, held, win, sems):
    per = own_ref.shape[2] // HD
    core = meta[CORE]
    row = lax.broadcasted_iota(jnp.int32, (PAIR, HD), 0)

    @pl.when(pl.program_id(0) == 0)
    def _():
        copies = [
            pltpu.make_async_copy(from_left, held.at[0, :, pl.ds(0, CAP), :], sems.at[0]),
            pltpu.make_async_copy(from_right, held.at[1, :, pl.ds(PAIR, CAP), :], sems.at[1]),
        ]
        for copy in copies:
            copy.start()
        for copy in copies:
            copy.wait()

    mine = pl.ds(pl.multiple_of(core * ROWS, ROWS), ROWS)
    theirs = pl.ds(pl.multiple_of((1 - core) * ROWS, ROWS), ROWS)
    for i in range(per):
        head = pl.program_id(0) * per + i
        use_left = head < meta[N_L]
        use_right = head >= meta[N_R]
        left_at = jnp.where(use_left, head * meta[PB_L], 0)
        right_at = jnp.where(use_right, (HEADS - head) * meta[PA_R], 0)
        head_rows = jnp.where(use_left, meta[B_L], 0)
        tail_row = jnp.where(use_right, PAIR - meta[A_R], PAIR)
        cols = slice(i * HD, (i + 1) * HD)
        for t in range(3):
            rows = own_ref[t, :, cols]
            rows = jnp.where(row < head_rows, held[0, t, pl.ds(aligned(left_at), PAIR), :], rows)
            rows = jnp.where(row >= tail_row, held[1, t, pl.ds(aligned(right_at), PAIR), :], rows)
            win[i, t] = rows
        for t in range(3):
            keep_ref[t, :, cols] = win[i, t, mine, :]
            send_ref[t, :, cols] = win[i, t, theirs, :]


def merge_returns(meta, own, returned, per=4):
    out = jax.ShapeDtypeStruct((3, ROWS, HEADS * HD), BF)
    half = pl.BlockSpec((3, ROWS, per * HD), lambda j, m: (0, 0, j))
    anywhere = pl.BlockSpec(memory_space=pl.ANY)
    return pl.pallas_call(
        merge_kernel,
        out_shape=(out, out),
        grid_spec=pltpu.PrefetchScalarGridSpec(
            num_scalar_prefetch=1,
            grid=(HEADS // per,),
            in_specs=[
                pl.BlockSpec((3, PAIR, per * HD), lambda j, m: (0, 0, j)),
                anywhere,
                anywhere,
            ],
            out_specs=(half, half),
            scratch_shapes=[
                pltpu.VMEM((2, 3, PADDED, HD), BF),
                pltpu.VMEM((per, 3, PAIR, HD), BF),
                pltpu.SemaphoreType.DMA((2,)),
            ],
        ),
        compiler_params=dims(),
    )(meta, own, *returned)


def weave_kernel(core_ref, keep_ref, rec_ref, *outs):
    core = core_ref[0]
    for t, out in enumerate(outs):
        for i in range(keep_ref.shape[2] // HD):
            cols = slice(i * HD, (i + 1) * HD)
            out[:, lanes(2 * i + core)] = keep_ref[t, :, cols]
            out[:, lanes(2 * i + 1 - core)] = rec_ref[t, :, cols]


def weave(core, keep, rec, per=4):
    half = pl.BlockSpec((3, ROWS, per * HD), lambda j, m: (0, 0, j))
    return pl.pallas_call(
        weave_kernel,
        out_shape=(jax.ShapeDtypeStruct((ROWS, 2 * HEADS * HD), BF),) * 3,
        grid_spec=pltpu.PrefetchScalarGridSpec(
            num_scalar_prefetch=1,
            grid=(HEADS // per,),
            in_specs=[half, half],
            out_specs=(pl.BlockSpec((ROWS, 2 * per * HD), lambda j, m: (0, j)),) * 3,
        ),
        compiler_params=dims(),
    )(core, keep, rec)


def edge_split(long_a, long_b):
    blocks_a = (long_a + ALIGN - 1) // ALIGN
    blocks_b = (long_b + ALIGN - 1) // ALIGN
    both = jnp.maximum(blocks_a + blocks_b, 1)
    to_left = (2 * HEADS * blocks_a + both) // (2 * both)
    return blocks_a * ALIGN, blocks_b * ALIGN, to_left


def plan(core, chip, chips, ids, counts, left, right):
    left_ids, left_counts = left
    right_ids, right_counts = right
    slot = jnp.arange(PAIR, dtype=jnp.int32)

    def live(pair_counts):
        return slot % ROWS < jnp.where(slot < ROWS, pair_counts[0], pair_counts[1])

    def run(same, crosses):
        return jnp.where(crosses, jnp.sum(same.astype(jnp.int32)), 0)

    cross_l = (chip > 0) & (left_ids[PAIR - 1] == ids[0])
    cross_r = (chip < chips - 1) & (right_ids[0] == ids[PAIR - 1])
    a_l = run(left_ids == left_ids[PAIR - 1], cross_l)
    b_l = run(ids == ids[0], cross_l)
    a_r = run(ids == ids[PAIR - 1], cross_r)
    b_r = run(right_ids == right_ids[0], cross_r)
    pa_l, pb_l, n_l = edge_split(a_l, b_l)
    pa_r, pb_r, n_r = edge_split(a_r, b_r)
    n_l = jnp.where(cross_l, n_l, HEADS)
    n_r = jnp.where(cross_r, n_r, 0)
    own_live = live(counts)
    head_l = slot < b_l
    tail_r = slot >= PAIR - a_r
    code_m = jnp.where(own_live & ~head_l & ~tail_r, ids, -1)
    code_l = jnp.where((own_live & head_l) | (live(left_counts) & (slot >= PAIR - a_l)), 0, -1)
    code_r = jnp.where((own_live & tail_r) | (live(right_counts) & (slot < b_r)), 0, -1)
    codes = jnp.stack([code_m, code_l, code_r] + [code_m] * 5)
    meta = jnp.stack(
        [core, a_l, b_l, a_r, b_r, n_l, n_r, pa_l, pb_l, pa_r, pb_r] + [core] * 5
    ).astype(jnp.int32)
    return meta, codes, codes.T


def shards(queries, keys, values, out_grad, gain_q, gain_k, clip_ids, counts):
    size = lax.axis_size("seq")
    groups = lax.axis_size("dp")
    chips = size // 2
    seq = lax.axis_index("seq")
    core = seq % 2
    chip = seq // 2
    swap = [(i, i ^ 1) for i in range(size)]
    rightward = [(i, i + 2) for i in range(size - 2)]
    leftward = [(i + 2, i) for i in range(size - 2)]
    same_core = [list(range(0, size, 2)), list(range(1, size, 2))]
    core_at = core.reshape(1).astype(jnp.int32)
    tensors = (queries, keys, values, out_grad)

    info = jnp.concatenate([clip_ids, jnp.broadcast_to(counts, (1, ROWS))], axis=0)
    info_other = lax.ppermute(info, "seq", swap)
    first = jnp.where(core == 0, info, info_other)
    second = jnp.where(core == 0, info_other, info)
    chip_info = jnp.stack([first, second])
    info_left = lax.ppermute(chip_info, "seq", rightward)
    info_right = lax.ppermute(chip_info, "seq", leftward)

    def parts(table):
        return table[:, 0, :].reshape(PAIR), table[:, 1, 0]

    meta, code_rows, code_cols = plan(
        core, chip, chips, *parts(chip_info), parts(info_left), parts(info_right)
    )

    rec = lax.ppermute(pick_other(core_at, tensors), "seq", swap)

    gain_own = jnp.concatenate([gain_q, gain_k], axis=0)
    gain_cols = lax.all_to_all(
        jnp.broadcast_to(gain_own[None], (groups,) + gain_own.shape), "dp", 0, 0, tiled=True
    )
    gain_row = gain_cols.transpose(1, 0, 2).reshape(2, HD)
    gains = lax.all_to_all(
        jnp.broadcast_to(gain_row[None], (chips, 2, HD)),
        "seq",
        0,
        0,
        axis_index_groups=same_core,
        tiled=True,
    )

    send_left, send_right = pack_halos(meta, tensors, rec)
    from_left = lax.ppermute(send_right, "seq", rightward)
    from_right = lax.ppermute(send_left, "seq", leftward)

    mid, gg_mid = solve_mid(meta, tensors, rec, gains, code_rows, code_cols)
    own, gg, back_left, back_right = solve_edges(
        meta, tensors, rec, gains, code_rows, code_cols, mid, gg_mid, (from_left, from_right)
    )
    returned_right = lax.ppermute(back_left, "seq", leftward)
    returned_left = lax.ppermute(back_right, "seq", rightward)

    gg_parts = lax.all_to_all(gg, "seq", 0, 0, axis_index_groups=same_core, tiled=True)
    gg_head = jnp.sum(gg_parts, axis=0)
    gg_sum = lax.psum(gg_head, "dp")

    keep, send = merge_returns(meta, own, (returned_left, returned_right))
    grads = weave(core_at, keep, lax.ppermute(send, "seq", swap))
    return (*grads, gg_sum[0:1], gg_sum[1:2])


def solution(mesh):
    rows = P(("dp", "seq"), None)
    cells = P("seq", "dp")
    slots = P("dp", "seq")
    return jax.shard_map(
        shards,
        mesh=mesh,
        in_specs=(rows, rows, rows, rows, cells, cells, slots, slots),
        out_specs=(rows, rows, rows, P("seq", None), P("seq", None)),
        check_vma=False,
    )
```

time: 533 us -> 245 us (0.46); the launches traced: 523 us -> 242 us
  matrix products: 91.6 us -> 0 us
  other arithmetic: 78.9 us -> 9.7 us
  waiting for transfers between devices: 88.7 us -> 21.9 us
  blocking collectives: 124 us -> 57.2 us
  local copies, waits for them, and re-layouts: 68.7 us -> 13.3 us
  Pallas kernels: 0 us -> 42.4 us
  starting transfers between devices: 63.1 us -> 91.1 us
  loops' own time: 5.55 us -> 0 us
    dot_general x48 -> x0, matrix products: 91.6 us -> none  [the longest x8 19.2 us: attend(): jnp.einsum('brc,brd->bcd', d_scores, q_norm, preferred_element_type=jnp.f...]
    all_to_all x7 -> x2, waiting for transfers between devices: 88.7 us -> 6.38 us  [the longest x1 3.91 us: shards(): lax.all_to_all(jnp.broadcast_to(gain_own[None], (groups,) + gain_own.shap...]
    all_gather x2 -> x0, blocking collectives: 73.9 us -> none  [the longest x1 60 us: shards(): lax.all_gather(clip_ids, 'seq', axis=1, tiled=True)]
    convert_element_type x15 -> x0, other arithmetic: 56.4 us -> none  [the longest x2 40.1 us: group_head(): norm_back(q_scale, q_unit, gain_q[:, None, :], dq_norm).astype(jnp.bfloat16)]
    pallas_call x0 -> x6, Pallas kernels: none -> 42.4 us  [the longest x1 13.8 us: solve_mid(): pl.pallas_call(mid_kernel, out_shape=(jax.ShapeDtypeStruct((3, PAIR, HEAD...]
    all_to_all x0 -> x1, blocking collectives: none -> 39.8 us  [shards(): lax.all_to_all(gg, 'seq', 0, 0, axis_index_groups=same_core, tiled=True)]
    ppermute x0 -> x9, starting transfers between devices: none -> 37.4 us  [the longest x1 12 us: shards(): grads = weave(core_at, keep, lax.ppermute(send, 'seq', swap))]
    unnamed x43 -> x24, local copies, waits for them, and re-layouts: 34.8 us -> 7.36 us
  transfers between devices with their start and end apart: 7 -> 11, of which waited for: 4 -> 5; matrix products, arithmetic and copies ran while one was open for 8% -> 6% of each run, Pallas kernels for 0% -> 6%
where the time goes in v1:
time: 245 us; the launch traced here: 242 us
  starting transfers between devices  91.1 us (37%)
  blocking collectives  57.2 us (23%)
  Pallas kernels  42.4 us (17%)
  waiting for transfers between devices  21.9 us (9%)
  local copies, waits for them, and re-layouts  13.3 us (5%)
  other arithmetic  9.7 us (4%)
  between operations  6.94 us (3%)
    all_to_all x1, starting transfers between devices, shards(): lax.all_to_all(jnp.broadcast_to(gain_row[None], (chips, 2, HD)), 'seq', 0...  49 us
    all_to_all x1, blocking collectives, shards(): lax.all_to_all(gg, 'seq', 0, 0, axis_index_groups=same_core, tiled=True)  39.8 us
    psum x1, blocking collectives, shards(): gg_sum = lax.psum(gg_head, 'dp')  17.4 us
    pallas_call x1, Pallas kernels, solve_mid(): pl.pallas_call(mid_kernel, out_shape=(jax.ShapeDtypeStruct((3, PAIR, HEAD...  13.8 us
    pallas_call x1, Pallas kernels, solve_edges(): pl.pallas_call(edge_kernel, out_shape=(jax.ShapeDtypeStruct((3, PAIR, HEA...  12.2 us
    ppermute x1, starting transfers between devices, shards(): grads = weave(core_at, keep, lax.ppermute(send, 'seq', swap))  12 us
    ppermute x1, starting transfers between devices, shards(): returned_left = lax.ppermute(back_right, 'seq', rightward)  10.9 us
    ppermute x1, waiting for transfers between devices, shards(): returned_left = lax.ppermute(back_right, 'seq', rightward)  8.61 us
  transfers between devices with their start and end apart: 11, of which 5 were waited for; matrix products, arithmetic and copies ran while one was open for 6% of the time, Pallas kernels for 6%

profile of v1, /device:TPU:1, one launch (start us, length us, event | category | flops | bytes accessed | tf_op | source)
XLA Modules:
  0.0 242.5 jit_solution(4126584599752690284)
XLA Ops:
  1.9 1.2 copy-done.2
  3.1 1.2 copy-done.4
  4.3 1.2 copy-done.6
  5.6 2.4 %shard_map.119 = bf16[4,128,2048]{2,1,0:T(8,128)(2,1)} custom-call(s32[1]{0:T(128)} %bitcast.core_ref, bf16[128,4096]{1,0:T(8,128)(2,1)S(1)} %copy-done, bf16[128,4096]{1,0:T(8,128)(2,1)S(1)} %copy-done.2, bf16[128,4096]{1,0:T(8,128)(2,1)S(1)} %copy-done.4, bf16[128,4096]{1,0:T(8,128)(2,1)S(1)} %copy-done.6), custom_call_target="tpu_custom_call" | custom-call | tf_op jit(solution)/shard_map/pallas_call | solution.py:46
  8.0 3.2 %collective-permute-start.3 = (bf16[4,128,2048]{2,1,0:T(8,128)(2,1)}, bf16[4,128,2048]{2,1,0:T(8,128)(2,1)}, u32[]{:S(2)}, u32[]{:S(2)}) collective-permute-start(bf16[4,128,2048]{2,1,0:T(8,128)(2,1)} %shard_map.119), channel_id=1, source_target_pairs={{0,1},{1,0},{2,3},{3,2},{4,5},{5,4},{6,7},{7,6},{8,9},{9,8},{10,11... | collective-permute-start | bytes 6291464 | tf_op jit(solution)/shard_map/ppermute | solution.py:512
  12.0 3.0 %collective-permute-done = s32[2,128]{1,0:T(2,128)S(1)} collective-permute-done((s32[2,128]{1,0:T(2,128)S(1)}, s32[2,128]{1,0:T(2,128)S(1)}, u32[]{:S(2)}, u32[]{:S(2)}) %collective-permute-start) | collective-permute-done | bytes 1056 | tf_op jit(solution)/shard_map/ppermute | solution.py:498
  15.0 1.3 collective-permute-start.2
  16.3 4.0 %collective-permute-start.1 = (s32[2,2,128]{2,1,0:T(2,128)S(1)}, s32[2,2,128]{2,1,0:T(2,128)S(1)}, u32[]{:S(2)}, u32[]{:S(2)}) collective-permute-start(s32[2,2,128]{2,1,0:T(2,128)S(1)} %pad_add_fusion), channel_id=1, source_target_pairs={{0,2},{1,3},{2,4},{3,5},{4,6},{5,7},{6,8},{7,9},{8,10},{9,11},{10,... | collective-permute-start | bytes 6152 | tf_op jit(solution)/shard_map/ppermute | solution.py:502
  20.9 1.9 fusion.3
  24.7 1.3 fusion.4
  29.9 1.3 fusion.1
  33.3 5.5 %shard_map.121 = (bf16[4,1152,128]{2,1,0:T(8,128)(2,1)}, bf16[4,1152,128]{2,1,0:T(8,128)(2,1)}) custom-call(s32[16]{0:T(128)S(1)} %stack.72.meta, bf16[128,4096]{1,0:T(8,128)(2,1)S(1)} %copy-done.1, bf16[128,4096]{1,0:T(8,128)(2,1)S(1)} %copy-done.3, bf16[128,4096]{1,0:T(8,128)(2,1)S(1)} %copy-done.5, bf16[128,4096]{1,0:T(8,128)(2,1)S(1)} %copy-done.7, ...), custom_call_target="tpu_custom_call" | custom-call | tf_op jit(solution)/shard_map/pallas_call | solution.py:100
  38.7 3.3 %collective-permute-start.4 = (bf16[4,1152,128]{2,1,0:T(8,128)(2,1)}, bf16[4,1152,128]{2,1,0:T(8,128)(2,1)}, u32[]{:S(2)}, u32[]{:S(2)}) collective-permute-start(bf16[4,1152,128]{2,1,0:T(8,128)(2,1)} %get-tuple-element.20), channel_id=1, source_target_pairs={{0,2},{1,3},{2,4},{3,5},{4,6},{5,7},{6,8},{7,9},{8,10},{9,11},{10,... | collective-permute-start | bytes 3538952 | tf_op jit(solution)/shard_map/ppermute | solution.py:529
  42.0 1.3 collective-permute-start.5
  44.0 4.8 %all-to-all-start = ((f32[8,2,16]{2,1,0:T(2,128)}), f32[8,2,16]{2,1,0:T(2,128)S(1)}, u32[]{:S(2)}, u32[]{:S(2)}) async-start(f32[8,2,16]{2,1,0:T(2,128)} %broadcast_in_dim.49), calls=%async_computation | async-start | bytes 16384 | tf_op jit(solution)/shard_map/all_to_all | solution.py:515
  49.9 3.9 %all-to-all-done = f32[8,2,16]{2,1,0:T(2,128)S(1)} async-done(((f32[8,2,16]{2,1,0:T(2,128)}), f32[8,2,16]{2,1,0:T(2,128)S(1)}, u32[]{:S(2)}, u32[]{:S(2)}) %all-to-all-start) | async-done | bytes 1056 | tf_op jit(solution)/shard_map/all_to_all | solution.py:515
  54.5 49.0 %all-to-all-start.1 = ((f32[16,2,128]{2,1,0:T(2,128)}), f32[16,2,128]{2,1,0:T(2,128)S(1)}, u32[]{:S(2)}, u32[]{:S(2)}) async-start(f32[16,2,128]{2,1,0:T(2,128)} %broadcast_in_dim.51), calls=%async_computation.1 | async-start | bytes 32768 | tf_op jit(solution)/shard_map/all_to_all | solution.py:519
  104.5 2.6 %or_select_fusion.1 = (s32[1,256]{1,0:T(1,128)S(1)}, s32[1,256]{1,0:T(1,128)S(1)}) fusion(s32[]{:T(128)S(6)} %sub.53, s32[]{:T(128)} %bitcast.26, s32[]{:T(128)} %bitcast.25, s32[]{:T(128)} %select_n.167, s32[]{:T(128)} %bitcast.23, s32[]{:T(128)} %bitcast.22, s32[2,1,128]{2,1,0:T(1,128)S(1)} %fusion, s32[]{:T(128)S(6)} %sub.52), kind=kLoop, calls=%fused_computation.1 | loop fusion | flops 5888 | bytes 3100 | tf_op jit(solution)/shard_map/jit(_where)/select_n | solution.py:474
  107.1 2.5 %or_select_fusion = s32[1,256]{1,0:T(1,128)S(1)} fusion(s32[]{:T(128)} %select_n.169, s32[]{:T(128)} %bitcast.28, s32[]{:T(128)} %bitcast.27, s32[]{:T(128)S(6)} %sub.52, s32[]{:T(128)} %bitcast.23, s32[]{:T(128)} %bitcast.22), kind=kLoop, calls=%fused_computation | loop fusion | flops 4352 | bytes 1048 | tf_op jit(solution)/shard_map/jit(_where)/select_n | solution.py:475
  109.8 2.5 %all-to-all-done.1.gains_ref = f32[16,2,128]{2,1,0:T(2,128)S(1)} async-done(((f32[16,2,128]{2,1,0:T(2,128)}), f32[16,2,128]{2,1,0:T(2,128)S(1)}, u32[]{:S(2)}, u32[]{:S(2)}) %all-to-all-start.1) | async-done | bytes 16416 | tf_op jit(solution)/shard_map/all_to_all | solution.py:519
  112.3 1.2 copy-done.8
  113.5 13.8 %shard_map.120 = (bf16[3,256,2048]{2,1,0:T(8,128)(2,1)}, f32[16,2,128]{2,1,0:T(2,128)S(1)}) custom-call(s32[16]{0:T(128)S(1)} %stack.72.meta, bf16[128,4096]{1,0:T(8,128)(2,1)S(1)} %copy-done.1, bf16[128,4096]{1,0:T(8,128)(2,1)S(1)} %copy-done.3, bf16[128,4096]{1,0:T(8,128)(2,1)S(1)} %copy-done.5, bf16[128,4096]{1,0:T(8,128)(2,1)S(1)} %copy-done.8, ...), custom_call_target="tpu_custom_call" | custom-call | tf_op jit(solution)/shard_map/pallas_call | solution.py:200
  127.3 12.2 %shard_map.122 = (bf16[3,256,2048]{2,1,0:T(8,128)(2,1)}, f32[16,2,128]{2,1,0:T(2,128)S(1)}, bf16[3,1152,128]{2,1,0:T(8,128)(2,1)S(1)}, bf16[3,1152,128]{2,1,0:T(8,128)(2,1)S(1)}) custom-call(s32[16]{0:T(128)S(1)} %stack.72.meta, bf16[128,4096]{1,0:T(8,128)(2,1)S(1)} %copy-done.1, bf16[128,4096]{1,0:T(8,128)(2,1)S(1)} %copy-done.3, ...), custom_call_target="tpu_custom_call" | custom-call | tf_op jit(solution)/shard_map/pallas_call | solution.py:327
  139.5 10.9 %collective-permute-start.6 = (bf16[3,1152,128]{2,1,0:T(8,128)(2,1)S(1)}, bf16[3,1152,128]{2,1,0:T(8,128)(2,1)S(1)}, u32[]{:S(2)}, u32[]{:S(2)}) collective-permute-start(bf16[3,1152,128]{2,1,0:T(8,128)(2,1)S(1)} %get-tuple-element.23), channel_id=1, source_target_pairs={{0,2},{1,3},{2,4},{3,5},{4,6},{5,7},{6,8},{7,9},{8,10},{9,11},{10,... | collective-permute-start | bytes 2654216 | tf_op jit(solution)/shard_map/ppermute | solution.py:537
  150.4 1.3 collective-permute-start.7
  151.7 8.6 %collective-permute-done.6.from_left = bf16[3,1152,128]{2,1,0:T(8,128)(2,1)S(1)} collective-permute-done((bf16[3,1152,128]{2,1,0:T(8,128)(2,1)S(1)}, bf16[3,1152,128]{2,1,0:T(8,128)(2,1)S(1)}, u32[]{:S(2)}, u32[]{:S(2)}) %collective-permute-start.6) | collective-permute-done | bytes 884768 | tf_op jit(solution)/shard_map/ppermute | solution.py:537
  160.3 3.9 %collective-permute-done.7.from_right = bf16[3,1152,128]{2,1,0:T(8,128)(2,1)S(1)} collective-permute-done((bf16[3,1152,128]{2,1,0:T(8,128)(2,1)S(1)}, bf16[3,1152,128]{2,1,0:T(8,128)(2,1)S(1)}, u32[]{:S(2)}, u32[]{:S(2)}) %collective-permute-start.7) | collective-permute-done | bytes 884768 | tf_op jit(solution)/shard_map/ppermute | solution.py:536
  164.2 5.9 %shard_map.123 = (bf16[3,128,2048]{2,1,0:T(8,128)(2,1)S(1)}, bf16[3,128,2048]{2,1,0:T(8,128)(2,1)}) custom-call(s32[16]{0:T(128)S(1)} %stack.72.meta, bf16[3,256,2048]{2,1,0:T(8,128)(2,1)} %get-tuple-element.22.own_ref, bf16[3,1152,128]{2,1,0:T(8,128)(2,1)S(1)} %collective-permute-done.6.from_left, bf16[3,1152,128]{2,1,0:T(8,128)(2,1)S(1)} %collective-permute-done.7.from_right), custom_call_target="tpu_custom_call" | custom-call | tf_op jit(solution)/shard_map/pallas_call | solution.py:395
  170.1 12.0 %collective-permute-start.8 = (bf16[3,128,2048]{2,1,0:T(8,128)(2,1)}, bf16[3,128,2048]{2,1,0:T(8,128)(2,1)S(1)}, u32[]{:S(2)}, u32[]{:S(2)}) collective-permute-start(bf16[3,128,2048]{2,1,0:T(8,128)(2,1)} %get-tuple-element.26), channel_id=1, source_target_pairs={{0,1},{1,0},{2,3},{3,2},{4,5},{5,4},{6,7},{7,6},{8,9},{9,8},{10,11... | collective-permute-start | bytes 4718600 | tf_op jit(solution)/shard_map/ppermute | solution.py:544
  182.1 39.8 %all_to_all.15 = f32[16,2,128]{2,1,0:T(2,128)S(1)} all-to-all(f32[16,2,128]{2,1,0:T(2,128)S(1)} %get-tuple-element.30), channel_id=1, replica_groups={{0,2,4,6,8,10,12,14,16,18,20,22,24,26,28,30},{1,3,5,7,9,11,13,15,17,19,..., dimensions={0} | all-to-all | bytes 32768 | tf_op jit(solution)/shard_map/all_to_all | solution.py:539
  221.9 17.4 %psum.7 = f32[2,128]{1,0:T(2,128)S(1)} all-reduce(f32[2,128]{1,0:T(2,128)S(1)} %reduce_sum.49), channel_id=1, replica_groups=mesh['dp'=8,'seq'=32] {'dp'}, use_global_device_ids=true, to_apply=%region_5.6 | all-reduce | flops 256 | bytes 2048 | tf_op jit(solution)/shard_map/psum | solution.py:541
  239.9 2.6 %shard_map.124 = (bf16[128,4096]{1,0:T(8,128)(2,1)}, bf16[128,4096]{1,0:T(8,128)(2,1)}, bf16[128,4096]{1,0:T(8,128)(2,1)}) custom-call(s32[1]{0:T(128)} %bitcast.core_ref, bf16[3,128,2048]{2,1,0:T(8,128)(2,1)S(1)} %get-tuple-element.25.keep_ref, bf16[3,128,2048]{2,1,0:T(8,128)(2,1)S(1)} %collective-permute-done.8.rec_ref), custom_call_target="tpu_custom_call" | custom-call | tf_op jit(solution)/shard_map/pallas_call | solution.py:428
  (50 shorter events, 8.5 us)
Async XLA Ops:
  0.6 1.2 copy-start
  1.9 1.2 copy-start.2
  3.1 1.2 copy-start.4
  4.3 1.2 copy-start.6
  5.5 6.3 %copy-start.9 = (s32[1,128]{1,0:T(1,128)S(1)}, s32[1,128]{1,0:T(1,128)}, u32[]{:S(2)}) copy-start(s32[1,128]{1,0:T(1,128)} %param.14) | copy-start | bytes 1540
  5.5 26.5 %copy-start.1 = (bf16[128,4096]{1,0:T(8,128)(2,1)S(1)}, bf16[128,4096]{1,0:T(8,128)(2,1)}, u32[]{:S(2)}) copy-start(bf16[128,4096]{1,0:T(8,128)(2,1)} %q_ref.7) | copy-start | bytes 3145732
  5.6 26.5 %copy-start.3 = (bf16[128,4096]{1,0:T(8,128)(2,1)S(1)}, bf16[128,4096]{1,0:T(8,128)(2,1)}, u32[]{:S(2)}) copy-start(bf16[128,4096]{1,0:T(8,128)(2,1)} %k_ref.7) | copy-start | bytes 3145732
  5.6 26.5 %copy-start.5 = (bf16[128,4096]{1,0:T(8,128)(2,1)S(1)}, bf16[128,4096]{1,0:T(8,128)(2,1)}, u32[]{:S(2)}) copy-start(bf16[128,4096]{1,0:T(8,128)(2,1)} %v_ref.7) | copy-start | bytes 3145732
  8.0 24.0 %collective-permute-start.3 = (bf16[4,128,2048]{2,1,0:T(8,128)(2,1)}, bf16[4,128,2048]{2,1,0:T(8,128)(2,1)}, u32[]{:S(2)}, u32[]{:S(2)}) collective-permute-start(bf16[4,128,2048]{2,1,0:T(8,128)(2,1)} %shard_map.119), channel_id=1, source_target_pairs={{0,1},{1,0},{2,3},{3,2},{4,5},{5,4},{6,7},{7,6},{8,9},{9,8},{10,11... | collective-permute-start | bytes 6291464 | tf_op jit(solution)/shard_map/ppermute | solution.py:512
  11.9 3.1 %collective-permute-start = (s32[2,128]{1,0:T(2,128)S(1)}, s32[2,128]{1,0:T(2,128)S(1)}, u32[]{:S(2)}, u32[]{:S(2)}) collective-permute-start(s32[2,128]{1,0:T(2,128)S(1)} %concatenate.6), channel_id=1, source_target_pairs={{0,1},{1,0},{2,3},{3,2},{4,5},{5,4},{6,7},{7,6},{8,9},{9,8},{10,11... | collective-permute-start | bytes 3080 | tf_op jit(solution)/shard_map/ppermute | solution.py:498
  15.0 7.8 %collective-permute-start.2 = (s32[2,2,128]{2,1,0:T(2,128)S(1)}, s32[2,2,128]{2,1,0:T(2,128)S(1)}, u32[]{:S(2)}, u32[]{:S(2)}) collective-permute-start(s32[2,2,128]{2,1,0:T(2,128)S(1)} %pad_add_fusion), channel_id=1, source_target_pairs={{2,0},{3,1},{4,2},{5,3},{6,4},{7,5},{8,6},{9,7},{10,8},{11,9},{12,... | collective-permute-start | bytes 6152 | tf_op jit(solution)/shard_map/ppermute | solution.py:503
  16.3 11.0 %collective-permute-start.1 = (s32[2,2,128]{2,1,0:T(2,128)S(1)}, s32[2,2,128]{2,1,0:T(2,128)S(1)}, u32[]{:S(2)}, u32[]{:S(2)}) collective-permute-start(s32[2,2,128]{2,1,0:T(2,128)S(1)} %pad_add_fusion), channel_id=1, source_target_pairs={{0,2},{1,3},{2,4},{3,5},{4,6},{5,7},{6,8},{7,9},{8,10},{9,11},{10,... | collective-permute-start | bytes 6152 | tf_op jit(solution)/shard_map/ppermute | solution.py:502
  32.0 1.2 copy-start.7
  33.3 10.1 %copy-start.10 = (f32[1,16]{1,0:T(1,128)S(1)}, f32[1,16]{1,0:T(1,128)}, u32[]{:S(2)}) copy-start(f32[1,16]{1,0:T(1,128)} %param.13) | copy-start | bytes 196
  33.3 10.1 %copy-start.11 = (f32[1,16]{1,0:T(1,128)S(1)}, f32[1,16]{1,0:T(1,128)}, u32[]{:S(2)}) copy-start(f32[1,16]{1,0:T(1,128)} %param.12) | copy-start | bytes 196
  38.7 88.6 %collective-permute-start.4 = (bf16[4,1152,128]{2,1,0:T(8,128)(2,1)}, bf16[4,1152,128]{2,1,0:T(8,128)(2,1)}, u32[]{:S(2)}, u32[]{:S(2)}) collective-permute-start(bf16[4,1152,128]{2,1,0:T(8,128)(2,1)} %get-tuple-element.20), channel_id=1, source_target_pairs={{0,2},{1,3},{2,4},{3,5},{4,6},{5,7},{6,8},{7,9},{8,10},{9,11},{10,... | collective-permute-start | bytes 3538952 | tf_op jit(solution)/shard_map/ppermute | solution.py:529
  42.0 85.3 %collective-permute-start.5 = (bf16[4,1152,128]{2,1,0:T(8,128)(2,1)}, bf16[4,1152,128]{2,1,0:T(8,128)(2,1)}, u32[]{:S(2)}, u32[]{:S(2)}) collective-permute-start(bf16[4,1152,128]{2,1,0:T(8,128)(2,1)} %get-tuple-element.21), channel_id=1, source_target_pairs={{2,0},{3,1},{4,2},{5,3},{6,4},{7,5},{8,6},{9,7},{10,8},{11,9},{12,... | collective-permute-start | bytes 3538952 | tf_op jit(solution)/shard_map/ppermute | solution.py:530
  44.0 9.8 %all-to-all-start = ((f32[8,2,16]{2,1,0:T(2,128)}), f32[8,2,16]{2,1,0:T(2,128)S(1)}, u32[]{:S(2)}, u32[]{:S(2)}) async-start(f32[8,2,16]{2,1,0:T(2,128)} %broadcast_in_dim.49), calls=%async_computation | async-start | bytes 16384 | tf_op jit(solution)/shard_map/all_to_all | solution.py:515
  54.5 57.8 %all-to-all-start.1 = ((f32[16,2,128]{2,1,0:T(2,128)}), f32[16,2,128]{2,1,0:T(2,128)S(1)}, u32[]{:S(2)}, u32[]{:S(2)}) async-start(f32[16,2,128]{2,1,0:T(2,128)} %broadcast_in_dim.51), calls=%async_computation.1 | async-start | bytes 32768 | tf_op jit(solution)/shard_map/all_to_all | solution.py:519
  112.3 1.2 copy-start.8
  139.5 20.8 %collective-permute-start.6 = (bf16[3,1152,128]{2,1,0:T(8,128)(2,1)S(1)}, bf16[3,1152,128]{2,1,0:T(8,128)(2,1)S(1)}, u32[]{:S(2)}, u32[]{:S(2)}) collective-permute-start(bf16[3,1152,128]{2,1,0:T(8,128)(2,1)S(1)} %get-tuple-element.23), channel_id=1, source_target_pairs={{0,2},{1,3},{2,4},{3,5},{4,6},{5,7},{6,8},{7,9},{8,10},{9,11},{10,... | collective-permute-start | bytes 2654216 | tf_op jit(solution)/shard_map/ppermute | solution.py:537
  150.4 13.8 %collective-permute-start.7 = (bf16[3,1152,128]{2,1,0:T(8,128)(2,1)S(1)}, bf16[3,1152,128]{2,1,0:T(8,128)(2,1)S(1)}, u32[]{:S(2)}, u32[]{:S(2)}) collective-permute-start(bf16[3,1152,128]{2,1,0:T(8,128)(2,1)S(1)} %get-tuple-element.24), channel_id=1, source_target_pairs={{2,0},{3,1},{4,2},{5,3},{6,4},{7,5},{8,6},{9,7},{10,8},{11,9},{12,... | collective-permute-start | bytes 2654216 | tf_op jit(solution)/shard_map/ppermute | solution.py:536
  170.1 69.8 %collective-permute-start.8 = (bf16[3,128,2048]{2,1,0:T(8,128)(2,1)}, bf16[3,128,2048]{2,1,0:T(8,128)(2,1)S(1)}, u32[]{:S(2)}, u32[]{:S(2)}) collective-permute-start(bf16[3,128,2048]{2,1,0:T(8,128)(2,1)} %get-tuple-element.26), channel_id=1, source_target_pairs={{0,1},{1,0},{2,3},{3,2},{4,5},{5,4},{6,7},{7,6},{8,9},{9,8},{10,11... | collective-permute-start | bytes 4718600 | tf_op jit(solution)/shard_map/ppermute | solution.py:544

commit v2 on v0

v2 whole, which is shorter than its diff:
```python
import functools

import jax
import jax.numpy as jnp
from jax import lax
from jax.experimental import pallas as pl
from jax.experimental.pallas import tpu as pltpu
from jax.sharding import PartitionSpec as P

EPS = 1e-06
NEG = -1e30
HD = 128
ROWS = 128
PAIR = 256
HEADS = 16
ALIGN = 16
LINE = 4
CAP = 1152
FIRST = 768
REST = CAP - FIRST
PADDED = CAP + PAIR
SCALE = HD**-0.5
LOG2E = 1.4426950408889634
BF = jnp.bfloat16
F32 = jnp.float32
CORE, CHIP, A_L, B_L, A_R, B_R, N_L, N_R, PA_L, PB_L, PA_R, PB_R = range(12)
GROUP = 2
ANYWHERE = pl.BlockSpec(memory_space=pl.ANY)
IN_VMEM = pl.BlockSpec(memory_space=pltpu.VMEM)
IN_SMEM = pl.BlockSpec(memory_space=pltpu.SMEM)


def aligned(index):
    return pl.multiple_of(index, ALIGN)


def lanes(position):
    return pl.ds(pl.multiple_of(position * HD, HD), HD)


def params(mib):
    return pltpu.CompilerParams(vmem_limit_bytes=mib * 1024 * 1024)


def whole(shape):
    return pl.BlockSpec(shape, lambda j, m: (0,) * len(shape))


def run_copies(copies):
    for copy in copies:
        copy.start()
    for copy in copies:
        copy.wait()


def rows_of(held, start, length):
    return held.at[:, pl.ds(start, length), :]


def pick_kernel(place, q_ref, k_ref, v_ref, d_ref, out_ref):
    other = 1 - place[CORE]
    for t, ref in enumerate((q_ref, k_ref, v_ref, d_ref)):
        for i in range(out_ref.shape[2] // HD):
            out_ref[t, :, i * HD : (i + 1) * HD] = ref[:, lanes(2 * i + other)]


def pick_other(place, tensors, per=4):
    return pl.pallas_call(
        pick_kernel,
        out_shape=jax.ShapeDtypeStruct((4, ROWS, HEADS * HD), BF),
        grid_spec=pltpu.PrefetchScalarGridSpec(
            num_scalar_prefetch=1,
            grid=(HEADS // per,),
            in_specs=own_specs(per)[:4],
            out_specs=own_specs(per)[4],
        ),
        compiler_params=params(12),
    )(place, *tensors)


def chip_halves(info, core):
    ids, counts = (info[1:2], info[2:3]), (info[0:1, 32:33], info[0:1, 33:34])

    def ordered(mine, other):
        return jnp.where(core == 0, mine, other), jnp.where(core == 0, other, mine)

    return ordered(*ids), ordered(*counts)


def count_equal(halves, wanted):
    hits = [jnp.where(half == wanted, 1.0, 0.0).astype(F32) for half in halves]
    return jnp.sum(hits[0] + hits[1]).astype(jnp.int32)


def edge_split(long_a, long_b):
    blocks_a = lax.div(long_a + ALIGN - 1, ALIGN)
    blocks_b = lax.div(long_b + ALIGN - 1, ALIGN)
    least = HEADS - lax.div(CAP // ALIGN, jnp.maximum(blocks_a, 1))
    most = lax.div(CAP // ALIGN, jnp.maximum(blocks_b, 1))
    to_left = jnp.minimum(jnp.maximum(HEADS // 2, least), most)
    return blocks_a * ALIGN, blocks_b * ALIGN, to_left


def write_plan(place, table, infos, meta):
    core, chip = place[CORE], place[CHIP]
    first = place[GROUP] * HEADS
    spots = (chip, jnp.maximum(chip - 1, 0), jnp.minimum(chip + 1, HEADS - 1))
    for n, spot in enumerate(spots):
        infos[n] = table[first + spot]
    own, _ = chip_halves(infos[0], core)
    left, _ = chip_halves(infos[1], core)
    right, _ = chip_halves(infos[2], core)
    left_last, own_first = jnp.max(left[1]), jnp.min(own[0])
    own_last, right_first = jnp.max(own[1]), jnp.min(right[0])
    cross_l = (chip > 0) & (left_last == own_first)
    cross_r = (chip < HEADS - 1) & (right_first == own_last)
    a_l = jnp.where(cross_l, count_equal(left, left_last), 0)
    b_l = jnp.where(cross_l, count_equal(own, own_first), 0)
    a_r = jnp.where(cross_r, count_equal(own, own_last), 0)
    b_r = jnp.where(cross_r, count_equal(right, right_first), 0)
    pa_l, pb_l, n_l = edge_split(a_l, b_l)
    pa_r, pb_r, n_r = edge_split(a_r, b_r)
    n_l = jnp.where(cross_l, n_l, HEADS)
    n_r = jnp.where(cross_r, n_r, 0)
    values = [core, chip, a_l, b_l, a_r, b_r, n_l, n_r, pa_l, pb_l, pa_r, pb_r]
    for n, value in enumerate(values):
        meta[n] = value


def turns_left(meta):
    return lax.rem(meta[CHIP], LINE) == 0


def turns_right(meta):
    return lax.rem(meta[CHIP], LINE) == LINE - 1


def either(wanted, yes, no):
    @pl.when(wanted)
    def _():
        for copy in yes:
            copy.start()

    @pl.when(jnp.logical_not(wanted))
    def _():
        for copy in no:
            copy.start()


def send_pieces(meta, left, right, left_all, right_all, turn_first, turn_rest, sems):
    def turn_copies(held):
        return [
            pltpu.make_async_copy(held.at[:, pl.ds(0, FIRST), :], turn_first, sems.at[0]),
            pltpu.make_async_copy(held.at[:, pl.ds(FIRST, REST), :], turn_rest, sems.at[1]),
        ]

    by_left, by_right = turn_copies(left), turn_copies(right)
    either(turns_left(meta), by_left, by_right)
    run_copies(
        [
            pltpu.make_async_copy(left, left_all, sems.at[2]),
            pltpu.make_async_copy(right, right_all, sems.at[3]),
        ]
    )
    for copy in by_left:
        copy.wait()


def load_pieces(all_rows, turn_first, turn_rest, held, by_turn, sems):
    spots = [held.at[:, pl.ds(0, FIRST), :], held.at[:, pl.ds(FIRST, REST), :]]
    pieces = [all_rows.at[:, pl.ds(0, FIRST), :], all_rows.at[:, pl.ds(FIRST, REST), :]]

    def copies(sources):
        return [pltpu.make_async_copy(*pair) for pair in zip(sources, spots, sems, strict=True)]

    straight = copies(pieces)
    either(by_turn, copies((turn_first, turn_rest)), straight)
    return straight


def load_both(meta, pieces, held_left, held_right, sems):
    from_left, from_right, turn_first, turn_rest = pieces
    return load_pieces(
        from_left, turn_first, turn_rest, held_left, turns_left(meta), (sems.at[0], sems.at[1])
    ) + load_pieces(
        from_right, turn_first, turn_rest, held_right, turns_right(meta), (sems.at[2], sems.at[3])
    )


def half_rows(half):
    return pl.ds(pl.multiple_of(half * ROWS, ROWS), ROWS)


def fill_windows(win, core, own_refs, rec_ref):
    for i in range(win.shape[0]):
        for t, ref in enumerate(own_refs):
            win[i, t, half_rows(core), :] = ref[:, lanes(2 * i + core)]
            win[i, t, half_rows(1 - core), :] = rec_ref[t, :, i * HD : (i + 1) * HD]


def pack_kernel(
    place,
    q_ref,
    k_ref,
    v_ref,
    d_ref,
    rec_ref,
    table,
    meta,
    infos,
    left_all,
    right_all,
    turn_first,
    turn_rest,
    win,
    left_ref,
    right_ref,
    sems,
):
    per = rec_ref.shape[2] // HD
    core = place[CORE]
    step = pl.program_id(0)

    @pl.when(step == 0)
    def _():
        write_plan(place, table, infos, meta)

    fill_windows(win, core, (q_ref, k_ref, v_ref, d_ref), rec_ref)
    for i in range(per):
        head = step * per + i

        @pl.when(head < meta[N_L])
        def _():
            for t in range(4):
                left_ref[t, pl.ds(aligned(head * meta[PB_L]), PAIR), :] = win[i, t]

        @pl.when(head >= meta[N_R])
        def _():
            for t in range(4):
                right_ref[t, pl.ds(aligned((HEADS - head) * meta[PA_R]), PAIR), :] = win[i, t]

    @pl.when(step == pl.num_programs(0) - 1)
    def _():
        send_pieces(
            meta,
            rows_of(left_ref, 0, CAP),
            rows_of(right_ref, PAIR, CAP),
            left_all,
            right_all,
            turn_first,
            turn_rest,
            sems,
        )


def own_specs(per):
    return [pl.BlockSpec((ROWS, 2 * per * HD), lambda j, m: (0, j))] * 4 + [
        pl.BlockSpec((4, ROWS, per * HD), lambda j, m: (0, 0, j))
    ]


def pieces_shape(tensors):
    return [jax.ShapeDtypeStruct((tensors, n, HD), BF) for n in (CAP, CAP, FIRST, REST)]


def pack_halos(place, tensors, rec, table, per=4):
    return pl.pallas_call(
        pack_kernel,
        out_shape=(
            jax.ShapeDtypeStruct((16,), jnp.int32),
            jax.ShapeDtypeStruct((3, 3, HD), F32),
            *pieces_shape(4),
        ),
        grid_spec=pltpu.PrefetchScalarGridSpec(
            num_scalar_prefetch=1,
            grid=(HEADS // per,),
            in_specs=own_specs(per) + [whole(table.shape)],
            out_specs=(IN_SMEM, whole((3, 3, HD)), *([ANYWHERE] * 4)),
            scratch_shapes=[
                pltpu.VMEM((per, 4, PAIR, HD), BF),
                pltpu.VMEM((4, PADDED, HD), BF),
                pltpu.VMEM((4, PADDED, HD), BF),
                pltpu.SemaphoreType.DMA((4,)),
            ],
        ),
        compiler_params=params(16),
    )(place, *tensors, rec, table)


def matmul(a, b, contract_a, contract_b):
    return lax.dot_general(
        a, b, (((contract_a,), (contract_b,)), ((), ())), preferred_element_type=F32
    )


def norm_parts(rows, gain):
    widened = rows.astype(F32)
    scaled = lax.rsqrt(jnp.mean(widened * widened, axis=-1, keepdims=True) + EPS)
    unit_rows = widened * scaled
    return scaled, unit_rows, (unit_rows * gain).astype(BF)


def norm_back(scaled, unit_rows, gain, upper):
    terms = upper * unit_rows
    gain = gain * SCALE
    mean = jnp.mean(terms * gain, axis=-1, keepdims=True)
    grad = scaled * (gain * upper - unit_rows * mean)
    return grad.astype(BF), jnp.sum(terms, axis=0, keepdims=True) * SCALE


def solve(problems):
    each = range(len(problems))
    q_rows, k_rows, v_rows, d_rows, gain_q, gain_k, bias, q_live = zip(*problems, strict=True)
    q_parts = [norm_parts(q_rows[n], gain_q[n]) for n in each]
    k_parts = [norm_parts(k_rows[n], gain_k[n]) for n in each]
    raw = [matmul(k_parts[n][2], q_parts[n][2], 1, 1) for n in each]
    d_weights = [matmul(v_rows[n], d_rows[n], 1, 1) for n in each]
    weights = []
    for n in each:
        scores = raw[n] * (SCALE * LOG2E) + bias[n]
        exponent = jnp.exp2(scores - jnp.max(scores, axis=0, keepdims=True))
        total = jnp.sum(exponent, axis=0, keepdims=True)
        weights.append((exponent * (q_live[n] / total)).astype(BF))
    dv_rows = [matmul(weights[n], d_rows[n], 1, 0) for n in each]
    d_scores = []
    for n in each:
        wide = weights[n].astype(F32)
        row_delta = jnp.sum(wide * d_weights[n], axis=0, keepdims=True)
        d_scores.append((wide * (d_weights[n] - row_delta)).astype(BF))
    dk = [matmul(d_scores[n], q_parts[n][2], 1, 0) for n in each]
    dq = [matmul(d_scores[n], k_parts[n][2], 0, 0) for n in each]
    results = []
    for n in each:
        grad_k, gain_k_part = norm_back(k_parts[n][0], k_parts[n][1], gain_k[n], dk[n])
        grad_q, gain_q_part = norm_back(q_parts[n][0], q_parts[n][1], gain_q[n], dq[n])
        grads = (grad_q, grad_k, dv_rows[n].astype(BF))
        results.append((grads, gain_q_part, gain_k_part))
    return results


def link_codes(side, core, meta, infos):
    own_ids, own_counts = chip_halves(infos[0], core)
    _, far_counts = chip_halves(infos[side], core)
    codes = []
    for half in range(2):
        lane = lax.broadcasted_iota(jnp.int32, (1, ROWS), 1)
        slot = lane + half * ROWS
        live = lane.astype(F32) < own_counts[half]
        far = lane.astype(F32) < far_counts[half]
        if side == 0:
            inside = live & (slot >= meta[B_L]) & (slot < PAIR - meta[A_R])
            code = jnp.where(inside, own_ids[half], -1.0)
        elif side == 1:
            inside = (live & (slot < meta[B_L])) | (far & (slot >= PAIR - meta[A_L]))
            code = jnp.where(inside, 0.0, -1.0)
        else:
            inside = (live & (slot >= PAIR - meta[A_R])) | (far & (slot < meta[B_R]))
            code = jnp.where(inside, 0.0, -1.0)
        codes.append(code.astype(F32))
    return codes


def fill_links(bias, q_live, codes):
    for a in range(2):
        q_live[0:1, a * ROWS : (a + 1) * ROWS] = (codes[a] >= 0.0).astype(F32)
        key_codes = jnp.broadcast_to(codes[a], (ROWS, ROWS)).T
        for b in range(2):
            linked = (key_codes == codes[b]) & (codes[b] >= 0.0)
            bias[a * ROWS : (a + 1) * ROWS, b * ROWS : (b + 1) * ROWS] = jnp.where(
                linked, 0.0, NEG
            ).astype(F32)


def gather_gains(table, gains):
    groups = table.shape[0] // HEADS
    width = HD // groups
    for n in range(groups):
        part = table[n * HEADS : (n + 1) * HEADS, 0:1, :]
        cols = slice(n * width, (n + 1) * width)
        gains[:, 0:1, cols] = part[:, :, 0:width]
        gains[:, 1:2, cols] = part[:, :, width : 2 * width]


def mid_kernel(
    meta,
    q_ref,
    k_ref,
    v_ref,
    d_ref,
    rec_ref,
    infos,
    table,
    out_ref,
    gg_ref,
    gains_ref,
    win,
    bias,
    q_live,
):
    per = rec_ref.shape[2] // HD
    core = meta[CORE]

    @pl.when(pl.program_id(0) == 0)
    def _():
        gather_gains(table, gains_ref)
        fill_links(bias, q_live, link_codes(0, core, meta, infos))

    fill_windows(win, core, (q_ref, k_ref, v_ref, d_ref), rec_ref)
    heads = [pl.program_id(0) * per + i for i in range(per)]
    gains = [gains_ref[head] for head in heads]
    results = solve(
        [
            (*(win[i, t] for t in range(4)), gains[i][0:1], gains[i][1:2], bias[...], q_live[0:1, :])
            for i in range(per)
        ]
    )
    for i, (grads, part_q, part_k) in enumerate(results):
        for t in range(3):
            for half in range(2):
                out_ref[lax.rem(half + core, 2), t, :, i * HD : (i + 1) * HD] = grads[t][
                    half * ROWS : (half + 1) * ROWS
                ]
        gg_ref[heads[i]] = jnp.concatenate([part_q, part_k], axis=0)


def solve_mid(meta, tensors, rec, infos, table, per=4):
    per_head = jax.ShapeDtypeStruct((HEADS, 2, HD), F32)
    return pl.pallas_call(
        mid_kernel,
        out_shape=(jax.ShapeDtypeStruct((2, 3, ROWS, HEADS * HD), BF), per_head, per_head),
        grid_spec=pltpu.PrefetchScalarGridSpec(
            num_scalar_prefetch=1,
            grid=(HEADS // per,),
            in_specs=own_specs(per) + [whole(infos.shape), whole(table.shape)],
            out_specs=(half_spec(per), whole(per_head.shape), whole(per_head.shape)),
            scratch_shapes=[
                pltpu.VMEM((per, 4, PAIR, HD), BF),
                pltpu.VMEM((PAIR, PAIR), F32),
                pltpu.VMEM((8, PAIR), F32),
            ],
        ),
        compiler_params=params(32),
    )(meta, *tensors, rec, infos, table)


def half_spec(per):
    return pl.BlockSpec((2, 3, ROWS, per * HD), lambda j, m: (0, 0, 0, j))


def row_numbers(rows):
    return lax.broadcasted_iota(jnp.int32, (rows, HD), 0).astype(F32).astype(BF)


def bound(value):
    return jnp.full((1, HD), value, jnp.int32).astype(F32).astype(BF)


def edge_kernel(
    meta,
    q_ref,
    k_ref,
    v_ref,
    d_ref,
    rec_ref,
    infos,
    gains_ref,
    mid_ref,
    gg_mid_ref,
    from_left,
    from_right,
    from_turn_first,
    from_turn_rest,
    out_ref,
    gg_ref,
    left_all,
    right_all,
    turn_first,
    turn_rest,
    win,
    bias,
    q_live,
    held,
    back,
    sems,
):
    per = rec_ref.shape[2] // HD
    core = meta[CORE]
    step = pl.program_id(0)

    @pl.when(step == 0)
    def _():
        copies = load_both(
            meta,
            (from_left, from_right, from_turn_first, from_turn_rest),
            rows_of(held.at[0], PAIR, CAP),
            rows_of(held.at[1], 0, CAP),
            sems,
        )
        for side in range(2):
            fill_links(
                bias.at[side], q_live.at[side], link_codes(side + 1, core, meta, infos)
            )
        gg_ref[...] = gg_mid_ref[...]
        for copy in copies:
            copy.wait()

    fill_windows(win, core, (q_ref, k_ref, v_ref, d_ref), rec_ref)
    out_ref[...] = mid_ref[...]
    heads = [step * per + i for i in range(per)]
    on_left = [head >= meta[N_L] for head in heads]
    on_right = [head < meta[N_R] for head in heads]
    row = row_numbers(PAIR)

    def solve_side(lefts, rights):
        problems, spots = [], []
        for i, head in enumerate(heads):
            side = jnp.where(lefts[i], 0, 1)
            use = jnp.logical_or(lefts[i], rights[i])
            at = jnp.where(lefts[i], (HEADS - head) * meta[PA_L], head * meta[PB_R])
            span = pl.ds(aligned(jnp.where(use, at, PADDED)), PAIR)
            source = pl.ds(aligned(jnp.where(use, at, 0)), PAIR)
            halo = (row >= bound(jnp.where(lefts[i], PAIR - meta[A_L], 0))) & (
                row < bound(jnp.where(lefts[i], PAIR, jnp.where(use, meta[B_R], 0)))
            )
            local = (row >= bound(jnp.where(lefts[i], 0, PAIR - meta[A_R]))) & (
                row < bound(jnp.where(lefts[i], meta[B_L], jnp.where(use, PAIR, 0)))
            )
            window = [jnp.where(halo, held[side, t, source, :], win[i, t]) for t in range(4)]
            gains = gains_ref[head]
            problems.append((*window, gains[0:1], gains[1:2], bias[side], q_live[side, 0:1, :]))
            spots.append((side, span, local, use.astype(F32)))
        for i, (grads, part_q, part_k) in enumerate(solve(problems)):
            side, span, local, counts = spots[i]
            cols = slice(i * HD, (i + 1) * HD)
            for t in range(3):
                back[side, t, span, :] = grads[t]
                for half in range(2):
                    rows = slice(half * ROWS, (half + 1) * ROWS)
                    place = lax.rem(half + core, 2)
                    out_ref[place, t, :, cols] = jnp.where(
                        local[rows], grads[t][rows], out_ref[place, t, :, cols]
                    )
            gg_ref[heads[i]] += jnp.concatenate([part_q, part_k], axis=0) * counts

    def some(flags):
        return functools.reduce(jnp.logical_or, flags)

    @pl.when(some(on_left + on_right))
    def _():
        solve_side(on_left, on_right)

    both = [jnp.logical_and(*pair) for pair in zip(on_left, on_right, strict=True)]

    @pl.when(some(both))
    def _():
        solve_side([jnp.logical_and(flag, jnp.logical_not(flag)) for flag in both], both)

    @pl.when(step == pl.num_programs(0) - 1)
    def _():
        send_pieces(
            meta,
            rows_of(back.at[0], PAIR, CAP),
            rows_of(back.at[1], 0, CAP),
            left_all,
            right_all,
            turn_first,
            turn_rest,
            sems,
        )


def solve_edges(meta, tensors, rec, infos, gains, mid, gg_mid, halos, per=4):
    return pl.pallas_call(
        edge_kernel,
        out_shape=(
            jax.ShapeDtypeStruct(mid.shape, BF),
            jax.ShapeDtypeStruct(gg_mid.shape, F32),
            *pieces_shape(3),
        ),
        grid_spec=pltpu.PrefetchScalarGridSpec(
            num_scalar_prefetch=1,
            grid=(HEADS // per,),
            in_specs=own_specs(per)
            + [whole(infos.shape), whole(gains.shape), half_spec(per), whole(gg_mid.shape)]
            + [ANYWHERE] * 4,
            out_specs=(half_spec(per), whole(gg_mid.shape), *([ANYWHERE] * 4)),
            scratch_shapes=[
                pltpu.VMEM((per, 4, PAIR, HD), BF),
                pltpu.VMEM((2, PAIR, PAIR), F32),
                pltpu.VMEM((2, 8, PAIR), F32),
                pltpu.VMEM((2, 4, PADDED, HD), BF),
                pltpu.VMEM((2, 3, PADDED + PAIR, HD), BF),
                pltpu.SemaphoreType.DMA((4,)),
            ],
        ),
        compiler_params=params(40),
    )(meta, *tensors, rec, infos, gains, mid, gg_mid, *halos)


def load_returned(meta, pieces, held_left, held_right, sems):
    for copy in load_both(
        meta, pieces, rows_of(held_left, 0, CAP), rows_of(held_right, PAIR, CAP), sems
    ):
        copy.wait()


def merged(meta, head, half, rows, held_left, held_right):
    use_left = head < meta[N_L]
    use_right = head >= meta[N_R]
    base = half * ROWS
    left_at = jnp.where(use_left, head * meta[PB_L], 0) + base
    right_at = jnp.where(use_right, (HEADS - head) * meta[PA_R], 0) + base
    row = row_numbers(ROWS)
    at_head = row < bound(jnp.where(use_left, meta[B_L], 0) - base)
    at_tail = row >= bound(jnp.where(use_right, PAIR - meta[A_R], PAIR) - base)
    done = []
    for t, part in enumerate(rows):
        part = jnp.where(at_head, held_left[t, pl.ds(aligned(left_at), ROWS), :], part)
        part = jnp.where(at_tail, held_right[t, pl.ds(aligned(right_at), ROWS), :], part)
        done.append(part)
    return done


def merge_kernel(meta, in_ref, *refs):
    pieces, (_, send_ref, held_left, held_right, sems) = refs[:4], refs[4:]
    per = in_ref.shape[3] // HD
    step = pl.program_id(0)

    @pl.when(step == 0)
    def _():
        load_returned(meta, pieces, held_left, held_right, sems)

    for i in range(per):
        cols = slice(i * HD, (i + 1) * HD)
        rows = [in_ref[0, t, :, cols] for t in range(3)]
        rows = merged(meta, step * per + i, 1 - meta[CORE], rows, held_left, held_right)
        for t in range(3):
            send_ref[t, :, cols] = rows[t]


def held_scratch():
    return [
        pltpu.VMEM((3, PADDED, HD), BF),
        pltpu.VMEM((3, PADDED, HD), BF),
        pltpu.SemaphoreType.DMA((4,)),
    ]


def merge_other(meta, own, returned, after, per=4):
    return pl.pallas_call(
        merge_kernel,
        out_shape=jax.ShapeDtypeStruct((3, ROWS, HEADS * HD), BF),
        grid_spec=pltpu.PrefetchScalarGridSpec(
            num_scalar_prefetch=1,
            grid=(HEADS // per,),
            in_specs=[pl.BlockSpec((1, 3, ROWS, per * HD), lambda j, m: (1, 0, 0, j))]
            + [ANYWHERE] * 5,
            out_specs=pl.BlockSpec((3, ROWS, per * HD), lambda j, m: (0, 0, j)),
            scratch_shapes=held_scratch(),
        ),
        compiler_params=params(16),
    )(meta, own, *returned, after)


def weave_kernel(meta, in_ref, rec_ref, *refs):
    pieces, (gg_parts, *outs, gg_q, gg_k, held_left, held_right, sems) = refs[:4], refs[4:]
    per = in_ref.shape[3] // HD
    core = meta[CORE]
    step = pl.program_id(0)

    @pl.when(step == 0)
    def _():
        load_returned(meta, pieces, held_left, held_right, sems)
        total = jnp.sum(gg_parts[...], axis=0)
        gg_q[...] = total[0:1]
        gg_k[...] = total[1:2]

    for i in range(per):
        cols = slice(i * HD, (i + 1) * HD)
        rows = [in_ref[0, t, :, cols] for t in range(3)]
        rows = merged(meta, step * per + i, core, rows, held_left, held_right)
        for t in range(3):
            outs[t][:, lanes(2 * i + core)] = rows[t]
            outs[t][:, lanes(2 * i + 1 - core)] = rec_ref[t, :, cols]


def weave(meta, own, rec, returned, gg_parts, per=4):
    return pl.pallas_call(
        weave_kernel,
        out_shape=(jax.ShapeDtypeStruct((ROWS, 2 * HEADS * HD), BF),) * 3
        + (jax.ShapeDtypeStruct((1, HD), F32),) * 2,
        grid_spec=pltpu.PrefetchScalarGridSpec(
            num_scalar_prefetch=1,
            grid=(HEADS // per,),
            in_specs=[
                pl.BlockSpec((1, 3, ROWS, per * HD), lambda j, m: (0, 0, 0, j)),
                pl.BlockSpec((3, ROWS, per * HD), lambda j, m: (0, 0, j)),
            ]
            + [ANYWHERE] * 4
            + [whole(gg_parts.shape)],
            out_specs=(pl.BlockSpec((ROWS, 2 * per * HD), lambda j, m: (0, j)),) * 3
            + (whole((1, HD)),) * 2,
            scratch_shapes=held_scratch(),
        ),
        compiler_params=params(16),
    )(meta, own, rec, *returned, gg_parts)


def exchange(pieces, size):
    left_all, right_all, turn_first, turn_rest = pieces
    line = 2 * LINE
    wrap = line - 2
    turns = [(i, i + 2) for i in range(size - 2) if i % line >= wrap]
    straight = [(i, i + 2) for i in range(size - 2) if i % line < wrap]

    def back(pairs):
        return [(j, i) for i, j in pairs]

    def move(array, pairs):
        return lax.ppermute(array, "seq", pairs)

    hop = move(turn_rest, [(i, i - wrap) for i, _ in turns] + [(j, j + wrap) for _, j in turns])
    from_left = move(right_all, straight)
    from_right = move(left_all, back(straight))
    from_turn = move(turn_first, turns + back(turns))
    from_hop = move(hop, [(i - wrap, j) for i, j in turns] + [(j + wrap, i) for i, j in turns])
    return from_left, from_right, from_turn, from_hop


def shards(queries, keys, values, out_grad, gain_q, gain_k, clip_ids, counts):
    size = lax.axis_size("seq")
    groups = lax.axis_size("dp")
    chips = size // 2
    seq = lax.axis_index("seq")
    swap = [(i, i ^ 1) for i in range(size)]
    place = jnp.stack([seq % 2, seq // 2, lax.axis_index("dp")]).astype(jnp.int32)
    tensors = tuple(
        pltpu.with_memory_space_constraint(t, pltpu.HBM)
        for t in (queries, keys, values, out_grad)
    )

    def all_to_all(array):
        same_core = [
            [d * size + 2 * c + core for d in range(groups) for c in range(chips)]
            for core in range(2)
        ]
        return lax.all_to_all(
            array, ("dp", "seq"), 0, 0, axis_index_groups=same_core, tiled=True
        )

    info = jnp.concatenate([clip_ids, jnp.broadcast_to(counts, (1, ROWS))], axis=0).astype(F32)
    info_other = lax.ppermute(info, "seq", swap)
    rec = lax.ppermute(pick_other(place, tensors), "seq", swap)
    cells = [gain_q, gain_k, info[1:2, 0:1], info_other[1:2, 0:1]]
    filled = sum(cell.shape[1] for cell in cells)
    first = jnp.concatenate(cells + [jnp.zeros((1, HD - filled), F32)], axis=1)
    known = jnp.concatenate([first, info[0:1], info_other[0:1]], axis=0)
    table = all_to_all(jnp.broadcast_to(known[None], (groups * chips,) + known.shape))

    meta, infos, *pieces = pack_halos(place, tensors, rec, table)
    halos = exchange(pieces, size)
    mid, gg_mid, gains = solve_mid(meta, tensors, rec, infos, table)
    own, gg, *pieces = solve_edges(meta, tensors, rec, infos, gains, mid, gg_mid, halos)
    returned = exchange(pieces, size)
    gg_parts = all_to_all(
        jnp.broadcast_to(gg[None], (groups,) + gg.shape).reshape(groups * chips, 2, HD)
    )
    send = merge_other(meta, own, returned, gg_parts)
    other = lax.ppermute(send, "seq", swap)
    return tuple(weave(meta, own, other, returned, gg_parts))


def solution(mesh):
    rows = P(("dp", "seq"), None)
    cells = P("seq", "dp")
    slots = P("dp", "seq")
    return jax.shard_map(
        shards,
        mesh=mesh,
        in_specs=(rows, rows, rows, rows, cells, cells, slots, slots),
        out_specs=(rows, rows, rows, P("seq", None), P("seq", None)),
        check_vma=False,
    )
```

time: 533 us -> 172 us (0.32); the launches traced: 523 us -> 171 us
  matrix products: 91.6 us -> 0 us
  other arithmetic: 78.9 us -> 0.09 us
  blocking collectives: 124 us -> 55.4 us
  local copies, waits for them, and re-layouts: 68.7 us -> 4.14 us
  waiting for transfers between devices: 88.7 us -> 40 us
  Pallas kernels: 0 us -> 33.7 us
  starting transfers between devices: 63.1 us -> 36.1 us
  loops' own time: 5.55 us -> 0 us
    dot_general x48 -> x0, matrix products: 91.6 us -> none  [the longest x8 19.2 us: attend(): jnp.einsum('brc,brd->bcd', d_scores, q_norm, preferred_element_type=jnp.f...]
    all_to_all x7 -> x0, waiting for transfers between devices: 88.7 us -> none  [the longest x1 26.4 us: shards(): lax.all_to_all(to_heads(queries), 'seq', split_axis=1, concat_axis=0, til...]
    all_gather x2 -> x0, blocking collectives: 73.9 us -> none  [the longest x1 60 us: shards(): lax.all_gather(clip_ids, 'seq', axis=1, tiled=True)]
    all_to_all x7 -> x0, starting transfers between devices: 63.1 us -> none  [the longest x1 12.6 us: shards(): lax.all_to_all(to_heads(queries), 'seq', split_axis=1, concat_axis=0, til...]
    convert_element_type x15 -> x1, other arithmetic: 56.4 us -> 0.01 us  [shards(): jnp.concatenate([clip_ids, jnp.broadcast_to(counts, (1, ROWS))], axis=0)]
    all_to_all x0 -> x2, blocking collectives: none -> 55.4 us  [all_to_all(): lax.all_to_all(array, ('dp', 'seq'), 0, 0, axis_index_groups=same_core, t...]
    ppermute x0 -> x13, waiting for transfers between devices: none -> 40 us  [the longest x10 34.5 us: move(): return lax.ppermute(array, 'seq', pairs)]
    ppermute x0 -> x13, starting transfers between devices: none -> 36.1 us  [the longest x10 24.9 us: move(): return lax.ppermute(array, 'seq', pairs)]
  transfers between devices with their start and end apart: 7 -> 13, of which waited for: 4 -> 4; matrix products, arithmetic and copies ran while one was open for 8% -> 1% of each run, Pallas kernels for 0% -> 5%
where the time goes in v2:
time: 172 us; the launch traced here: 171 us
  blocking collectives  55.4 us (32%)
  waiting for transfers between devices  40 us (23%)
  starting transfers between devices  36.1 us (21%)
  Pallas kernels  33.7 us (20%)
  local copies, waits for them, and re-layouts  4.14 us (2%)
    all_to_all x2, blocking collectives, all_to_all(): lax.all_to_all(array, ('dp', 'seq'), 0, 0, axis_index_groups=same_core, t...  55.4 us
    ppermute x10, waiting for transfers between devices, move(): return lax.ppermute(array, 'seq', pairs)  34.5 us
    ppermute x10, starting transfers between devices, move(): return lax.ppermute(array, 'seq', pairs)  24.9 us
    pallas_call x1, Pallas kernels, solve_mid(): pl.pallas_call(mid_kernel, out_shape=(jax.ShapeDtypeStruct((2, 3, ROWS, H...  9.37 us
    pallas_call x1, Pallas kernels, solve_edges(): pl.pallas_call(edge_kernel, out_shape=(jax.ShapeDtypeStruct(mid.shape, BF...  8.73 us
    ppermute x1, starting transfers between devices, shards(): other = lax.ppermute(send, 'seq', swap)  7.82 us
    pallas_call x1, Pallas kernels, pack_halos(): pl.pallas_call(pack_kernel, out_shape=(jax.ShapeDtypeStruct((16,), jnp.in...  5.52 us
    pallas_call x1, Pallas kernels, pick_other(): pl.pallas_call(pick_kernel, out_shape=jax.ShapeDtypeStruct((4, ROWS, HEAD...  5.01 us
  transfers between devices with their start and end apart: 13, of which 4 were waited for; matrix products, arithmetic and copies ran while one was open for 1% of the time, Pallas kernels for 5%

profile of v2, /device:TPU:1, one launch (start us, length us, event | category | flops | bytes accessed | tf_op | source)
XLA Modules:
  0.0 171.1 jit_solution(7412639639869544286)
XLA Ops:
  0.6 0.1 pad_add_fusion.place
  0.7 5.0 %shard_map.119 = bf16[4,128,2048]{2,1,0:T(8,128)(2,1)} custom-call(s32[3]{0:T(128)S(1)} %pad_add_fusion.place, bf16[128,4096]{1,0:T(8,128)(2,1)} %q_ref.7, bf16[128,4096]{1,0:T(8,128)(2,1)} %k_ref.7, bf16[128,4096]{1,0:T(8,128)(2,1)} %v_ref.7, bf16[128,4096]{1,0:T(8,128)(2,1)} %d_ref.7), custom_call_target="tpu_custom_call" | custom-call | tf_op jit(solution)/shard_map/pallas_call | solution.py:68
  5.7 3.2 %collective-permute-start = (bf16[4,128,2048]{2,1,0:T(8,128)(2,1)}, bf16[4,128,2048]{2,1,0:T(8,128)(2,1)S(1)}, u32[]{:S(2)}, u32[]{:S(2)}) collective-permute-start(bf16[4,128,2048]{2,1,0:T(8,128)(2,1)} %shard_map.119), channel_id=1, source_target_pairs={{0,1},{1,0},{2,3},{3,2},{4,5},{5,4},{6,7},{7,6},{8,9},{9,8},{10,11... | collective-permute-start | bytes 6291464 | tf_op jit(solution)/shard_map/ppermute | solution.py:753
  9.7 0.1 collective-permute-start.1
  9.8 0.5 slice.12
  10.3 2.5 %collective-permute-done.1 = f32[2,128]{1,0:T(2,128)S(1)} collective-permute-done((f32[2,128]{1,0:T(2,128)S(1)}, f32[2,128]{1,0:T(2,128)S(1)}, u32[]{:S(2)}, u32[]{:S(2)}) %collective-permute-start.1) | collective-permute-done | bytes 1056 | tf_op jit(solution)/shard_map/ppermute | solution.py:752
  12.8 0.5 slice.13
  13.3 1.4 concatenate.10
  14.7 24.8 %all_to_all.10.table = f32[128,3,128]{2,1,0:T(4,128)S(1)} all-to-all(f32[128,3,128]{2,1,0:T(4,128)S(1)} %broadcast_in_dim.10), channel_id=1, replica_groups={{0,2,4,6,8,10,12,14,16,18,20,22,24,26,28,30,32,34,36,38,40,42,44,46,48,..., dimensions={0} | all-to-all | bytes 393216 | tf_op jit(solution)/shard_map/all_to_all | solution.py:747
  39.6 0.0 collective-permute-done.rec_ref
  39.6 5.5 %shard_map.120 = (s32[16]{0:T(128)S(1)}, f32[3,3,128]{2,1,0:T(4,128)S(1)}, bf16[4,1152,128]{2,1,0:T(8,128)(2,1)S(1)}, bf16[4,1152,128]{2,1,0:T(8,128)(2,1)S(1)},...) custom-call(s32[3]{0:T(128)S(1)} %pad_add_fusion.place, bf16[128,4096]{1,0:T(8,128)(2,1)} %q_ref.7, ...), custom_call_target="tpu_custom_call" | custom-call | tf_op jit(solution)/shard_map/pallas_call | solution.py:267
  45.1 2.1 %collective-permute-start.2 = (bf16[4,1152,128]{2,1,0:T(8,128)(2,1)S(1)}, bf16[4,1152,128]{2,1,0:T(8,128)(2,1)S(1)}, u32[]{:S(2)}, u32[]{:S(2)}) collective-permute-start(bf16[4,1152,128]{2,1,0:T(8,128)(2,1)S(1)} %get-tuple-element.25), channel_id=1, source_target_pairs={{0,2},{1,3},{2,4},{3,5},{4,6},{5,7},{8,10},{9,11},{10,12},{11,13},... | collective-permute-start | bytes 3538952 | tf_op jit(solution)/shard_map/ppermute | solution.py:720
  47.2 1.3 collective-permute-start.3
  48.5 1.3 collective-permute-start.5
  49.8 0.7 collective-permute-start.4
  50.5 8.9 %collective-permute-done.5 = bf16[4,384,128]{2,1,0:T(8,128)(2,1)S(1)} collective-permute-done((bf16[4,384,128]{2,1,0:T(8,128)(2,1)S(1)}, bf16[4,384,128]{2,1,0:T(8,128)(2,1)S(1)}, u32[]{:S(2)}, u32[]{:S(2)}) %collective-permute-start.5) | collective-permute-done | bytes 393248 | tf_op jit(solution)/shard_map/ppermute | solution.py:720
  59.4 5.8 %collective-permute-start.6 = (bf16[4,384,128]{2,1,0:T(8,128)(2,1)S(1)}, bf16[4,384,128]{2,1,0:T(8,128)(2,1)S(1)}, u32[]{:S(2)}, u32[]{:S(2)}) collective-permute-start(bf16[4,384,128]{2,1,0:T(8,128)(2,1)S(1)} %collective-permute-done.5), channel_id=1, source_target_pairs={{0,8},{1,9},{8,16},{9,17},{16,24},{17,25},{14,6},{15,7},{22,14},{2... | collective-permute-start | bytes 1179656 | tf_op jit(solution)/shard_map/ppermute | solution.py:720
  65.2 9.4 %shard_map.121 = (bf16[2,3,128,2048]{3,2,1,0:T(8,128)(2,1)S(1)}, f32[16,2,128]{2,1,0:T(2,128)S(1)}, f32[16,2,128]{2,1,0:T(2,128)S(1)}) custom-call(s32[16]{0:T(128)S(1)} %get-tuple-element.20.meta, bf16[128,4096]{1,0:T(8,128)(2,1)} %q_ref.7, bf16[128,4096]{1,0:T(8,128)(2,1)} %k_ref.7, bf16[128,4096]{1,0:T(8,128)(2,1)} %v_ref.7, bf16[128,4096]{1,0:T(8,128)(2,1)} %d_ref.7, ...), custom_call_target="tpu_custom_call" | custom-call | tf_op jit(solution)/shard_map/pallas_call | solution.py:428
  74.6 1.6 copy-done
  76.2 0.0 collective-permute-done.6.from_turn_rest
  76.2 8.7 %shard_map.122 = (bf16[2,3,128,2048]{3,2,1,0:T(8,128)(2,1)S(1)}, f32[16,2,128]{2,1,0:T(2,128)S(1)}, bf16[3,1152,128]{2,1,0:T(8,128)(2,1)S(1)}, bf16[3,1152,128]{...) custom-call(s32[16]{0:T(128)S(1)} %get-tuple-element.20.meta, ...), custom_call_target="tpu_custom_call" | custom-call | tf_op jit(solution)/shard_map/pallas_call | solution.py:573
  85.0 2.7 %collective-permute-start.7 = (bf16[3,1152,128]{2,1,0:T(8,128)(2,1)S(1)}, bf16[3,1152,128]{2,1,0:T(8,128)(2,1)S(1)}, u32[]{:S(2)}, u32[]{:S(2)}) collective-permute-start(bf16[3,1152,128]{2,1,0:T(8,128)(2,1)S(1)} %get-tuple-element.30), channel_id=1, source_target_pairs={{0,2},{1,3},{2,4},{3,5},{4,6},{5,7},{8,10},{9,11},{10,12},{11,13},... | collective-permute-start | bytes 2654216 | tf_op jit(solution)/shard_map/ppermute | solution.py:720
  87.7 1.3 collective-permute-start.8
  89.0 1.5 collective-permute-start.10
  90.4 0.7 collective-permute-start.9
  91.1 25.5 %collective-permute-done.10 = bf16[3,384,128]{2,1,0:T(8,128)(2,1)S(1)} collective-permute-done((bf16[3,384,128]{2,1,0:T(8,128)(2,1)S(1)}, bf16[3,384,128]{2,1,0:T(8,128)(2,1)S(1)}, u32[]{:S(2)}, u32[]{:S(2)}) %collective-permute-start.10) | collective-permute-done | bytes 294944 | tf_op jit(solution)/shard_map/ppermute | solution.py:720
  116.7 7.6 %collective-permute-start.11 = (bf16[3,384,128]{2,1,0:T(8,128)(2,1)S(1)}, bf16[3,384,128]{2,1,0:T(8,128)(2,1)S(1)}, u32[]{:S(2)}, u32[]{:S(2)}) collective-permute-start(bf16[3,384,128]{2,1,0:T(8,128)(2,1)S(1)} %collective-permute-done.10), channel_id=1, source_target_pairs={{0,8},{1,9},{8,16},{9,17},{16,24},{17,25},{14,6},{15,7},{22,14},{2... | collective-permute-start | bytes 884744 | tf_op jit(solution)/shard_map/ppermute | solution.py:720
  124.4 30.6 %all_to_all.11.refs_4_ = f32[128,2,128]{2,1,0:T(2,128)S(1)} all-to-all(f32[128,2,128]{2,1,0:T(2,128)S(1)} %bitcast.6), channel_id=1, replica_groups={{0,2,4,6,8,10,12,14,16,18,20,22,24,26,28,30,32,34,36,38,40,42,44,46,48,..., dimensions={0} | all-to-all | bytes 262144 | tf_op jit(solution)/shard_map/all_to_all | solution.py:747
  154.9 1.4 shard_map.123
  156.4 7.8 %collective-permute-start.12 = (bf16[3,128,2048]{2,1,0:T(8,128)(2,1)S(1)}, bf16[3,128,2048]{2,1,0:T(8,128)(2,1)S(1)}, u32[]{:S(2)}, u32[]{:S(2)}) collective-permute-start(bf16[3,128,2048]{2,1,0:T(8,128)(2,1)S(1)} %shard_map.123), channel_id=1, source_target_pairs={{0,1},{1,0},{2,3},{3,2},{4,5},{5,4},{6,7},{7,6},{8,9},{9,8},{10,11... | collective-permute-start | bytes 4718600 | tf_op jit(solution)/shard_map/ppermute | solution.py:769
  164.2 3.0 %collective-permute-done.12.rec_ref = bf16[3,128,2048]{2,1,0:T(8,128)(2,1)S(1)} collective-permute-done((bf16[3,128,2048]{2,1,0:T(8,128)(2,1)S(1)}, bf16[3,128,2048]{2,1,0:T(8,128)(2,1)S(1)}, u32[]{:S(2)}, u32[]{:S(2)}) %collective-permute-start.12) | collective-permute-done | bytes 1572896 | tf_op jit(solution)/shard_map/ppermute | solution.py:769
  167.2 3.7 %shard_map.124 = (bf16[128,4096]{1,0:T(8,128)(2,1)}, bf16[128,4096]{1,0:T(8,128)(2,1)}, bf16[128,4096]{1,0:T(8,128)(2,1)}, f32[1,128]{1,0:T(1,128)}, f32[1,128]{1,0:T(1,128)}) custom-call(s32[16]{0:T(128)S(1)} %get-tuple-element.20.meta, bf16[2,3,128,2048]{3,2,1,0:T(8,128)(2,1)S(1)} %get-tuple-element.29.in_ref, ...), custom_call_target="tpu_custom_call" | custom-call | tf_op jit(solution)/shard_map/pallas_call | solution.py:688
  (21 shorter events, 0.1 us)
Async XLA Ops:
  0.7 8.9 %copy-start.1 = (s32[1,128]{1,0:T(1,128)S(1)}, s32[1,128]{1,0:T(1,128)}, u32[]{:S(2)}) copy-start(s32[1,128]{1,0:T(1,128)} %param.14) | copy-start | bytes 1540
  0.7 12.6 %copy-start.2 = (f32[1,16]{1,0:T(1,128)S(1)}, f32[1,16]{1,0:T(1,128)}, u32[]{:S(2)}) copy-start(f32[1,16]{1,0:T(1,128)} %param.12) | copy-start | bytes 196
  0.7 12.6 %copy-start.3 = (f32[1,16]{1,0:T(1,128)S(1)}, f32[1,16]{1,0:T(1,128)}, u32[]{:S(2)}) copy-start(f32[1,16]{1,0:T(1,128)} %param.13) | copy-start | bytes 196
  5.7 33.8 %collective-permute-start = (bf16[4,128,2048]{2,1,0:T(8,128)(2,1)}, bf16[4,128,2048]{2,1,0:T(8,128)(2,1)S(1)}, u32[]{:S(2)}, u32[]{:S(2)}) collective-permute-start(bf16[4,128,2048]{2,1,0:T(8,128)(2,1)} %shard_map.119), channel_id=1, source_target_pairs={{0,1},{1,0},{2,3},{3,2},{4,5},{5,4},{6,7},{7,6},{8,9},{9,8},{10,11... | collective-permute-start | bytes 6291464 | tf_op jit(solution)/shard_map/ppermute | solution.py:753
  9.7 3.1 %collective-permute-start.1 = (f32[2,128]{1,0:T(2,128)S(1)}, f32[2,128]{1,0:T(2,128)S(1)}, u32[]{:S(2)}, u32[]{:S(2)}) collective-permute-start(f32[2,128]{1,0:T(2,128)S(1)} %pad_convert_fusion), channel_id=1, source_target_pairs={{0,1},{1,0},{2,3},{3,2},{4,5},{5,4},{6,7},{7,6},{8,9},{9,8},{10,11... | collective-permute-start | bytes 3080 | tf_op jit(solution)/shard_map/ppermute | solution.py:752
  45.1 31.1 %collective-permute-start.2 = (bf16[4,1152,128]{2,1,0:T(8,128)(2,1)S(1)}, bf16[4,1152,128]{2,1,0:T(8,128)(2,1)S(1)}, u32[]{:S(2)}, u32[]{:S(2)}) collective-permute-start(bf16[4,1152,128]{2,1,0:T(8,128)(2,1)S(1)} %get-tuple-element.25), channel_id=1, source_target_pairs={{0,2},{1,3},{2,4},{3,5},{4,6},{5,7},{8,10},{9,11},{10,12},{11,13},... | collective-permute-start | bytes 3538952 | tf_op jit(solution)/shard_map/ppermute | solution.py:720
  47.2 29.0 %collective-permute-start.3 = (bf16[4,1152,128]{2,1,0:T(8,128)(2,1)S(1)}, bf16[4,1152,128]{2,1,0:T(8,128)(2,1)S(1)}, u32[]{:S(2)}, u32[]{:S(2)}) collective-permute-start(bf16[4,1152,128]{2,1,0:T(8,128)(2,1)S(1)} %get-tuple-element.26), channel_id=1, source_target_pairs={{2,0},{3,1},{4,2},{5,3},{6,4},{7,5},{10,8},{11,9},{12,10},{13,11},... | collective-permute-start | bytes 3538952 | tf_op jit(solution)/shard_map/ppermute | solution.py:720
  48.5 10.9 %collective-permute-start.5 = (bf16[4,384,128]{2,1,0:T(8,128)(2,1)S(1)}, bf16[4,384,128]{2,1,0:T(8,128)(2,1)S(1)}, u32[]{:S(2)}, u32[]{:S(2)}) collective-permute-start(bf16[4,384,128]{2,1,0:T(8,128)(2,1)S(1)} %get-tuple-element.28), channel_id=1, source_target_pairs={{6,0},{7,1},{14,8},{15,9},{22,16},{23,17},{8,14},{9,15},{16,22},{1... | collective-permute-start | bytes 1179656 | tf_op jit(solution)/shard_map/ppermute | solution.py:720
  49.8 26.4 %collective-permute-start.4 = (bf16[4,768,128]{2,1,0:T(8,128)(2,1)S(1)}, bf16[4,768,128]{2,1,0:T(8,128)(2,1)S(1)}, u32[]{:S(2)}, u32[]{:S(2)}) collective-permute-start(bf16[4,768,128]{2,1,0:T(8,128)(2,1)S(1)} %get-tuple-element.27), channel_id=1, source_target_pairs={{6,8},{7,9},{14,16},{15,17},{22,24},{23,25},{8,6},{9,7},{16,14},{1... | collective-permute-start | bytes 2359304 | tf_op jit(solution)/shard_map/ppermute | solution.py:720
  59.4 16.8 %collective-permute-start.6 = (bf16[4,384,128]{2,1,0:T(8,128)(2,1)S(1)}, bf16[4,384,128]{2,1,0:T(8,128)(2,1)S(1)}, u32[]{:S(2)}, u32[]{:S(2)}) collective-permute-start(bf16[4,384,128]{2,1,0:T(8,128)(2,1)S(1)} %collective-permute-done.5), channel_id=1, source_target_pairs={{0,8},{1,9},{8,16},{9,17},{16,24},{17,25},{14,6},{15,7},{22,14},{2... | collective-permute-start | bytes 1179656 | tf_op jit(solution)/shard_map/ppermute | solution.py:720
  74.6 1.6 copy-start
  85.0 70.0 %collective-permute-start.7 = (bf16[3,1152,128]{2,1,0:T(8,128)(2,1)S(1)}, bf16[3,1152,128]{2,1,0:T(8,128)(2,1)S(1)}, u32[]{:S(2)}, u32[]{:S(2)}) collective-permute-start(bf16[3,1152,128]{2,1,0:T(8,128)(2,1)S(1)} %get-tuple-element.30), channel_id=1, source_target_pairs={{0,2},{1,3},{2,4},{3,5},{4,6},{5,7},{8,10},{9,11},{10,12},{11,13},... | collective-permute-start | bytes 2654216 | tf_op jit(solution)/shard_map/ppermute | solution.py:720
  87.7 67.3 %collective-permute-start.8 = (bf16[3,1152,128]{2,1,0:T(8,128)(2,1)S(1)}, bf16[3,1152,128]{2,1,0:T(8,128)(2,1)S(1)}, u32[]{:S(2)}, u32[]{:S(2)}) collective-permute-start(bf16[3,1152,128]{2,1,0:T(8,128)(2,1)S(1)} %get-tuple-element.31), channel_id=1, source_target_pairs={{2,0},{3,1},{4,2},{5,3},{6,4},{7,5},{10,8},{11,9},{12,10},{13,11},... | collective-permute-start | bytes 2654216 | tf_op jit(solution)/shard_map/ppermute | solution.py:720
  89.0 27.7 %collective-permute-start.10 = (bf16[3,384,128]{2,1,0:T(8,128)(2,1)S(1)}, bf16[3,384,128]{2,1,0:T(8,128)(2,1)S(1)}, u32[]{:S(2)}, u32[]{:S(2)}) collective-permute-start(bf16[3,384,128]{2,1,0:T(8,128)(2,1)S(1)} %get-tuple-element.33), channel_id=1, source_target_pairs={{6,0},{7,1},{14,8},{15,9},{22,16},{23,17},{8,14},{9,15},{16,22},{1... | collective-permute-start | bytes 884744 | tf_op jit(solution)/shard_map/ppermute | solution.py:720
  90.4 64.5 %collective-permute-start.9 = (bf16[3,768,128]{2,1,0:T(8,128)(2,1)S(1)}, bf16[3,768,128]{2,1,0:T(8,128)(2,1)S(1)}, u32[]{:S(2)}, u32[]{:S(2)}) collective-permute-start(bf16[3,768,128]{2,1,0:T(8,128)(2,1)S(1)} %get-tuple-element.32), channel_id=1, source_target_pairs={{6,8},{7,9},{14,16},{15,17},{22,24},{23,25},{8,6},{9,7},{16,14},{1... | collective-permute-start | bytes 1769480 | tf_op jit(solution)/shard_map/ppermute | solution.py:720
  116.7 38.2 %collective-permute-start.11 = (bf16[3,384,128]{2,1,0:T(8,128)(2,1)S(1)}, bf16[3,384,128]{2,1,0:T(8,128)(2,1)S(1)}, u32[]{:S(2)}, u32[]{:S(2)}) collective-permute-start(bf16[3,384,128]{2,1,0:T(8,128)(2,1)S(1)} %collective-permute-done.10), channel_id=1, source_target_pairs={{0,8},{1,9},{8,16},{9,17},{16,24},{17,25},{14,6},{15,7},{22,14},{2... | collective-permute-start | bytes 884744 | tf_op jit(solution)/shard_map/ppermute | solution.py:720
  156.4 10.9 %collective-permute-start.12 = (bf16[3,128,2048]{2,1,0:T(8,128)(2,1)S(1)}, bf16[3,128,2048]{2,1,0:T(8,128)(2,1)S(1)}, u32[]{:S(2)}, u32[]{:S(2)}) collective-permute-start(bf16[3,128,2048]{2,1,0:T(8,128)(2,1)S(1)} %shard_map.123), channel_id=1, source_target_pairs={{0,1},{1,0},{2,3},{3,2},{4,5},{5,4},{6,7},{7,6},{8,9},{9,8},{10,11... | collective-permute-start | bytes 4718600 | tf_op jit(solution)/shard_map/ppermute | solution.py:769

commit v3 on v2

--- a/solution.py
+++ b/solution.py
@@ -18,13 +18,14 @@
 CAP = 1152
 FIRST = 768
 REST = CAP - FIRST
+HALF = CAP // 2
 PADDED = CAP + PAIR
 SCALE = HD**-0.5
 LOG2E = 1.4426950408889634
 BF = jnp.bfloat16
 F32 = jnp.float32
 CORE, CHIP, A_L, B_L, A_R, B_R, N_L, N_R, PA_L, PB_L, PA_R, PB_R = range(12)
-GROUP = 2
+KNOWN = 5
 ANYWHERE = pl.BlockSpec(memory_space=pl.ANY)
 IN_VMEM = pl.BlockSpec(memory_space=pltpu.VMEM)
 IN_SMEM = pl.BlockSpec(memory_space=pltpu.SMEM)
@@ -57,29 +58,47 @@
     return held.at[:, pl.ds(start, length), :]
 
 
-def pick_kernel(place, q_ref, k_ref, v_ref, d_ref, out_ref):
+def pick_kernel(
+    place, q_ref, k_ref, v_ref, d_ref, gain_cols, info, info_other, out_ref, known_ref, row
+):
     other = 1 - place[CORE]
+
+    @pl.when(pl.program_id(0) == 0)
+    def _():
+        width = gain_cols.shape[2]
+        row[...] = jnp.zeros_like(row)
+        for n in range(gain_cols.shape[0]):
+            row[0:2, n * width : (n + 1) * width] = gain_cols[n]
+        row[2:3, :] = info[0:1, :]
+        row[3:4, :] = info_other[0:1, :]
+        row[4:5, 0:1] = info[1:2, 0:1]
+        row[4:5, 1:2] = info_other[1:2, 0:1]
+        known_ref[...] = jnp.broadcast_to(row[0:KNOWN, :][None], known_ref.shape)
+
     for t, ref in enumerate((q_ref, k_ref, v_ref, d_ref)):
         for i in range(out_ref.shape[2] // HD):
             out_ref[t, :, i * HD : (i + 1) * HD] = ref[:, lanes(2 * i + other)]
 
 
-def pick_other(place, tensors, per=4):
+def pick_other(place, tensors, gain_cols, info, info_other, per=4):
+    known = jax.ShapeDtypeStruct((HEADS, KNOWN, HD), F32)
+    small = (gain_cols, info, info_other)
     return pl.pallas_call(
         pick_kernel,
-        out_shape=jax.ShapeDtypeStruct((4, ROWS, HEADS * HD), BF),
+        out_shape=(jax.ShapeDtypeStruct((4, ROWS, HEADS * HD), BF), known),
         grid_spec=pltpu.PrefetchScalarGridSpec(
             num_scalar_prefetch=1,
             grid=(HEADS // per,),
-            in_specs=own_specs(per)[:4],
-            out_specs=own_specs(per)[4],
+            in_specs=own_specs(per)[:4] + [whole(array.shape) for array in small],
+            out_specs=(own_specs(per)[4], whole(known.shape)),
+            scratch_shapes=[pltpu.VMEM((8, HD), F32)],
         ),
         compiler_params=params(12),
-    )(place, *tensors)
+    )(place, *tensors, *small)
 
 
 def chip_halves(info, core):
-    ids, counts = (info[1:2], info[2:3]), (info[0:1, 32:33], info[0:1, 33:34])
+    ids, counts = (info[0:1], info[1:2]), (info[2:3, 0:1], info[2:3, 1:2])
 
     def ordered(mine, other):
         return jnp.where(core == 0, mine, other), jnp.where(core == 0, other, mine)
@@ -101,12 +120,14 @@
     return blocks_a * ALIGN, blocks_b * ALIGN, to_left
 
 
-def write_plan(place, table, infos, meta):
+def chip_infos(table, chip):
+    spots = (chip, jnp.maximum(chip - 1, 0), jnp.minimum(chip + 1, HEADS - 1))
+    return [table[spot][2:KNOWN] for spot in spots]
+
+
+def write_plan(place, table, meta):
     core, chip = place[CORE], place[CHIP]
-    first = place[GROUP] * HEADS
-    spots = (chip, jnp.maximum(chip - 1, 0), jnp.minimum(chip + 1, HEADS - 1))
-    for n, spot in enumerate(spots):
-        infos[n] = table[first + spot]
+    infos = chip_infos(table, chip)
     own, _ = chip_halves(infos[0], core)
     left, _ = chip_halves(infos[1], core)
     right, _ = chip_halves(infos[2], core)
@@ -147,44 +168,47 @@
             copy.start()
 
 
-def send_pieces(meta, left, right, left_all, right_all, turn_first, turn_rest, sems):
-    def turn_copies(held):
-        return [
-            pltpu.make_async_copy(held.at[:, pl.ds(0, FIRST), :], turn_first, sems.at[0]),
-            pltpu.make_async_copy(held.at[:, pl.ds(FIRST, REST), :], turn_rest, sems.at[1]),
-        ]
-
-    by_left, by_right = turn_copies(left), turn_copies(right)
+def cut(table, *lengths):
+    starts = [sum(lengths[:n]) for n in range(len(lengths))]
+    return [table.at[:, pl.ds(a, n), :] for a, n in zip(starts, lengths, strict=True)]
+
+
+def copies_of(sources, targets, sems):
+    return [pltpu.make_async_copy(*trio) for trio in zip(sources, targets, sems, strict=True)]
+
+
+def send_pieces(meta, left, right, pieces, sems):
+    left_pieces, right_pieces, turn_pieces = pieces[0:2], pieces[2:4], pieces[4:6]
+    turn_sems = [sems.at[0], sems.at[1]]
+    by_left = copies_of(cut(left, FIRST, REST), turn_pieces, turn_sems)
+    by_right = copies_of(cut(right, FIRST, REST), turn_pieces, turn_sems)
     either(turns_left(meta), by_left, by_right)
     run_copies(
-        [
-            pltpu.make_async_copy(left, left_all, sems.at[2]),
-            pltpu.make_async_copy(right, right_all, sems.at[3]),
-        ]
+        copies_of(
+            cut(left, HALF, HALF) + cut(right, HALF, HALF),
+            (*left_pieces, *right_pieces),
+            [sems.at[n] for n in range(2, 6)],
+        )
     )
     for copy in by_left:
         copy.wait()
 
 
-def load_pieces(all_rows, turn_first, turn_rest, held, by_turn, sems):
-    spots = [held.at[:, pl.ds(0, FIRST), :], held.at[:, pl.ds(FIRST, REST), :]]
-    pieces = [all_rows.at[:, pl.ds(0, FIRST), :], all_rows.at[:, pl.ds(FIRST, REST), :]]
-
-    def copies(sources):
-        return [pltpu.make_async_copy(*pair) for pair in zip(sources, spots, sems, strict=True)]
-
-    straight = copies(pieces)
-    either(by_turn, copies((turn_first, turn_rest)), straight)
-    return straight
+def load_pieces(straight_pieces, turn_pieces, held, by_turn, sems):
+    spots = cut(held, HALF, FIRST - HALF, REST)
+    straight = [straight_pieces[0], *cut(straight_pieces[1], FIRST - HALF, REST)]
+    turned = [*cut(turn_pieces[0], HALF, FIRST - HALF), turn_pieces[1]]
+    plain = copies_of(straight, spots, sems)
+    either(by_turn, copies_of(turned, spots, sems), plain)
+    return plain
 
 
 def load_both(meta, pieces, held_left, held_right, sems):
-    from_left, from_right, turn_first, turn_rest = pieces
+    turn_pieces = pieces[4:6]
+    lefts, rights = [sems.at[n] for n in range(3)], [sems.at[n] for n in range(3, 6)]
     return load_pieces(
-        from_left, turn_first, turn_rest, held_left, turns_left(meta), (sems.at[0], sems.at[1])
-    ) + load_pieces(
-        from_right, turn_first, turn_rest, held_right, turns_right(meta), (sems.at[2], sems.at[3])
-    )
+        pieces[0:2], turn_pieces, held_left, turns_left(meta), lefts
+    ) + load_pieces(pieces[2:4], turn_pieces, held_right, turns_right(meta), rights)
 
 
 def half_rows(half):
@@ -207,9 +231,10 @@
     rec_ref,
     table,
     meta,
-    infos,
-    left_all,
-    right_all,
+    left_first,
+    left_second,
+    right_first,
+    right_second,
     turn_first,
     turn_rest,
     win,
@@ -223,7 +248,7 @@
 
     @pl.when(step == 0)
     def _():
-        write_plan(place, table, infos, meta)
+        write_plan(place, table, meta)
 
     fill_windows(win, core, (q_ref, k_ref, v_ref, d_ref), rec_ref)
     for i in range(per):
@@ -245,10 +270,7 @@
             meta,
             rows_of(left_ref, 0, CAP),
             rows_of(right_ref, PAIR, CAP),
-            left_all,
-            right_all,
-            turn_first,
-            turn_rest,
+            (left_first, left_second, right_first, right_second, turn_first, turn_rest),
             sems,
         )
 
@@ -260,7 +282,7 @@
 
 
 def pieces_shape(tensors):
-    return [jax.ShapeDtypeStruct((tensors, n, HD), BF) for n in (CAP, CAP, FIRST, REST)]
+    return [jax.ShapeDtypeStruct((tensors, n, HD), BF) for n in (HALF, HALF, HALF, HALF, FIRST, REST)]
 
 
 def pack_halos(place, tensors, rec, table, per=4):
@@ -268,19 +290,18 @@
         pack_kernel,
         out_shape=(
             jax.ShapeDtypeStruct((16,), jnp.int32),
-            jax.ShapeDtypeStruct((3, 3, HD), F32),
             *pieces_shape(4),
         ),
         grid_spec=pltpu.PrefetchScalarGridSpec(
             num_scalar_prefetch=1,
             grid=(HEADS // per,),
             in_specs=own_specs(per) + [whole(table.shape)],
-            out_specs=(IN_SMEM, whole((3, 3, HD)), *([ANYWHERE] * 4)),
+            out_specs=(IN_SMEM, *([ANYWHERE] * 6)),
             scratch_shapes=[
                 pltpu.VMEM((per, 4, PAIR, HD), BF),
                 pltpu.VMEM((4, PADDED, HD), BF),
                 pltpu.VMEM((4, PADDED, HD), BF),
-                pltpu.SemaphoreType.DMA((4,)),
+                pltpu.SemaphoreType.DMA((6,)),
             ],
         ),
         compiler_params=params(16),
@@ -338,7 +359,8 @@
     return results
 
 
-def link_codes(side, core, meta, infos):
+def link_codes(side, meta, table):
+    core, infos = meta[CORE], chip_infos(table, meta[CHIP])
     own_ids, own_counts = chip_halves(infos[0], core)
     _, far_counts = chip_halves(infos[side], core)
     codes = []
@@ -371,16 +393,6 @@
             ).astype(F32)
 
 
-def gather_gains(table, gains):
-    groups = table.shape[0] // HEADS
-    width = HD // groups
-    for n in range(groups):
-        part = table[n * HEADS : (n + 1) * HEADS, 0:1, :]
-        cols = slice(n * width, (n + 1) * width)
-        gains[:, 0:1, cols] = part[:, :, 0:width]
-        gains[:, 1:2, cols] = part[:, :, width : 2 * width]
-
-
 def mid_kernel(
     meta,
     q_ref,
@@ -388,11 +400,9 @@
     v_ref,
     d_ref,
     rec_ref,
-    infos,
     table,
     out_ref,
     gg_ref,
-    gains_ref,
     win,
     bias,
     q_live,
@@ -402,12 +412,11 @@
 
     @pl.when(pl.program_id(0) == 0)
     def _():
-        gather_gains(table, gains_ref)
-        fill_links(bias, q_live, link_codes(0, core, meta, infos))
+        fill_links(bias, q_live, link_codes(0, meta, table))
 
     fill_windows(win, core, (q_ref, k_ref, v_ref, d_ref), rec_ref)
     heads = [pl.program_id(0) * per + i for i in range(per)]
-    gains = [gains_ref[head] for head in heads]
+    gains = [table[head] for head in heads]
     results = solve(
         [
             (*(win[i, t] for t in range(4)), gains[i][0:1], gains[i][1:2], bias[...], q_live[0:1, :])
@@ -423,16 +432,16 @@
         gg_ref[heads[i]] = jnp.concatenate([part_q, part_k], axis=0)
 
 
-def solve_mid(meta, tensors, rec, infos, table, per=4):
+def solve_mid(meta, tensors, rec, table, per=4):
     per_head = jax.ShapeDtypeStruct((HEADS, 2, HD), F32)
     return pl.pallas_call(
         mid_kernel,
-        out_shape=(jax.ShapeDtypeStruct((2, 3, ROWS, HEADS * HD), BF), per_head, per_head),
+        out_shape=(jax.ShapeDtypeStruct((2, 3, ROWS, HEADS * HD), BF), per_head),
         grid_spec=pltpu.PrefetchScalarGridSpec(
             num_scalar_prefetch=1,
             grid=(HEADS // per,),
-            in_specs=own_specs(per) + [whole(infos.shape), whole(table.shape)],
-            out_specs=(half_spec(per), whole(per_head.shape), whole(per_head.shape)),
+            in_specs=own_specs(per) + [whole(table.shape)],
+            out_specs=(half_spec(per), whole(per_head.shape)),
             scratch_shapes=[
                 pltpu.VMEM((per, 4, PAIR, HD), BF),
                 pltpu.VMEM((PAIR, PAIR), F32),
@@ -440,7 +449,7 @@
             ],
         ),
         compiler_params=params(32),
-    )(meta, *tensors, rec, infos, table)
+    )(meta, *tensors, rec, table)
 
 
 def half_spec(per):
@@ -462,18 +471,21 @@
     v_ref,
     d_ref,
     rec_ref,
-    infos,
-    gains_ref,
+    table,
     mid_ref,
     gg_mid_ref,
-    from_left,
-    from_right,
+    from_left_first,
+    from_left_second,
+    from_right_first,
+    from_right_second,
     from_turn_first,
     from_turn_rest,
     out_ref,
     gg_ref,
-    left_all,
-    right_all,
+    left_first,
+    left_second,
+    right_first,
+    right_second,
     turn_first,
     turn_rest,
     win,
@@ -491,14 +503,21 @@
     def _():
         copies = load_both(
             meta,
-            (from_left, from_right, from_turn_first, from_turn_rest),
+            (
+                from_left_first,
+                from_left_second,
+                from_right_first,
+                from_right_second,
+                from_turn_first,
+                from_turn_rest,
+            ),
             rows_of(held.at[0], PAIR, CAP),
             rows_of(held.at[1], 0, CAP),
             sems,
         )
         for side in range(2):
             fill_links(
-                bias.at[side], q_live.at[side], link_codes(side + 1, core, meta, infos)
+                bias.at[side], q_live.at[side], link_codes(side + 1, meta, table)
             )
         gg_ref[...] = gg_mid_ref[...]
         for copy in copies:
@@ -526,7 +545,7 @@
                 row < bound(jnp.where(lefts[i], meta[B_L], jnp.where(use, PAIR, 0)))
             )
             window = [jnp.where(halo, held[side, t, source, :], win[i, t]) for t in range(4)]
-            gains = gains_ref[head]
+            gains = table[head]
             problems.append((*window, gains[0:1], gains[1:2], bias[side], q_live[side, 0:1, :]))
             spots.append((side, span, local, use.astype(F32)))
         for i, (grads, part_q, part_k) in enumerate(solve(problems)):
@@ -561,15 +580,12 @@
             meta,
             rows_of(back.at[0], PAIR, CAP),
             rows_of(back.at[1], 0, CAP),
-            left_all,
-            right_all,
-            turn_first,
-            turn_rest,
+            (left_first, left_second, right_first, right_second, turn_first, turn_rest),
             sems,
         )
 
 
-def solve_edges(meta, tensors, rec, infos, gains, mid, gg_mid, halos, per=4):
+def solve_edges(meta, tensors, rec, table, mid, gg_mid, halos, per=4):
     return pl.pallas_call(
         edge_kernel,
         out_shape=(
@@ -581,20 +597,20 @@
             num_scalar_prefetch=1,
             grid=(HEADS // per,),
             in_specs=own_specs(per)
-            + [whole(infos.shape), whole(gains.shape), half_spec(per), whole(gg_mid.shape)]
-            + [ANYWHERE] * 4,
-            out_specs=(half_spec(per), whole(gg_mid.shape), *([ANYWHERE] * 4)),
+            + [whole(table.shape), half_spec(per), whole(gg_mid.shape)]
+            + [ANYWHERE] * 6,
+            out_specs=(half_spec(per), whole(gg_mid.shape), *([ANYWHERE] * 6)),
             scratch_shapes=[
                 pltpu.VMEM((per, 4, PAIR, HD), BF),
                 pltpu.VMEM((2, PAIR, PAIR), F32),
                 pltpu.VMEM((2, 8, PAIR), F32),
                 pltpu.VMEM((2, 4, PADDED, HD), BF),
                 pltpu.VMEM((2, 3, PADDED + PAIR, HD), BF),
-                pltpu.SemaphoreType.DMA((4,)),
+                pltpu.SemaphoreType.DMA((6,)),
             ],
         ),
         compiler_params=params(40),
-    )(meta, *tensors, rec, infos, gains, mid, gg_mid, *halos)
+    )(meta, *tensors, rec, table, mid, gg_mid, *halos)
 
 
 def load_returned(meta, pieces, held_left, held_right, sems):
@@ -622,7 +638,7 @@
 
 
 def merge_kernel(meta, in_ref, *refs):
-    pieces, (_, send_ref, held_left, held_right, sems) = refs[:4], refs[4:]
+    pieces, (_, send_ref, held_left, held_right, sems) = refs[:6], refs[6:]
     per = in_ref.shape[3] // HD
     step = pl.program_id(0)
 
@@ -642,7 +658,7 @@
     return [
         pltpu.VMEM((3, PADDED, HD), BF),
         pltpu.VMEM((3, PADDED, HD), BF),
-        pltpu.SemaphoreType.DMA((4,)),
+        pltpu.SemaphoreType.DMA((6,)),
     ]
 
 
@@ -654,7 +670,7 @@
             num_scalar_prefetch=1,
             grid=(HEADS // per,),
             in_specs=[pl.BlockSpec((1, 3, ROWS, per * HD), lambda j, m: (1, 0, 0, j))]
-            + [ANYWHERE] * 5,
+            + [ANYWHERE] * 7,
             out_specs=pl.BlockSpec((3, ROWS, per * HD), lambda j, m: (0, 0, j)),
             scratch_shapes=held_scratch(),
         ),
@@ -663,7 +679,7 @@
 
 
 def weave_kernel(meta, in_ref, rec_ref, *refs):
-    pieces, (gg_parts, *outs, gg_q, gg_k, held_left, held_right, sems) = refs[:4], refs[4:]
+    pieces, (gg_parts, *outs, gg_q, gg_k, held_left, held_right, sems) = refs[:6], refs[6:]
     per = in_ref.shape[3] // HD
     core = meta[CORE]
     step = pl.program_id(0)
@@ -696,7 +712,7 @@
                 pl.BlockSpec((1, 3, ROWS, per * HD), lambda j, m: (0, 0, 0, j)),
                 pl.BlockSpec((3, ROWS, per * HD), lambda j, m: (0, 0, j)),
             ]
-            + [ANYWHERE] * 4
+            + [ANYWHERE] * 6
             + [whole(gg_parts.shape)],
             out_specs=(pl.BlockSpec((ROWS, 2 * per * HD), lambda j, m: (0, j)),) * 3
             + (whole((1, HD)),) * 2,
@@ -707,7 +723,7 @@
 
 
 def exchange(pieces, size):
-    left_all, right_all, turn_first, turn_rest = pieces
+    lefts, rights, (turn_first, turn_rest) = pieces[0:2], pieces[2:4], pieces[4:6]
     line = 2 * LINE
     wrap = line - 2
     turns = [(i, i + 2) for i in range(size - 2) if i % line >= wrap]
@@ -720,11 +736,11 @@
         return lax.ppermute(array, "seq", pairs)
 
     hop = move(turn_rest, [(i, i - wrap) for i, _ in turns] + [(j, j + wrap) for _, j in turns])
-    from_left = move(right_all, straight)
-    from_right = move(left_all, back(straight))
+    from_left = [move(piece, straight) for piece in rights]
+    from_right = [move(piece, back(straight)) for piece in lefts]
     from_turn = move(turn_first, turns + back(turns))
     from_hop = move(hop, [(i - wrap, j) for i, j in turns] + [(j + wrap, i) for i, j in turns])
-    return from_left, from_right, from_turn, from_hop
+    return (*from_left, *from_right, from_turn, from_hop)
 
 
 def shards(queries, keys, values, out_grad, gain_q, gain_k, clip_ids, counts):
@@ -733,37 +749,37 @@
     chips = size // 2
     seq = lax.axis_index("seq")
     swap = [(i, i ^ 1) for i in range(size)]
-    place = jnp.stack([seq % 2, seq // 2, lax.axis_index("dp")]).astype(jnp.int32)
+    place = jnp.stack([seq % 2, seq // 2]).astype(jnp.int32)
     tensors = tuple(
         pltpu.with_memory_space_constraint(t, pltpu.HBM)
         for t in (queries, keys, values, out_grad)
     )
 
-    def all_to_all(array):
-        same_core = [
-            [d * size + 2 * c + core for d in range(groups) for c in range(chips)]
-            for core in range(2)
-        ]
-        return lax.all_to_all(
-            array, ("dp", "seq"), 0, 0, axis_index_groups=same_core, tiled=True
-        )
+    same_core = [list(range(core, size, 2)) for core in range(2)]
+    same_cores = [
+        [d * size + at for d in range(groups) for at in one_core] for one_core in same_core
+    ]
+
+    def all_to_all(array, axis, among=None):
+        return lax.all_to_all(array, axis, 0, 0, axis_index_groups=among, tiled=True)
 
     info = jnp.concatenate([clip_ids, jnp.broadcast_to(counts, (1, ROWS))], axis=0).astype(F32)
     info_other = lax.ppermute(info, "seq", swap)
-    rec = lax.ppermute(pick_other(place, tensors), "seq", swap)
-    cells = [gain_q, gain_k, info[1:2, 0:1], info_other[1:2, 0:1]]
-    filled = sum(cell.shape[1] for cell in cells)
-    first = jnp.concatenate(cells + [jnp.zeros((1, HD - filled), F32)], axis=1)
-    known = jnp.concatenate([first, info[0:1], info_other[0:1]], axis=0)
-    table = all_to_all(jnp.broadcast_to(known[None], (groups * chips,) + known.shape))
-
-    meta, infos, *pieces = pack_halos(place, tensors, rec, table)
+    gain_own = jnp.concatenate([gain_q, gain_k], axis=0)
+    gain_cols = all_to_all(jnp.broadcast_to(gain_own[None], (groups,) + gain_own.shape), "dp")
+    picked, known = pick_other(place, tensors, gain_cols, info, info_other)
+    rec = lax.ppermute(picked, "seq", swap)
+    table = all_to_all(known, "seq", same_core)
+
+    meta, *pieces = pack_halos(place, tensors, rec, table)
     halos = exchange(pieces, size)
-    mid, gg_mid, gains = solve_mid(meta, tensors, rec, infos, table)
-    own, gg, *pieces = solve_edges(meta, tensors, rec, infos, gains, mid, gg_mid, halos)
+    mid, gg_mid = solve_mid(meta, tensors, rec, table)
+    own, gg, *pieces = solve_edges(meta, tensors, rec, table, mid, gg_mid, halos)
     returned = exchange(pieces, size)
     gg_parts = all_to_all(
-        jnp.broadcast_to(gg[None], (groups,) + gg.shape).reshape(groups * chips, 2, HD)
+        jnp.broadcast_to(gg[None], (groups,) + gg.shape).reshape(groups * chips, 2, HD),
+        ("dp", "seq"),
+        same_cores,
     )
     send = merge_other(meta, own, returned, gg_parts)
     other = lax.ppermute(send, "seq", swap)

time: 172 us -> 158 us (0.919)
  starting transfers between devices: 36.1 us -> 59.3 us
  waiting for transfers between devices: 40 us -> 17.7 us
  blocking collectives: 55.4 us -> 43.1 us
  local copies, waits for them, and re-layouts: 4.14 us -> 2.27 us
    ppermute x10 -> x14, waiting for transfers between devices: 34.5 us -> 11.9 us  [move(): return lax.ppermute(array, 'seq', pairs)]
    ppermute x10 -> x14, starting transfers between devices: 24.9 us -> 41.1 us  [move(): return lax.ppermute(array, 'seq', pairs)]
    all_to_all x2, blocking collectives: 55.4 us -> 43.1 us  [all_to_all(): lax.all_to_all(array, axis, 0, 0, axis_index_groups=among, tiled=True)]
    all_to_all x0 -> x1, starting transfers between devices: none -> 6.37 us  [all_to_all(): lax.all_to_all(array, axis, 0, 0, axis_index_groups=among, tiled=True)]
    all_to_all x0 -> x1, waiting for transfers between devices: none -> 1.95 us  [all_to_all(): lax.all_to_all(array, axis, 0, 0, axis_index_groups=among, tiled=True)]
    ppermute x1, waiting for transfers between devices: 2.5 us -> 0.74 us  [shards(): info_other = lax.ppermute(info, 'seq', swap)]
  transfers between devices with their start and end apart: 13 -> 18, of which waited for: 4 -> 6; matrix products, arithmetic and copies ran while one was open for 1% -> 0% of each run, Pallas kernels for 5% -> 6%
where the time goes in v3:
time: 158 us; the launch traced here: 159 us
  starting transfers between devices  59.3 us (38%)
  blocking collectives  43.1 us (27%)
  Pallas kernels  33.3 us (21%)
  waiting for transfers between devices  17.7 us (11%)
  local copies, waits for them, and re-layouts  2.27 us (1%)
  between operations  1.67 us (1%)
    all_to_all x2, blocking collectives, all_to_all(): lax.all_to_all(array, axis, 0, 0, axis_index_groups=among, tiled=True)  43.1 us
    ppermute x14, starting transfers between devices, move(): return lax.ppermute(array, 'seq', pairs)  41.1 us
    ppermute x14, waiting for transfers between devices, move(): return lax.ppermute(array, 'seq', pairs)  11.9 us
    pallas_call x1, Pallas kernels, solve_edges(): pl.pallas_call(edge_kernel, out_shape=(jax.ShapeDtypeStruct(mid.shape, BF...  9.21 us
    pallas_call x1, Pallas kernels, solve_mid(): pl.pallas_call(mid_kernel, out_shape=(jax.ShapeDtypeStruct((2, 3, ROWS, H...  9.21 us
    ppermute x1, starting transfers between devices, shards(): other = lax.ppermute(send, 'seq', swap)  8.62 us
    all_to_all x1, starting transfers between devices, all_to_all(): lax.all_to_all(array, axis, 0, 0, axis_index_groups=among, tiled=True)  6.37 us
    pallas_call x1, Pallas kernels, pack_halos(): pl.pallas_call(pack_kernel, out_shape=(jax.ShapeDtypeStruct((16,), jnp.in...  5.53 us
  transfers between devices with their start and end apart: 18, of which 6 were waited for; matrix products, arithmetic and copies ran while one was open for 0% of the time, Pallas kernels for 6%

profile of v3, /device:TPU:1, one launch (start us, length us, event | category | flops | bytes accessed | tf_op | source)
XLA Modules:
  0.0 158.8 jit_solution(10721185786074201929)
XLA Ops:
  1.9 6.4 %all-to-all-start = ((f32[8,2,16]{2,1,0:T(2,128)}), f32[8,2,16]{2,1,0:T(2,128)S(1)}, u32[]{:S(2)}, u32[]{:S(2)}) async-start(f32[8,2,16]{2,1,0:T(2,128)} %broadcast_in_dim.6), calls=%async_computation | async-start | bytes 16384 | tf_op jit(solution)/shard_map/all_to_all | solution.py:764
  9.6 1.0 collective-permute-start
  10.6 0.7 collective-permute-done.info_other
  11.4 1.9 %all-to-all-done.gain_cols = f32[8,2,16]{2,1,0:T(2,128)S(1)} async-done(((f32[8,2,16]{2,1,0:T(2,128)}), f32[8,2,16]{2,1,0:T(2,128)S(1)}, u32[]{:S(2)}, u32[]{:S(2)}) %all-to-all-start) | async-done | bytes 1056 | tf_op jit(solution)/shard_map/all_to_all | solution.py:764
  13.3 3.8 %shard_map.119 = (bf16[4,128,2048]{2,1,0:T(8,128)(2,1)S(1)}, f32[16,5,128]{2,1,0:T(8,128)S(1)}) custom-call(s32[2]{0:T(128)S(1)} %pad_add_fusion.place, bf16[128,4096]{1,0:T(8,128)(2,1)} %q_ref.7, bf16[128,4096]{1,0:T(8,128)(2,1)} %k_ref.7, bf16[128,4096]{1,0:T(8,128)(2,1)} %v_ref.7, bf16[128,4096]{1,0:T(8,128)(2,1)} %d_ref.7, ...), custom_call_target="tpu_custom_call" | custom-call | tf_op jit(solution)/shard_map/pallas_call | solution.py:86
  17.1 2.2 %collective-permute-start.1 = (bf16[4,128,2048]{2,1,0:T(8,128)(2,1)S(1)}, bf16[4,128,2048]{2,1,0:T(8,128)(2,1)S(1)}, u32[]{:S(2)}, u32[]{:S(2)}) collective-permute-start(bf16[4,128,2048]{2,1,0:T(8,128)(2,1)S(1)} %get-tuple-element.24), channel_id=1, source_target_pairs={{0,1},{1,0},{2,3},{3,2},{4,5},{5,4},{6,7},{7,6},{8,9},{9,8},{10,11... | collective-permute-start | bytes 6291464 | tf_op jit(solution)/shard_map/ppermute | solution.py:771
  19.3 18.6 %all_to_all.15.table = f32[16,5,128]{2,1,0:T(8,128)S(1)} all-to-all(f32[16,5,128]{2,1,0:T(8,128)S(1)} %get-tuple-element.25), channel_id=1, replica_groups={{0,2,4,6,8,10,12,14,16,18,20,22,24,26,28,30},{1,3,5,7,9,11,13,15,17,19,..., dimensions={0} | all-to-all | bytes 81920 | tf_op jit(solution)/shard_map/all_to_all | solution.py:764
  37.9 5.5 %shard_map.120 = (s32[16]{0:T(128)S(1)}, bf16[4,576,128]{2,1,0:T(8,128)(2,1)S(1)}, bf16[4,576,128]{2,1,0:T(8,128)(2,1)S(1)}, bf16[4,576,128]{2,1,0:T(8,128)(2,1)...) custom-call(s32[2]{0:T(128)S(1)} %pad_add_fusion.place, ...), custom_call_target="tpu_custom_call" | custom-call | tf_op jit(solution)/shard_map/pallas_call | solution.py:289
  43.5 1.3 collective-permute-start.7
  44.8 1.5 collective-permute-start.2
  46.3 0.7 collective-permute-start.6
  47.0 2.8 %collective-permute-start.3 = (bf16[4,576,128]{2,1,0:T(8,128)(2,1)S(1)}, bf16[4,576,128]{2,1,0:T(8,128)(2,1)S(1)}, u32[]{:S(2)}, u32[]{:S(2)}) collective-permute-start(bf16[4,576,128]{2,1,0:T(8,128)(2,1)S(1)} %get-tuple-element.30), channel_id=1, source_target_pairs={{0,2},{1,3},{2,4},{3,5},{4,6},{5,7},{8,10},{9,11},{10,12},{11,13},... | collective-permute-start | bytes 1769480 | tf_op jit(solution)/shard_map/ppermute | solution.py:736
  49.8 1.3 collective-permute-start.4
  51.1 4.6 %collective-permute-done.7 = bf16[4,384,128]{2,1,0:T(8,128)(2,1)S(1)} collective-permute-done((bf16[4,384,128]{2,1,0:T(8,128)(2,1)S(1)}, bf16[4,384,128]{2,1,0:T(8,128)(2,1)S(1)}, u32[]{:S(2)}, u32[]{:S(2)}) %collective-permute-start.7) | collective-permute-done | bytes 393248 | tf_op jit(solution)/shard_map/ppermute | solution.py:736
  55.7 1.3 collective-permute-start.5
  57.4 19.5 %collective-permute-start.8 = (bf16[4,384,128]{2,1,0:T(8,128)(2,1)S(1)}, bf16[4,384,128]{2,1,0:T(8,128)(2,1)S(1)}, u32[]{:S(2)}, u32[]{:S(2)}) collective-permute-start(bf16[4,384,128]{2,1,0:T(8,128)(2,1)S(1)} %collective-permute-done.7), channel_id=1, source_target_pairs={{0,8},{1,9},{8,16},{9,17},{16,24},{17,25},{14,6},{15,7},{22,14},{2... | collective-permute-start | bytes 1179656 | tf_op jit(solution)/shard_map/ppermute | solution.py:736
  76.9 9.2 %shard_map.121 = (bf16[2,3,128,2048]{3,2,1,0:T(8,128)(2,1)S(1)}, f32[16,2,128]{2,1,0:T(2,128)S(1)}) custom-call(s32[16]{0:T(128)S(1)} %get-tuple-element.26.meta, bf16[128,4096]{1,0:T(8,128)(2,1)} %q_ref.7, bf16[128,4096]{1,0:T(8,128)(2,1)} %k_ref.7, bf16[128,4096]{1,0:T(8,128)(2,1)} %v_ref.7, bf16[128,4096]{1,0:T(8,128)(2,1)} %d_ref.7, ...), custom_call_target="tpu_custom_call" | custom-call | tf_op jit(solution)/shard_map/pallas_call | solution.py:437
  86.1 1.6 %copy-done = bf16[2,3,128,2048]{3,2,1,0:T(8,128)(2,1)} copy-done((bf16[2,3,128,2048]{3,2,1,0:T(8,128)(2,1)}, bf16[2,3,128,2048]{3,2,1,0:T(8,128)(2,1)S(1)}, u32[]{:S(2)}) %copy-start) | copy-done | bytes 3145752
  87.8 9.2 %shard_map.122 = (bf16[2,3,128,2048]{3,2,1,0:T(8,128)(2,1)S(1)}, f32[16,2,128]{2,1,0:T(2,128)S(1)}, bf16[3,576,128]{2,1,0:T(8,128)(2,1)S(1)}, bf16[3,576,128]{2,...) custom-call(s32[16]{0:T(128)S(1)} %get-tuple-element.26.meta, ...), custom_call_target="tpu_custom_call" | custom-call | tf_op jit(solution)/shard_map/pallas_call | solution.py:589
  97.0 1.3 collective-permute-start.14
  98.3 1.3 collective-permute-start.9
  99.6 0.7 collective-permute-start.13
  100.3 1.3 collective-permute-start.10
  101.6 1.3 collective-permute-start.11
  102.9 6.9 %collective-permute-done.14 = bf16[3,384,128]{2,1,0:T(8,128)(2,1)S(1)} collective-permute-done((bf16[3,384,128]{2,1,0:T(8,128)(2,1)S(1)}, bf16[3,384,128]{2,1,0:T(8,128)(2,1)S(1)}, u32[]{:S(2)}, u32[]{:S(2)}) %collective-permute-start.14) | collective-permute-done | bytes 294944 | tf_op jit(solution)/shard_map/ppermute | solution.py:736
  109.9 1.3 collective-permute-start.12
  111.2 5.6 %collective-permute-start.15 = (bf16[3,384,128]{2,1,0:T(8,128)(2,1)S(1)}, bf16[3,384,128]{2,1,0:T(8,128)(2,1)S(1)}, u32[]{:S(2)}, u32[]{:S(2)}) collective-permute-start(bf16[3,384,128]{2,1,0:T(8,128)(2,1)S(1)} %collective-permute-done.14), channel_id=1, source_target_pairs={{0,8},{1,9},{8,16},{9,17},{16,24},{17,25},{14,6},{15,7},{22,14},{2... | collective-permute-start | bytes 884744 | tf_op jit(solution)/shard_map/ppermute | solution.py:736
  116.8 24.5 %all_to_all.16.refs_6_ = f32[128,2,128]{2,1,0:T(2,128)S(1)} all-to-all(f32[128,2,128]{2,1,0:T(2,128)S(1)} %bitcast.5), channel_id=1, replica_groups={{0,2,4,6,8,10,12,14,16,18,20,22,24,26,28,30,32,34,36,38,40,42,44,46,48,..., dimensions={0} | all-to-all | bytes 262144 | tf_op jit(solution)/shard_map/all_to_all | solution.py:764
  141.3 1.7 %shard_map.123 = bf16[3,128,2048]{2,1,0:T(8,128)(2,1)S(1)} custom-call(s32[16]{0:T(128)S(1)} %get-tuple-element.26.meta, bf16[2,3,128,2048]{3,2,1,0:T(8,128)(2,1)S(1)} %get-tuple-element.35.in_ref, bf16[3,576,128]{2,1,0:T(8,128)(2,1)S(1)} %collective-permute-done.9.refs_0_, bf16[3,576,128]{2,1,0:T(8,128)(2,1)S(1)} %collective-permute-done.10.refs_1_, ...), custom_call_target="tpu_custom_call" | custom-call | tf_op jit(solution)/shard_map/pallas_call | solution.py:666
  143.0 8.6 %collective-permute-start.16 = (bf16[3,128,2048]{2,1,0:T(8,128)(2,1)S(1)}, bf16[3,128,2048]{2,1,0:T(8,128)(2,1)S(1)}, u32[]{:S(2)}, u32[]{:S(2)}) collective-permute-start(bf16[3,128,2048]{2,1,0:T(8,128)(2,1)S(1)} %shard_map.123), channel_id=1, source_target_pairs={{0,1},{1,0},{2,3},{3,2},{4,5},{5,4},{6,7},{7,6},{8,9},{9,8},{10,11... | collective-permute-start | bytes 4718600 | tf_op jit(solution)/shard_map/ppermute | solution.py:785
  151.6 3.0 %collective-permute-done.16.rec_ref = bf16[3,128,2048]{2,1,0:T(8,128)(2,1)S(1)} collective-permute-done((bf16[3,128,2048]{2,1,0:T(8,128)(2,1)S(1)}, bf16[3,128,2048]{2,1,0:T(8,128)(2,1)S(1)}, u32[]{:S(2)}, u32[]{:S(2)}) %collective-permute-start.16) | collective-permute-done | bytes 1572896 | tf_op jit(solution)/shard_map/ppermute | solution.py:785
  154.6 3.9 %shard_map.124 = (bf16[128,4096]{1,0:T(8,128)(2,1)}, bf16[128,4096]{1,0:T(8,128)(2,1)}, bf16[128,4096]{1,0:T(8,128)(2,1)}, f32[1,128]{1,0:T(1,128)}, f32[1,128]{1,0:T(1,128)}) custom-call(s32[16]{0:T(128)S(1)} %get-tuple-element.26.meta, bf16[2,3,128,2048]{3,2,1,0:T(8,128)(2,1)S(1)} %get-tuple-element.35.in_ref, ...), custom_call_target="tpu_custom_call" | custom-call | tf_op jit(solution)/shard_map/pallas_call | solution.py:704
  (19 shorter events, 2.5 us)
Async XLA Ops:
  1.9 11.4 %all-to-all-start = ((f32[8,2,16]{2,1,0:T(2,128)}), f32[8,2,16]{2,1,0:T(2,128)S(1)}, u32[]{:S(2)}, u32[]{:S(2)}) async-start(f32[8,2,16]{2,1,0:T(2,128)} %broadcast_in_dim.6), calls=%async_computation | async-start | bytes 16384 | tf_op jit(solution)/shard_map/all_to_all | solution.py:764
  9.6 1.8 %collective-permute-start = (f32[2,128]{1,0:T(2,128)S(1)}, f32[2,128]{1,0:T(2,128)S(1)}, u32[]{:S(2)}, u32[]{:S(2)}) collective-permute-start(f32[2,128]{1,0:T(2,128)S(1)} %pad_convert_fusion.info), channel_id=1, source_target_pairs={{0,1},{1,0},{2,3},{3,2},{4,5},{5,4},{6,7},{7,6},{8,9},{9,8},{10,11... | collective-permute-start | bytes 3080 | tf_op jit(solution)/shard_map/ppermute | solution.py:767
  17.1 20.8 %collective-permute-start.1 = (bf16[4,128,2048]{2,1,0:T(8,128)(2,1)S(1)}, bf16[4,128,2048]{2,1,0:T(8,128)(2,1)S(1)}, u32[]{:S(2)}, u32[]{:S(2)}) collective-permute-start(bf16[4,128,2048]{2,1,0:T(8,128)(2,1)S(1)} %get-tuple-element.24), channel_id=1, source_target_pairs={{0,1},{1,0},{2,3},{3,2},{4,5},{5,4},{6,7},{7,6},{8,9},{9,8},{10,11... | collective-permute-start | bytes 6291464 | tf_op jit(solution)/shard_map/ppermute | solution.py:771
  43.5 12.2 %collective-permute-start.7 = (bf16[4,384,128]{2,1,0:T(8,128)(2,1)S(1)}, bf16[4,384,128]{2,1,0:T(8,128)(2,1)S(1)}, u32[]{:S(2)}, u32[]{:S(2)}) collective-permute-start(bf16[4,384,128]{2,1,0:T(8,128)(2,1)S(1)} %get-tuple-element.34), channel_id=1, source_target_pairs={{6,0},{7,1},{14,8},{15,9},{22,16},{23,17},{8,14},{9,15},{16,22},{1... | collective-permute-start | bytes 1179656 | tf_op jit(solution)/shard_map/ppermute | solution.py:736
  44.8 12.6 %collective-permute-start.2 = (bf16[4,576,128]{2,1,0:T(8,128)(2,1)S(1)}, bf16[4,576,128]{2,1,0:T(8,128)(2,1)S(1)}, u32[]{:S(2)}, u32[]{:S(2)}) collective-permute-start(bf16[4,576,128]{2,1,0:T(8,128)(2,1)S(1)} %get-tuple-element.29), channel_id=1, source_target_pairs={{0,2},{1,3},{2,4},{3,5},{4,6},{5,7},{8,10},{9,11},{10,12},{11,13},... | collective-permute-start | bytes 1769480 | tf_op jit(solution)/shard_map/ppermute | solution.py:736
  46.3 41.5 %collective-permute-start.6 = (bf16[4,768,128]{2,1,0:T(8,128)(2,1)S(1)}, bf16[4,768,128]{2,1,0:T(8,128)(2,1)S(1)}, u32[]{:S(2)}, u32[]{:S(2)}) collective-permute-start(bf16[4,768,128]{2,1,0:T(8,128)(2,1)S(1)} %get-tuple-element.33), channel_id=1, source_target_pairs={{6,8},{7,9},{14,16},{15,17},{22,24},{23,25},{8,6},{9,7},{16,14},{1... | collective-permute-start | bytes 2359304 | tf_op jit(solution)/shard_map/ppermute | solution.py:736
  47.0 40.7 %collective-permute-start.3 = (bf16[4,576,128]{2,1,0:T(8,128)(2,1)S(1)}, bf16[4,576,128]{2,1,0:T(8,128)(2,1)S(1)}, u32[]{:S(2)}, u32[]{:S(2)}) collective-permute-start(bf16[4,576,128]{2,1,0:T(8,128)(2,1)S(1)} %get-tuple-element.30), channel_id=1, source_target_pairs={{0,2},{1,3},{2,4},{3,5},{4,6},{5,7},{8,10},{9,11},{10,12},{11,13},... | collective-permute-start | bytes 1769480 | tf_op jit(solution)/shard_map/ppermute | solution.py:736
  49.8 37.9 %collective-permute-start.4 = (bf16[4,576,128]{2,1,0:T(8,128)(2,1)S(1)}, bf16[4,576,128]{2,1,0:T(8,128)(2,1)S(1)}, u32[]{:S(2)}, u32[]{:S(2)}) collective-permute-start(bf16[4,576,128]{2,1,0:T(8,128)(2,1)S(1)} %get-tuple-element.31), channel_id=1, source_target_pairs={{2,0},{3,1},{4,2},{5,3},{6,4},{7,5},{10,8},{11,9},{12,10},{13,11},... | collective-permute-start | bytes 1769480 | tf_op jit(solution)/shard_map/ppermute | solution.py:736
  55.7 32.0 %collective-permute-start.5 = (bf16[4,576,128]{2,1,0:T(8,128)(2,1)S(1)}, bf16[4,576,128]{2,1,0:T(8,128)(2,1)S(1)}, u32[]{:S(2)}, u32[]{:S(2)}) collective-permute-start(bf16[4,576,128]{2,1,0:T(8,128)(2,1)S(1)} %get-tuple-element.32), channel_id=1, source_target_pairs={{2,0},{3,1},{4,2},{5,3},{6,4},{7,5},{10,8},{11,9},{12,10},{13,11},... | collective-permute-start | bytes 1769480 | tf_op jit(solution)/shard_map/ppermute | solution.py:736
  57.4 30.4 %collective-permute-start.8 = (bf16[4,384,128]{2,1,0:T(8,128)(2,1)S(1)}, bf16[4,384,128]{2,1,0:T(8,128)(2,1)S(1)}, u32[]{:S(2)}, u32[]{:S(2)}) collective-permute-start(bf16[4,384,128]{2,1,0:T(8,128)(2,1)S(1)} %collective-permute-done.7), channel_id=1, source_target_pairs={{0,8},{1,9},{8,16},{9,17},{16,24},{17,25},{14,6},{15,7},{22,14},{2... | collective-permute-start | bytes 1179656 | tf_op jit(solution)/shard_map/ppermute | solution.py:736
  86.1 1.6 %copy-start = (bf16[2,3,128,2048]{3,2,1,0:T(8,128)(2,1)}, bf16[2,3,128,2048]{3,2,1,0:T(8,128)(2,1)S(1)}, u32[]{:S(2)}) copy-start(bf16[2,3,128,2048]{3,2,1,0:T(8,128)(2,1)S(1)} %get-tuple-element.27.mid_ref) | copy-start | bytes 9437188
  97.0 12.9 %collective-permute-start.14 = (bf16[3,384,128]{2,1,0:T(8,128)(2,1)S(1)}, bf16[3,384,128]{2,1,0:T(8,128)(2,1)S(1)}, u32[]{:S(2)}, u32[]{:S(2)}) collective-permute-start(bf16[3,384,128]{2,1,0:T(8,128)(2,1)S(1)} %get-tuple-element.41), channel_id=1, source_target_pairs={{6,0},{7,1},{14,8},{15,9},{22,16},{23,17},{8,14},{9,15},{16,22},{1... | collective-permute-start | bytes 884744 | tf_op jit(solution)/shard_map/ppermute | solution.py:736
  98.3 12.9 %collective-permute-start.9 = (bf16[3,576,128]{2,1,0:T(8,128)(2,1)S(1)}, bf16[3,576,128]{2,1,0:T(8,128)(2,1)S(1)}, u32[]{:S(2)}, u32[]{:S(2)}) collective-permute-start(bf16[3,576,128]{2,1,0:T(8,128)(2,1)S(1)} %get-tuple-element.36), channel_id=1, source_target_pairs={{0,2},{1,3},{2,4},{3,5},{4,6},{5,7},{8,10},{9,11},{10,12},{11,13},... | collective-permute-start | bytes 1327112 | tf_op jit(solution)/shard_map/ppermute | solution.py:736
  99.6 41.7 %collective-permute-start.13 = (bf16[3,768,128]{2,1,0:T(8,128)(2,1)S(1)}, bf16[3,768,128]{2,1,0:T(8,128)(2,1)S(1)}, u32[]{:S(2)}, u32[]{:S(2)}) collective-permute-start(bf16[3,768,128]{2,1,0:T(8,128)(2,1)S(1)} %get-tuple-element.40), channel_id=1, source_target_pairs={{6,8},{7,9},{14,16},{15,17},{22,24},{23,25},{8,6},{9,7},{16,14},{1... | collective-permute-start | bytes 1769480 | tf_op jit(solution)/shard_map/ppermute | solution.py:736
  100.3 40.9 %collective-permute-start.10 = (bf16[3,576,128]{2,1,0:T(8,128)(2,1)S(1)}, bf16[3,576,128]{2,1,0:T(8,128)(2,1)S(1)}, u32[]{:S(2)}, u32[]{:S(2)}) collective-permute-start(bf16[3,576,128]{2,1,0:T(8,128)(2,1)S(1)} %get-tuple-element.37), channel_id=1, source_target_pairs={{0,2},{1,3},{2,4},{3,5},{4,6},{5,7},{8,10},{9,11},{10,12},{11,13},... | collective-permute-start | bytes 1327112 | tf_op jit(solution)/shard_map/ppermute | solution.py:736
  101.6 39.6 %collective-permute-start.11 = (bf16[3,576,128]{2,1,0:T(8,128)(2,1)S(1)}, bf16[3,576,128]{2,1,0:T(8,128)(2,1)S(1)}, u32[]{:S(2)}, u32[]{:S(2)}) collective-permute-start(bf16[3,576,128]{2,1,0:T(8,128)(2,1)S(1)} %get-tuple-element.38), channel_id=1, source_target_pairs={{2,0},{3,1},{4,2},{5,3},{6,4},{7,5},{10,8},{11,9},{12,10},{13,11},... | collective-permute-start | bytes 1327112 | tf_op jit(solution)/shard_map/ppermute | solution.py:736
  109.9 31.4 %collective-permute-start.12 = (bf16[3,576,128]{2,1,0:T(8,128)(2,1)S(1)}, bf16[3,576,128]{2,1,0:T(8,128)(2,1)S(1)}, u32[]{:S(2)}, u32[]{:S(2)}) collective-permute-start(bf16[3,576,128]{2,1,0:T(8,128)(2,1)S(1)} %get-tuple-element.39), channel_id=1, source_target_pairs={{2,0},{3,1},{4,2},{5,3},{6,4},{7,5},{10,8},{11,9},{12,10},{13,11},... | collective-permute-start | bytes 1327112 | tf_op jit(solution)/shard_map/ppermute | solution.py:736
  111.2 30.1 %collective-permute-start.15 = (bf16[3,384,128]{2,1,0:T(8,128)(2,1)S(1)}, bf16[3,384,128]{2,1,0:T(8,128)(2,1)S(1)}, u32[]{:S(2)}, u32[]{:S(2)}) collective-permute-start(bf16[3,384,128]{2,1,0:T(8,128)(2,1)S(1)} %collective-permute-done.14), channel_id=1, source_target_pairs={{0,8},{1,9},{8,16},{9,17},{16,24},{17,25},{14,6},{15,7},{22,14},{2... | collective-permute-start | bytes 884744 | tf_op jit(solution)/shard_map/ppermute | solution.py:736
  143.0 11.7 %collective-permute-start.16 = (bf16[3,128,2048]{2,1,0:T(8,128)(2,1)S(1)}, bf16[3,128,2048]{2,1,0:T(8,128)(2,1)S(1)}, u32[]{:S(2)}, u32[]{:S(2)}) collective-permute-start(bf16[3,128,2048]{2,1,0:T(8,128)(2,1)S(1)} %shard_map.123), channel_id=1, source_target_pairs={{0,1},{1,0},{2,3},{3,2},{4,5},{5,4},{6,7},{7,6},{8,9},{9,8},{10,11... | collective-permute-start | bytes 4718600 | tf_op jit(solution)/shard_map/ppermute | solution.py:785

commit v4 on v3

--- a/solution.py
+++ b/solution.py
@@ -16,9 +16,10 @@
 ALIGN = 16
 LINE = 4
 CAP = 1152
+PARTS = (CAP // 2,) * 2
 FIRST = 768
 REST = CAP - FIRST
-HALF = CAP // 2
+SENT = len(PARTS) + 2
 PADDED = CAP + PAIR
 SCALE = HD**-0.5
 LOG2E = 1.4426950408889634
@@ -148,24 +149,13 @@
         meta[n] = value
 
 
-def turns_left(meta):
-    return lax.rem(meta[CHIP], LINE) == 0
-
-
-def turns_right(meta):
-    return lax.rem(meta[CHIP], LINE) == LINE - 1
-
-
-def either(wanted, yes, no):
-    @pl.when(wanted)
-    def _():
-        for copy in yes:
-            copy.start()
-
-    @pl.when(jnp.logical_not(wanted))
-    def _():
-        for copy in no:
-            copy.start()
+def even(meta):
+    return lax.rem(meta[CHIP], 2) == 0
+
+
+def at_corner(meta):
+    place = lax.rem(meta[CHIP], LINE)
+    return (place == 0) | (place == LINE - 1)
 
 
 def cut(table, *lengths):
@@ -174,41 +164,59 @@
 
 
 def copies_of(sources, targets, sems):
-    return [pltpu.make_async_copy(*trio) for trio in zip(sources, targets, sems, strict=True)]
+    return [
+        pltpu.make_async_copy(a, b, sems.at[n])
+        for n, (a, b) in enumerate(zip(sources, targets, strict=True))
+    ]
+
+
+def start_one(cases):
+    for wanted, copies in cases:
+
+        @pl.when(wanted)
+        def _():
+            for copy in copies:
+                copy.start()
+
+    return cases[0][1]
+
+
+def wait_all(copies):
+    for copy in copies:
+        copy.wait()
 
 
 def send_pieces(meta, left, right, pieces, sems):
-    left_pieces, right_pieces, turn_pieces = pieces[0:2], pieces[2:4], pieces[4:6]
-    turn_sems = [sems.at[0], sems.at[1]]
-    by_left = copies_of(cut(left, FIRST, REST), turn_pieces, turn_sems)
-    by_right = copies_of(cut(right, FIRST, REST), turn_pieces, turn_sems)
-    either(turns_left(meta), by_left, by_right)
-    run_copies(
-        copies_of(
-            cut(left, HALF, HALF) + cut(right, HALF, HALF),
-            (*left_pieces, *right_pieces),
-            [sems.at[n] for n in range(2, 6)],
+    def pieces_of(a, b):
+        return copies_of(cut(a, *PARTS) + cut(b, FIRST, REST), pieces, sems)
+
+    is_even = even(meta)
+    wait_all(
+        start_one(
+            [
+                (is_even, pieces_of(right, left)),
+                (jnp.logical_not(is_even), pieces_of(left, right)),
+            ]
         )
     )
-    for copy in by_left:
-        copy.wait()
-
-
-def load_pieces(straight_pieces, turn_pieces, held, by_turn, sems):
-    spots = cut(held, HALF, FIRST - HALF, REST)
-    straight = [straight_pieces[0], *cut(straight_pieces[1], FIRST - HALF, REST)]
-    turned = [*cut(turn_pieces[0], HALF, FIRST - HALF), turn_pieces[1]]
-    plain = copies_of(straight, spots, sems)
-    either(by_turn, copies_of(turned, spots, sems), plain)
-    return plain
 
 
 def load_both(meta, pieces, held_left, held_right, sems):
-    turn_pieces = pieces[4:6]
-    lefts, rights = [sems.at[n] for n in range(3)], [sems.at[n] for n in range(3, 6)]
-    return load_pieces(
-        pieces[0:2], turn_pieces, held_left, turns_left(meta), lefts
-    ) + load_pieces(pieces[2:4], turn_pieces, held_right, turns_right(meta), rights)
+    *direct, rest, relayed = pieces
+
+    def pieces_of(a, b, last):
+        return copies_of([*direct, last], cut(a, *PARTS) + cut(b, FIRST, REST), sems)
+
+    is_even, corner = even(meta), at_corner(meta)
+    is_odd, inner = jnp.logical_not(is_even), jnp.logical_not(corner)
+    return start_one(
+        [
+            (is_even & corner, pieces_of(held_right, held_left, relayed)),
+            (is_even & inner, pieces_of(held_right, held_left, rest)),
+            (is_odd & corner, pieces_of(held_left, held_right, relayed)),
+            (is_odd & inner, pieces_of(held_left, held_right, rest)),
+        ]
+    )
 
 
 def half_rows(half):
@@ -222,26 +230,8 @@
             win[i, t, half_rows(1 - core), :] = rec_ref[t, :, i * HD : (i + 1) * HD]
 
 
-def pack_kernel(
-    place,
-    q_ref,
-    k_ref,
-    v_ref,
-    d_ref,
-    rec_ref,
-    table,
-    meta,
-    left_first,
-    left_second,
-    right_first,
-    right_second,
-    turn_first,
-    turn_rest,
-    win,
-    left_ref,
-    right_ref,
-    sems,
-):
+def pack_kernel(place, q_ref, k_ref, v_ref, d_ref, rec_ref, table, meta, *refs):
+    *pieces, win, left_ref, right_ref, sems = refs
     per = rec_ref.shape[2] // HD
     core = place[CORE]
     step = pl.program_id(0)
@@ -270,7 +260,7 @@
             meta,
             rows_of(left_ref, 0, CAP),
             rows_of(right_ref, PAIR, CAP),
-            (left_first, left_second, right_first, right_second, turn_first, turn_rest),
+            pieces,
             sems,
         )
 
@@ -282,7 +272,7 @@
 
 
 def pieces_shape(tensors):
-    return [jax.ShapeDtypeStruct((tensors, n, HD), BF) for n in (HALF, HALF, HALF, HALF, FIRST, REST)]
+    return [jax.ShapeDtypeStruct((tensors, n, HD), BF) for n in (*PARTS, FIRST, REST)]
 
 
 def pack_halos(place, tensors, rec, table, per=4):
@@ -296,12 +286,12 @@
             num_scalar_prefetch=1,
             grid=(HEADS // per,),
             in_specs=own_specs(per) + [whole(table.shape)],
-            out_specs=(IN_SMEM, *([ANYWHERE] * 6)),
+            out_specs=(IN_SMEM, *([ANYWHERE] * SENT)),
             scratch_shapes=[
                 pltpu.VMEM((per, 4, PAIR, HD), BF),
                 pltpu.VMEM((4, PADDED, HD), BF),
                 pltpu.VMEM((4, PADDED, HD), BF),
-                pltpu.SemaphoreType.DMA((6,)),
+                pltpu.SemaphoreType.DMA((SENT,)),
             ],
         ),
         compiler_params=params(16),
@@ -465,36 +455,10 @@
 
 
 def edge_kernel(
-    meta,
-    q_ref,
-    k_ref,
-    v_ref,
-    d_ref,
-    rec_ref,
-    table,
-    mid_ref,
-    gg_mid_ref,
-    from_left_first,
-    from_left_second,
-    from_right_first,
-    from_right_second,
-    from_turn_first,
-    from_turn_rest,
-    out_ref,
-    gg_ref,
-    left_first,
-    left_second,
-    right_first,
-    right_second,
-    turn_first,
-    turn_rest,
-    win,
-    bias,
-    q_live,
-    held,
-    back,
-    sems,
+    meta, q_ref, k_ref, v_ref, d_ref, rec_ref, table, mid_ref, gg_mid_ref, *refs
 ):
+    halos, (out_ref, gg_ref, *pieces) = refs[: SENT + 1], refs[SENT + 1 : -6]
+    win, bias, q_live, held, back, sems = refs[-6:]
     per = rec_ref.shape[2] // HD
     core = meta[CORE]
     step = pl.program_id(0)
@@ -503,14 +467,7 @@
     def _():
         copies = load_both(
             meta,
-            (
-                from_left_first,
-                from_left_second,
-                from_right_first,
-                from_right_second,
-                from_turn_first,
-                from_turn_rest,
-            ),
+            halos,
             rows_of(held.at[0], PAIR, CAP),
             rows_of(held.at[1], 0, CAP),
             sems,
@@ -580,7 +537,7 @@
             meta,
             rows_of(back.at[0], PAIR, CAP),
             rows_of(back.at[1], 0, CAP),
-            (left_first, left_second, right_first, right_second, turn_first, turn_rest),
+            pieces,
             sems,
         )
 
@@ -598,15 +555,15 @@
             grid=(HEADS // per,),
             in_specs=own_specs(per)
             + [whole(table.shape), half_spec(per), whole(gg_mid.shape)]
-            + [ANYWHERE] * 6,
-            out_specs=(half_spec(per), whole(gg_mid.shape), *([ANYWHERE] * 6)),
+            + [ANYWHERE] * (SENT + 1),
+            out_specs=(half_spec(per), whole(gg_mid.shape), *([ANYWHERE] * SENT)),
             scratch_shapes=[
                 pltpu.VMEM((per, 4, PAIR, HD), BF),
                 pltpu.VMEM((2, PAIR, PAIR), F32),
                 pltpu.VMEM((2, 8, PAIR), F32),
                 pltpu.VMEM((2, 4, PADDED, HD), BF),
                 pltpu.VMEM((2, 3, PADDED + PAIR, HD), BF),
-                pltpu.SemaphoreType.DMA((6,)),
+                pltpu.SemaphoreType.DMA((SENT,)),
             ],
         ),
         compiler_params=params(40),
@@ -638,7 +595,7 @@
 
 
 def merge_kernel(meta, in_ref, *refs):
-    pieces, (_, send_ref, held_left, held_right, sems) = refs[:6], refs[6:]
+    pieces, (_, send_ref, held_left, held_right, sems) = refs[: SENT + 1], refs[SENT + 1 :]
     per = in_ref.shape[3] // HD
     step = pl.program_id(0)
 
@@ -658,7 +615,7 @@
     return [
         pltpu.VMEM((3, PADDED, HD), BF),
         pltpu.VMEM((3, PADDED, HD), BF),
-        pltpu.SemaphoreType.DMA((6,)),
+        pltpu.SemaphoreType.DMA((SENT,)),
     ]
 
 
@@ -670,7 +627,7 @@
             num_scalar_prefetch=1,
             grid=(HEADS // per,),
             in_specs=[pl.BlockSpec((1, 3, ROWS, per * HD), lambda j, m: (1, 0, 0, j))]
-            + [ANYWHERE] * 7,
+            + [ANYWHERE] * (SENT + 2),
             out_specs=pl.BlockSpec((3, ROWS, per * HD), lambda j, m: (0, 0, j)),
             scratch_shapes=held_scratch(),
         ),
@@ -679,7 +636,7 @@
 
 
 def weave_kernel(meta, in_ref, rec_ref, *refs):
-    pieces, (gg_parts, *outs, gg_q, gg_k, held_left, held_right, sems) = refs[:6], refs[6:]
+    pieces, (gg_parts, *outs, gg_q, gg_k, held_left, held_right, sems) = refs[: SENT + 1], refs[SENT + 1 :]
     per = in_ref.shape[3] // HD
     core = meta[CORE]
     step = pl.program_id(0)
@@ -712,7 +669,7 @@
                 pl.BlockSpec((1, 3, ROWS, per * HD), lambda j, m: (0, 0, 0, j)),
                 pl.BlockSpec((3, ROWS, per * HD), lambda j, m: (0, 0, j)),
             ]
-            + [ANYWHERE] * 6
+            + [ANYWHERE] * (SENT + 1)
             + [whole(gg_parts.shape)],
             out_specs=(pl.BlockSpec((ROWS, 2 * per * HD), lambda j, m: (0, j)),) * 3
             + (whole((1, HD)),) * 2,
@@ -723,24 +680,27 @@
 
 
 def exchange(pieces, size):
-    lefts, rights, (turn_first, turn_rest) = pieces[0:2], pieces[2:4], pieces[4:6]
+    *straight, first, rest = pieces
     line = 2 * LINE
     wrap = line - 2
-    turns = [(i, i + 2) for i in range(size - 2) if i % line >= wrap]
-    straight = [(i, i + 2) for i in range(size - 2) if i % line < wrap]
-
-    def back(pairs):
-        return [(j, i) for i, j in pairs]
+    steps = [(i, i + 2) for i in range(size - 2)]
+    evens = [pair for pair in steps if pair[0] // 2 % 2 == 0]
+    odds = [pair for pair in steps if pair[0] // 2 % 2 == 1]
+    turns = [pair for pair in odds if pair[0] % line >= wrap]
+    inner = [pair for pair in odds if pair[0] % line < wrap]
+
+    def both(pairs):
+        return pairs + [(j, i) for i, j in pairs]
 
     def move(array, pairs):
         return lax.ppermute(array, "seq", pairs)
 
-    hop = move(turn_rest, [(i, i - wrap) for i, _ in turns] + [(j, j + wrap) for _, j in turns])
-    from_left = [move(piece, straight) for piece in rights]
-    from_right = [move(piece, back(straight)) for piece in lefts]
-    from_turn = move(turn_first, turns + back(turns))
-    from_hop = move(hop, [(i - wrap, j) for i, j in turns] + [(j + wrap, i) for i, j in turns])
-    return (*from_left, *from_right, from_turn, from_hop)
+    along_x = [(i, i - wrap) for i, _ in turns] + [(j, j + wrap) for _, j in turns]
+    along_z = [(i - wrap, j) for i, j in turns] + [(j + wrap, i) for i, j in turns]
+    hop = move(rest, both(inner) + along_x)
+    from_first = move(first, both(odds))
+    from_even = [move(piece, both(evens)) for piece in straight]
+    return (*from_even, from_first, hop, move(hop, along_z))
 
 
 def shards(queries, keys, values, out_grad, gain_q, gain_k, clip_ids, counts):

time: 158 us -> 154 us (0.975)
  waiting for transfers between devices: 17.7 us -> 24 us
  starting transfers between devices: 59.3 us -> 55.6 us
  blocking collectives: 43.1 us -> 39.9 us
  local copies, waits for them, and re-layouts: 2.27 us -> 0.64 us
    ppermute x14 -> x10, waiting for transfers between devices: 11.9 us -> 18.3 us  [move(): return lax.ppermute(array, 'seq', pairs)]
    ppermute x14 -> x10, starting transfers between devices: 41.1 us -> 37.1 us  [move(): return lax.ppermute(array, 'seq', pairs)]
    all_to_all x2, blocking collectives: 43.1 us -> 39.9 us  [all_to_all(): lax.all_to_all(array, axis, 0, 0, axis_index_groups=among, tiled=True)]
    unnamed x2 -> x0, local copies, waits for them, and re-layouts: 1.63 us -> none
  transfers between devices with their start and end apart: 18 -> 14, of which waited for: 6 -> 5; matrix products, arithmetic and copies ran while one was open for 0% -> 0% of each run, Pallas kernels for 6% -> 6%
where the time goes in v4:
time: 154 us; the launch traced here: 155 us
  starting transfers between devices  55.6 us (36%)
  blocking collectives  39.9 us (26%)
  Pallas kernels  32 us (21%)
  waiting for transfers between devices  24 us (16%)
  between operations  1.6 us (1%)
    all_to_all x2, blocking collectives, all_to_all(): lax.all_to_all(array, axis, 0, 0, axis_index_groups=among, tiled=True)  39.9 us
    ppermute x10, starting transfers between devices, move(): return lax.ppermute(array, 'seq', pairs)  37.1 us
    ppermute x10, waiting for transfers between devices, move(): return lax.ppermute(array, 'seq', pairs)  18.3 us
    pallas_call x1, Pallas kernels, solve_mid(): pl.pallas_call(mid_kernel, out_shape=(jax.ShapeDtypeStruct((2, 3, ROWS, H...  9.21 us
    ppermute x1, starting transfers between devices, shards(): other = lax.ppermute(send, 'seq', swap)  9.03 us
    pallas_call x1, Pallas kernels, solve_edges(): pl.pallas_call(edge_kernel, out_shape=(jax.ShapeDtypeStruct(mid.shape, BF...  8.33 us
    all_to_all x1, starting transfers between devices, all_to_all(): lax.all_to_all(array, axis, 0, 0, axis_index_groups=among, tiled=True)  6.37 us
    pallas_call x1, Pallas kernels, pack_halos(): pl.pallas_call(pack_kernel, out_shape=(jax.ShapeDtypeStruct((16,), jnp.in...  5.39 us
  transfers between devices with their start and end apart: 14, of which 5 were waited for; matrix products, arithmetic and copies ran while one was open for 0% of the time, Pallas kernels for 6%

profile of v4, /device:TPU:1, one launch (start us, length us, event | category | flops | bytes accessed | tf_op | source)
XLA Modules:
  0.0 155.2 jit_solution(16445408129029338403)
XLA Ops:
  0.6 0.7 pad_maximum_fusion
  1.3 0.6 broadcast_in_dim.6
  1.9 6.4 %all-to-all-start = ((f32[8,2,16]{2,1,0:T(2,128)}), f32[8,2,16]{2,1,0:T(2,128)S(1)}, u32[]{:S(2)}, u32[]{:S(2)}) async-start(f32[8,2,16]{2,1,0:T(2,128)} %broadcast_in_dim.6), calls=%async_computation | async-start | bytes 16384 | tf_op jit(solution)/shard_map/all_to_all | solution.py:724
  8.9 0.7 pad_convert_fusion.info
  9.6 1.0 collective-permute-start
  10.6 0.1 pad_add_fusion.place
  10.6 0.7 collective-permute-done.info_other
  11.4 1.9 %all-to-all-done.gain_cols = f32[8,2,16]{2,1,0:T(2,128)S(1)} async-done(((f32[8,2,16]{2,1,0:T(2,128)}), f32[8,2,16]{2,1,0:T(2,128)S(1)}, u32[]{:S(2)}, u32[]{:S(2)}) %all-to-all-start) | async-done | bytes 1056 | tf_op jit(solution)/shard_map/all_to_all | solution.py:724
  13.3 3.8 %shard_map.119 = (bf16[4,128,2048]{2,1,0:T(8,128)(2,1)S(1)}, f32[16,5,128]{2,1,0:T(8,128)S(1)}) custom-call(s32[2]{0:T(128)S(1)} %pad_add_fusion.place, bf16[128,4096]{1,0:T(8,128)(2,1)} %q_ref.7, bf16[128,4096]{1,0:T(8,128)(2,1)} %k_ref.7, bf16[128,4096]{1,0:T(8,128)(2,1)} %v_ref.7, bf16[128,4096]{1,0:T(8,128)(2,1)} %d_ref.7, ...), custom_call_target="tpu_custom_call" | custom-call | tf_op jit(solution)/shard_map/pallas_call | solution.py:87
  17.1 2.2 %collective-permute-start.1 = (bf16[4,128,2048]{2,1,0:T(8,128)(2,1)S(1)}, bf16[4,128,2048]{2,1,0:T(8,128)(2,1)S(1)}, u32[]{:S(2)}, u32[]{:S(2)}) collective-permute-start(bf16[4,128,2048]{2,1,0:T(8,128)(2,1)S(1)} %get-tuple-element.20), channel_id=1, source_target_pairs={{0,1},{1,0},{2,3},{3,2},{4,5},{5,4},{6,7},{7,6},{8,9},{9,8},{10,11... | collective-permute-start | bytes 6291464 | tf_op jit(solution)/shard_map/ppermute | solution.py:731
  19.3 18.6 %all_to_all.15.table = f32[16,5,128]{2,1,0:T(8,128)S(1)} all-to-all(f32[16,5,128]{2,1,0:T(8,128)S(1)} %get-tuple-element.21), channel_id=1, replica_groups={{0,2,4,6,8,10,12,14,16,18,20,22,24,26,28,30},{1,3,5,7,9,11,13,15,17,19,..., dimensions={0} | all-to-all | bytes 81920 | tf_op jit(solution)/shard_map/all_to_all | solution.py:724
  37.9 5.4 %shard_map.120 = (s32[16]{0:T(128)S(1)}, bf16[4,576,128]{2,1,0:T(8,128)(2,1)S(1)}, bf16[4,576,128]{2,1,0:T(8,128)(2,1)S(1)}, bf16[4,768,128]{2,1,0:T(8,128)(2,1)S(1)}, bf16[4,384,128]{2,1,0:T(8,128)(2,1)S(1)}) custom-call(s32[2]{0:T(128)S(1)} %pad_add_fusion.place, bf16[128,4096]{1,0:T(8,128)(2,1)} %q_ref.7, bf16[128,4096]{1,0:T(8,128)(2,1)} %k_ref.7, ...), custom_call_target="tpu_custom_call" | custom-call | tf_op jit(solution)/shard_map/pallas_call | solution.py:279
  43.3 1.3 collective-permute-start.5
  44.6 0.7 collective-permute-start.4
  45.3 3.6 %collective-permute-start.2 = (bf16[4,576,128]{2,1,0:T(8,128)(2,1)S(1)}, bf16[4,576,128]{2,1,0:T(8,128)(2,1)S(1)}, u32[]{:S(2)}, u32[]{:S(2)}) collective-permute-start(bf16[4,576,128]{2,1,0:T(8,128)(2,1)S(1)} %get-tuple-element.25), channel_id=1, source_target_pairs={{0,2},{1,3},{4,6},{5,7},{8,10},{9,11},{12,14},{13,15},{16,18},{17,... | collective-permute-start | bytes 1769480 | tf_op jit(solution)/shard_map/ppermute | solution.py:696
  48.9 0.1 collective-permute-start.3
  49.0 6.6 %collective-permute-done.5.refs_3_ = bf16[4,384,128]{2,1,0:T(8,128)(2,1)S(1)} collective-permute-done((bf16[4,384,128]{2,1,0:T(8,128)(2,1)S(1)}, bf16[4,384,128]{2,1,0:T(8,128)(2,1)S(1)}, u32[]{:S(2)}, u32[]{:S(2)}) %collective-permute-start.5) | collective-permute-done | bytes 393248 | tf_op jit(solution)/shard_map/ppermute | solution.py:696
  55.6 19.9 %collective-permute-start.6 = (bf16[4,384,128]{2,1,0:T(8,128)(2,1)S(1)}, bf16[4,384,128]{2,1,0:T(8,128)(2,1)S(1)}, u32[]{:S(2)}, u32[]{:S(2)}) collective-permute-start(bf16[4,384,128]{2,1,0:T(8,128)(2,1)S(1)} %collective-permute-done.5.refs_3_), channel_id=1, source_target_pairs={{0,8},{1,9},{8,16},{9,17},{16,24},{17,25},{14,6},{15,7},{22,14},{2... | collective-permute-start | bytes 1179656 | tf_op jit(solution)/shard_map/ppermute | solution.py:696
  75.4 9.2 %shard_map.121 = (bf16[2,3,128,2048]{3,2,1,0:T(8,128)(2,1)S(1)}, f32[16,2,128]{2,1,0:T(2,128)S(1)}) custom-call(s32[16]{0:T(128)S(1)} %get-tuple-element.22.meta, bf16[128,4096]{1,0:T(8,128)(2,1)} %q_ref.7, bf16[128,4096]{1,0:T(8,128)(2,1)} %k_ref.7, bf16[128,4096]{1,0:T(8,128)(2,1)} %v_ref.7, bf16[128,4096]{1,0:T(8,128)(2,1)} %d_ref.7, ...), custom_call_target="tpu_custom_call" | custom-call | tf_op jit(solution)/shard_map/pallas_call | solution.py:427
  84.6 0.0 collective-permute-done.3.refs_1_
  84.7 8.3 %shard_map.122 = (bf16[2,3,128,2048]{3,2,1,0:T(8,128)(2,1)S(1)}, f32[16,2,128]{2,1,0:T(2,128)S(1)}, bf16[3,576,128]{2,1,0:T(8,128)(2,1)S(1)}, bf16[3,576,128]{2,...) custom-call(s32[16]{0:T(128)S(1)} %get-tuple-element.22.meta, ...), custom_call_target="tpu_custom_call" | custom-call | tf_op jit(solution)/shard_map/pallas_call | solution.py:546
  93.0 1.3 collective-permute-start.10
  94.3 0.7 collective-permute-start.9
  95.0 0.1 collective-permute-start.7
  95.1 1.5 collective-permute-start.8
  96.6 11.7 %collective-permute-done.10.refs_3_ = bf16[3,384,128]{2,1,0:T(8,128)(2,1)S(1)} collective-permute-done((bf16[3,384,128]{2,1,0:T(8,128)(2,1)S(1)}, bf16[3,384,128]{2,1,0:T(8,128)(2,1)S(1)}, u32[]{:S(2)}, u32[]{:S(2)}) %collective-permute-start.10) | collective-permute-done | bytes 294944 | tf_op jit(solution)/shard_map/ppermute | solution.py:696
  108.3 8.0 %collective-permute-start.11 = (bf16[3,384,128]{2,1,0:T(8,128)(2,1)S(1)}, bf16[3,384,128]{2,1,0:T(8,128)(2,1)S(1)}, u32[]{:S(2)}, u32[]{:S(2)}) collective-permute-start(bf16[3,384,128]{2,1,0:T(8,128)(2,1)S(1)} %collective-permute-done.10.refs_3_), channel_id=1, source_target_pairs={{0,8},{1,9},{8,16},{9,17},{16,24},{17,25},{14,6},{15,7},{22,14},{2... | collective-permute-start | bytes 884744 | tf_op jit(solution)/shard_map/ppermute | solution.py:696
  116.3 21.3 %all_to_all.16.refs_5_ = f32[128,2,128]{2,1,0:T(2,128)S(1)} all-to-all(f32[128,2,128]{2,1,0:T(2,128)S(1)} %bitcast.5), channel_id=1, replica_groups={{0,2,4,6,8,10,12,14,16,18,20,22,24,26,28,30,32,34,36,38,40,42,44,46,48,..., dimensions={0} | all-to-all | bytes 262144 | tf_op jit(solution)/shard_map/all_to_all | solution.py:724
  137.7 1.5 shard_map.123
  139.2 9.0 %collective-permute-start.12 = (bf16[3,128,2048]{2,1,0:T(8,128)(2,1)S(1)}, bf16[3,128,2048]{2,1,0:T(8,128)(2,1)S(1)}, u32[]{:S(2)}, u32[]{:S(2)}) collective-permute-start(bf16[3,128,2048]{2,1,0:T(8,128)(2,1)S(1)} %shard_map.123), channel_id=1, source_target_pairs={{0,1},{1,0},{2,3},{3,2},{4,5},{5,4},{6,7},{7,6},{8,9},{9,8},{10,11... | collective-permute-start | bytes 4718600 | tf_op jit(solution)/shard_map/ppermute | solution.py:745
  148.3 3.0 %collective-permute-done.12.rec_ref = bf16[3,128,2048]{2,1,0:T(8,128)(2,1)S(1)} collective-permute-done((bf16[3,128,2048]{2,1,0:T(8,128)(2,1)S(1)}, bf16[3,128,2048]{2,1,0:T(8,128)(2,1)S(1)}, u32[]{:S(2)}, u32[]{:S(2)}) %collective-permute-start.12) | collective-permute-done | bytes 1572896 | tf_op jit(solution)/shard_map/ppermute | solution.py:745
  151.3 3.8 %shard_map.124 = (bf16[128,4096]{1,0:T(8,128)(2,1)}, bf16[128,4096]{1,0:T(8,128)(2,1)}, bf16[128,4096]{1,0:T(8,128)(2,1)}, f32[1,128]{1,0:T(1,128)}, f32[1,128]{1,0:T(1,128)}) custom-call(s32[16]{0:T(128)S(1)} %get-tuple-element.22.meta, bf16[2,3,128,2048]{3,2,1,0:T(8,128)(2,1)S(1)} %get-tuple-element.29.in_ref, ...), custom_call_target="tpu_custom_call" | custom-call | tf_op jit(solution)/shard_map/pallas_call | solution.py:661
  (9 shorter events, 0.1 us)
Async XLA Ops:
  1.9 11.4 %all-to-all-start = ((f32[8,2,16]{2,1,0:T(2,128)}), f32[8,2,16]{2,1,0:T(2,128)S(1)}, u32[]{:S(2)}, u32[]{:S(2)}) async-start(f32[8,2,16]{2,1,0:T(2,128)} %broadcast_in_dim.6), calls=%async_computation | async-start | bytes 16384 | tf_op jit(solution)/shard_map/all_to_all | solution.py:724
  9.6 1.8 %collective-permute-start = (f32[2,128]{1,0:T(2,128)S(1)}, f32[2,128]{1,0:T(2,128)S(1)}, u32[]{:S(2)}, u32[]{:S(2)}) collective-permute-start(f32[2,128]{1,0:T(2,128)S(1)} %pad_convert_fusion.info), channel_id=1, source_target_pairs={{0,1},{1,0},{2,3},{3,2},{4,5},{5,4},{6,7},{7,6},{8,9},{9,8},{10,11... | collective-permute-start | bytes 3080 | tf_op jit(solution)/shard_map/ppermute | solution.py:727
  17.1 20.8 %collective-permute-start.1 = (bf16[4,128,2048]{2,1,0:T(8,128)(2,1)S(1)}, bf16[4,128,2048]{2,1,0:T(8,128)(2,1)S(1)}, u32[]{:S(2)}, u32[]{:S(2)}) collective-permute-start(bf16[4,128,2048]{2,1,0:T(8,128)(2,1)S(1)} %get-tuple-element.20), channel_id=1, source_target_pairs={{0,1},{1,0},{2,3},{3,2},{4,5},{5,4},{6,7},{7,6},{8,9},{9,8},{10,11... | collective-permute-start | bytes 6291464 | tf_op jit(solution)/shard_map/ppermute | solution.py:731
  43.3 12.2 %collective-permute-start.5 = (bf16[4,384,128]{2,1,0:T(8,128)(2,1)S(1)}, bf16[4,384,128]{2,1,0:T(8,128)(2,1)S(1)}, u32[]{:S(2)}, u32[]{:S(2)}) collective-permute-start(bf16[4,384,128]{2,1,0:T(8,128)(2,1)S(1)} %get-tuple-element.28), channel_id=1, source_target_pairs={{2,4},{3,5},{10,12},{11,13},{18,20},{19,21},{26,28},{27,29},{4,2},... | collective-permute-start | bytes 1179656 | tf_op jit(solution)/shard_map/ppermute | solution.py:696
  44.6 40.1 %collective-permute-start.4 = (bf16[4,768,128]{2,1,0:T(8,128)(2,1)S(1)}, bf16[4,768,128]{2,1,0:T(8,128)(2,1)S(1)}, u32[]{:S(2)}, u32[]{:S(2)}) collective-permute-start(bf16[4,768,128]{2,1,0:T(8,128)(2,1)S(1)} %get-tuple-element.27), channel_id=1, source_target_pairs={{2,4},{3,5},{6,8},{7,9},{10,12},{11,13},{14,16},{15,17},{18,20},{1... | collective-permute-start | bytes 2359304 | tf_op jit(solution)/shard_map/ppermute | solution.py:696
  45.3 39.3 %collective-permute-start.2 = (bf16[4,576,128]{2,1,0:T(8,128)(2,1)S(1)}, bf16[4,576,128]{2,1,0:T(8,128)(2,1)S(1)}, u32[]{:S(2)}, u32[]{:S(2)}) collective-permute-start(bf16[4,576,128]{2,1,0:T(8,128)(2,1)S(1)} %get-tuple-element.25), channel_id=1, source_target_pairs={{0,2},{1,3},{4,6},{5,7},{8,10},{9,11},{12,14},{13,15},{16,18},{17,... | collective-permute-start | bytes 1769480 | tf_op jit(solution)/shard_map/ppermute | solution.py:696
  48.9 35.8 %collective-permute-start.3 = (bf16[4,576,128]{2,1,0:T(8,128)(2,1)S(1)}, bf16[4,576,128]{2,1,0:T(8,128)(2,1)S(1)}, u32[]{:S(2)}, u32[]{:S(2)}) collective-permute-start(bf16[4,576,128]{2,1,0:T(8,128)(2,1)S(1)} %get-tuple-element.26), channel_id=1, source_target_pairs={{0,2},{1,3},{4,6},{5,7},{8,10},{9,11},{12,14},{13,15},{16,18},{17,... | collective-permute-start | bytes 1769480 | tf_op jit(solution)/shard_map/ppermute | solution.py:696
  55.6 29.1 %collective-permute-start.6 = (bf16[4,384,128]{2,1,0:T(8,128)(2,1)S(1)}, bf16[4,384,128]{2,1,0:T(8,128)(2,1)S(1)}, u32[]{:S(2)}, u32[]{:S(2)}) collective-permute-start(bf16[4,384,128]{2,1,0:T(8,128)(2,1)S(1)} %collective-permute-done.5.refs_3_), channel_id=1, source_target_pairs={{0,8},{1,9},{8,16},{9,17},{16,24},{17,25},{14,6},{15,7},{22,14},{2... | collective-permute-start | bytes 1179656 | tf_op jit(solution)/shard_map/ppermute | solution.py:696
  93.0 15.3 %collective-permute-start.10 = (bf16[3,384,128]{2,1,0:T(8,128)(2,1)S(1)}, bf16[3,384,128]{2,1,0:T(8,128)(2,1)S(1)}, u32[]{:S(2)}, u32[]{:S(2)}) collective-permute-start(bf16[3,384,128]{2,1,0:T(8,128)(2,1)S(1)} %get-tuple-element.33), channel_id=1, source_target_pairs={{2,4},{3,5},{10,12},{11,13},{18,20},{19,21},{26,28},{27,29},{4,2},... | collective-permute-start | bytes 884744 | tf_op jit(solution)/shard_map/ppermute | solution.py:696
  94.3 43.4 %collective-permute-start.9 = (bf16[3,768,128]{2,1,0:T(8,128)(2,1)S(1)}, bf16[3,768,128]{2,1,0:T(8,128)(2,1)S(1)}, u32[]{:S(2)}, u32[]{:S(2)}) collective-permute-start(bf16[3,768,128]{2,1,0:T(8,128)(2,1)S(1)} %get-tuple-element.32), channel_id=1, source_target_pairs={{2,4},{3,5},{6,8},{7,9},{10,12},{11,13},{14,16},{15,17},{18,20},{1... | collective-permute-start | bytes 1769480 | tf_op jit(solution)/shard_map/ppermute | solution.py:696
  95.0 42.6 %collective-permute-start.7 = (bf16[3,576,128]{2,1,0:T(8,128)(2,1)S(1)}, bf16[3,576,128]{2,1,0:T(8,128)(2,1)S(1)}, u32[]{:S(2)}, u32[]{:S(2)}) collective-permute-start(bf16[3,576,128]{2,1,0:T(8,128)(2,1)S(1)} %get-tuple-element.30), channel_id=1, source_target_pairs={{0,2},{1,3},{4,6},{5,7},{8,10},{9,11},{12,14},{13,15},{16,18},{17,... | collective-permute-start | bytes 1327112 | tf_op jit(solution)/shard_map/ppermute | solution.py:696
  95.1 42.6 %collective-permute-start.8 = (bf16[3,576,128]{2,1,0:T(8,128)(2,1)S(1)}, bf16[3,576,128]{2,1,0:T(8,128)(2,1)S(1)}, u32[]{:S(2)}, u32[]{:S(2)}) collective-permute-start(bf16[3,576,128]{2,1,0:T(8,128)(2,1)S(1)} %get-tuple-element.31), channel_id=1, source_target_pairs={{0,2},{1,3},{4,6},{5,7},{8,10},{9,11},{12,14},{13,15},{16,18},{17,... | collective-permute-start | bytes 1327112 | tf_op jit(solution)/shard_map/ppermute | solution.py:696
  108.3 29.4 %collective-permute-start.11 = (bf16[3,384,128]{2,1,0:T(8,128)(2,1)S(1)}, bf16[3,384,128]{2,1,0:T(8,128)(2,1)S(1)}, u32[]{:S(2)}, u32[]{:S(2)}) collective-permute-start(bf16[3,384,128]{2,1,0:T(8,128)(2,1)S(1)} %collective-permute-done.10.refs_3_), channel_id=1, source_target_pairs={{0,8},{1,9},{8,16},{9,17},{16,24},{17,25},{14,6},{15,7},{22,14},{2... | collective-permute-start | bytes 884744 | tf_op jit(solution)/shard_map/ppermute | solution.py:696
  139.2 12.1 %collective-permute-start.12 = (bf16[3,128,2048]{2,1,0:T(8,128)(2,1)S(1)}, bf16[3,128,2048]{2,1,0:T(8,128)(2,1)S(1)}, u32[]{:S(2)}, u32[]{:S(2)}) collective-permute-start(bf16[3,128,2048]{2,1,0:T(8,128)(2,1)S(1)} %shard_map.123), channel_id=1, source_target_pairs={{0,1},{1,0},{2,3},{3,2},{4,5},{5,4},{6,7},{7,6},{8,9},{9,8},{10,11... | collective-permute-start | bytes 4718600 | tf_op jit(solution)/shard_map/ppermute | solution.py:745
